TPU v7x, 32 devices: a whole 2x2x4 slice. The times are simulated.
32 devices in a mesh: dp: 8 (over z, x), group: 4 (over y, core).
Axes of the slice: x: 2, y: 2, z: 4, core: 2. Of those that a mesh axis runs over, the one named last changes fastest.
Arguments:
- tokens: bfloat16 [1024, 96, 128], P(('dp', 'group')), may hold values from -6 to 6
- lengths: int32 [1024], P(('dp', 'group')), may hold values from 3 to 90, as said below
- norm_gains: float32 [2, 2, 128], replicated, may hold values from 0.5 to 1.5
- norm_shifts: float32 [2, 2, 128], replicated, may hold values from -1.8 to 1.8
- w_qkv: bfloat16 [2, 128, 384], replicated, may hold values from -0.5 to 0.5
- qv_bias: float32 [2, 2, 128], replicated, may hold values from -1.8 to 1.8
- w_out: bfloat16 [2, 128, 128], replicated, may hold values from -1 to 1
- out_biases: float32 [2, 2, 128], replicated, may hold values from -1.8 to 1.8
- w_up: bfloat16 [2, 128, 512], replicated, may hold values from -0.5 to 0.5
- up_bias: float32 [2, 512], replicated, may hold values from -1.8 to 1.8
- w_down: bfloat16 [2, 512, 128], replicated, may hold values from -0.25 to 0.25
- cotangent: bfloat16 [1024, 96, 128], P(('dp', 'group')), may hold values from -6 to 6
Outputs:
- output: bfloat16 [1024, 96, 128], P(('dp', 'group'))
- grad_tokens: bfloat16 [1024, 96, 128], P(('dp', 'group'))
- grad_gains: float32 [2, 2, 128], replicated
- grad_shifts: float32 [2, 2, 128], replicated
- grad_qkv: float32 [2, 128, 384], replicated
- grad_qv_bias: float32 [2, 2, 128], replicated
- grad_out: float32 [2, 128, 128], replicated
- grad_out_biases: float32 [2, 2, 128], replicated
- grad_up: float32 [2, 128, 512], replicated
- grad_up_bias: float32 [2, 512], replicated
- grad_down: float32 [2, 512, 128], replicated
Inputs may be any that keep to these rules, and one draw needn't show every extreme that they name: `lengths`: every length is 3 s for a whole number s of timesteps. With e_b = (b * 30) // 8, a trajectory is in band b when e_b < s <= e_(b+1). Among the trajectories of one group (the 4 devices of one dp index) every band holds exactly 16. On one device, bands b and 7 - b together hold at most 12 trajectories, and that many on some device of every group. Some trajectory of every group has 30 timesteps.
All inputs are finite; a program needn't handle non-finite values.
Results may differ from a plain program's by a relative error of at most 0.014.
Values may be sent and summed in bfloat16 or wider, within the bound.
No kernel may reach another device: no remote copies, remote signals or barrier semaphores. Data moves between devices by JAX's collectives and lax.ppermute only.
A program may use at most 128 MiB of HBM per device.

v0:
```python
import jax
import jax.numpy as jnp
from jax import lax
from jax.sharding import PartitionSpec as P

HEAD = 16
LAYERS = 2
STEPS = 30
PAIR = 128


eps = 1e-05
rtg_factor = 0.5
dead_score = -1e30
slots_per_block = 4


def normalize(stream):
    centered = stream - jnp.mean(stream, -1, keepdims=True)
    return centered * lax.rsqrt(jnp.mean(centered * centered, -1, keepdims=True) + eps)


def affine_norm(stream, gain, shift):
    return normalize(stream) * gain + shift


def allowed_of(segment):
    row_iota = jnp.arange(segment.shape[-1])
    causal = row_iota[:, None] >= row_iota[None, :]
    return ((segment[:, :, None] == segment[:, None, :]) & causal[None])[:, None]


def attend(query, keys, values, segment):
    scores = jnp.einsum(
        "bqhd,bkhd->bhqk", query, keys, preferred_element_type=jnp.float32
    ) * HEAD ** (-0.5)
    scores = jnp.where(allowed_of(segment), scores, dead_score)
    top_score = jnp.max(scores, -1, keepdims=True)
    expo = jnp.exp(scores - top_score)
    total = jnp.sum(expo, -1, keepdims=True)
    probs = expo / total
    attended = jnp.einsum(
        "bhqk,bkhd->bqhd", probs.astype(jnp.bfloat16), values, preferred_element_type=jnp.float32
    )
    return (attended, (top_score + jnp.log(total))[..., 0])


def attend_back(query, keys, values, segment, log_total, d_mixed):
    scores = jnp.einsum(
        "bqhd,bkhd->bhqk", query, keys, preferred_element_type=jnp.float32
    ) * HEAD ** (-0.5)
    scores = jnp.where(allowed_of(segment), scores, dead_score)
    probs = jnp.exp(scores - log_total[..., None])
    d_probs = jnp.einsum("bqhd,bkhd->bhqk", d_mixed, values, preferred_element_type=jnp.float32)
    d_values = jnp.einsum(
        "bhqk,bqhd->bkhd", probs.astype(jnp.bfloat16), d_mixed, preferred_element_type=jnp.float32
    )
    inner = jnp.sum(d_probs * probs, -1, keepdims=True)
    d_scores = (probs * (d_probs - inner)).astype(jnp.bfloat16)
    d_query = jnp.einsum(
        "bhqk,bkhd->bqhd", d_scores, keys, preferred_element_type=jnp.float32
    ) * HEAD ** (-0.5)
    d_keys = jnp.einsum(
        "bhqk,bqhd->bkhd", d_scores, query, preferred_element_type=jnp.float32
    ) * HEAD ** (-0.5)
    return (d_query, d_keys, d_values)


def split_blocks(matrix, width, shape):
    return matrix.reshape(-1, shape[0], shape[1], width // HEAD, HEAD)


def layer_forward(stream, layer, weights, segment, shape):
    norm_gains, norm_shifts, w_qkv, qv_bias, w_out, out_biases, w_up, up_bias, w_down = weights
    width = stream.shape[1]
    normed = affine_norm(stream, norm_gains[layer, 0], norm_shifts[layer, 0]).astype(jnp.bfloat16)
    joint = jnp.dot(normed, w_qkv[layer], preferred_element_type=jnp.float32)
    query = (joint[:, :width] + qv_bias[layer, 0]).astype(jnp.bfloat16)
    keys = joint[:, width : 2 * width].astype(jnp.bfloat16)
    values = (joint[:, 2 * width :] + qv_bias[layer, 1]).astype(jnp.bfloat16)
    seg_blocks = segment.reshape(-1, shape[0], shape[1])
    attended, log_total = lax.map(
        lambda block: attend(*block),
        (
            split_blocks(query, width, shape),
            split_blocks(keys, width, shape),
            split_blocks(values, width, shape),
            seg_blocks,
        ),
    )
    mixed = attended.reshape(-1, width).astype(jnp.bfloat16)
    middle = (
        stream
        + jnp.dot(mixed, w_out[layer], preferred_element_type=jnp.float32)
        + out_biases[layer, 0]
    )
    normed_two = affine_norm(middle, norm_gains[layer, 1], norm_shifts[layer, 1]).astype(
        jnp.bfloat16
    )
    hidden = jnp.dot(normed_two, w_up[layer], preferred_element_type=jnp.float32) + up_bias[layer]
    active = jax.nn.gelu(hidden).astype(jnp.bfloat16)
    result = (
        middle
        + jnp.dot(active, w_down[layer], preferred_element_type=jnp.float32)
        + out_biases[layer, 1]
    )
    return (
        result,
        (stream, normed, query, keys, values, log_total, mixed, middle, normed_two, hidden, active),
    )


def layer_backward(d_result, layer, weights, saved, segment, shape):
    norm_gains, norm_shifts, w_qkv, qv_bias, w_out, out_biases, w_up, up_bias, w_down = weights
    stream, normed, query, keys, values, log_total, mixed, middle, normed_two, hidden, active = (
        saved
    )
    width = stream.shape[1]
    d_down = d_result.astype(jnp.bfloat16)
    g_down = jnp.einsum("rf,rd->fd", active, d_down, preferred_element_type=jnp.float32)
    g_down_bias = jnp.sum(d_down.astype(jnp.float32), 0)
    d_active = jnp.einsum("rd,fd->rf", d_down, w_down[layer], preferred_element_type=jnp.float32)
    unused, gelu_back = jax.vjp(jax.nn.gelu, hidden)
    d_hidden = gelu_back(d_active)[0].astype(jnp.bfloat16)
    g_up = jnp.einsum("rd,rf->df", normed_two, d_hidden, preferred_element_type=jnp.float32)
    g_up_bias = jnp.sum(d_hidden.astype(jnp.float32), 0)
    d_normed_two = jnp.einsum(
        "rf,df->rd", d_hidden, w_up[layer], preferred_element_type=jnp.float32
    )
    unused, norm_two_back = jax.vjp(
        affine_norm, middle, norm_gains[layer, 1], norm_shifts[layer, 1]
    )
    d_mid_part, g_gain_two, g_shift_two = norm_two_back(d_normed_two)
    d_middle = d_result + d_mid_part
    d_branch = d_middle.astype(jnp.bfloat16)
    g_out = jnp.einsum("rd,re->de", mixed, d_branch, preferred_element_type=jnp.float32)
    g_out_bias = jnp.sum(d_branch.astype(jnp.float32), 0)
    d_mixed = jnp.einsum(
        "re,de->rd", d_branch, w_out[layer], preferred_element_type=jnp.float32
    ).astype(jnp.bfloat16)
    seg_blocks = segment.reshape(-1, shape[0], shape[1])
    d_query, d_keys, d_values = lax.map(
        lambda block: attend_back(*block),
        (
            split_blocks(query, width, shape),
            split_blocks(keys, width, shape),
            split_blocks(values, width, shape),
            seg_blocks,
            log_total,
            split_blocks(d_mixed, width, shape),
        ),
    )
    d_joint = jnp.concatenate(
        [d_query.reshape(-1, width), d_keys.reshape(-1, width), d_values.reshape(-1, width)], axis=1
    ).astype(jnp.bfloat16)
    g_qkv = jnp.einsum("rd,re->de", normed, d_joint, preferred_element_type=jnp.float32)
    joint_sums = jnp.sum(d_joint.astype(jnp.float32), 0)
    d_normed = jnp.einsum("re,de->rd", d_joint, w_qkv[layer], preferred_element_type=jnp.float32)
    unused, norm_one_back = jax.vjp(
        affine_norm, stream, norm_gains[layer, 0], norm_shifts[layer, 0]
    )
    d_stream_part, g_gain_one, g_shift_one = norm_one_back(d_normed)
    grads = (
        jnp.stack([g_gain_one, g_gain_two]),
        jnp.stack([g_shift_one, g_shift_two]),
        g_qkv,
        jnp.stack([joint_sums[:width], joint_sums[2 * width :]]),
        g_out,
        jnp.stack([g_out_bias, g_down_bias]),
        g_up,
        g_up_bias,
        g_down,
    )
    return (d_middle + d_stream_part, grads)


def run_layers(stream, cot_rows, weights, segment, shape):
    kept = []
    inputs = []
    for layer in range(LAYERS):
        inputs.append(stream)
        stream, saved = layer_forward(stream, layer, weights, segment, shape)
        kept.append(saved)
    stream_grad = cot_rows
    layer_grads = [None] * LAYERS
    for layer in reversed(range(LAYERS)):
        saved = kept[layer]
        stream_grad, grads = layer_backward(stream_grad, layer, weights, saved, segment, shape)
        layer_grads[layer] = grads
    stacked = tuple(
        (jnp.stack([layer_grads[layer][member] for layer in range(LAYERS)]) for member in range(9))
    )
    stacked = lax.psum(
        (
            stacked[0],
            stacked[1],
            stacked[2],
            stacked[3],
            stacked[4],
            stacked[5],
            stacked[6],
            stacked[7],
            stacked[8],
        ),
        ("dp", "group"),
    )
    return (stream, stream_grad, stacked)


def per_device(
    tokens,
    lengths,
    norm_gains,
    norm_shifts,
    w_qkv,
    qv_bias,
    w_out,
    out_biases,
    w_up,
    up_bias,
    w_down,
    cotangent,
):
    weights = (norm_gains, norm_shifts, w_qkv, qv_bias, w_out, out_biases, w_up, up_bias, w_down)
    traj_count, slot_rows, width = tokens.shape
    bf_zero = jnp.zeros((), jnp.bfloat16)
    group_size = lax.axis_size("group")
    bands = 2 * group_size
    capacity = 3 * traj_count // bands
    slots_total = group_size * capacity
    pairs = traj_count // 2
    edges = jnp.arange(bands + 1) * STEPS // bands

    def bucket_of(count_steps):
        band = jnp.sum(count_steps[:, None] > edges[None, :bands], axis=1) - 1
        return (band, jnp.where(band < group_size, band, bands - 1 - band))

    band, target = bucket_of(lengths // 3)
    traj_iota = jnp.arange(traj_count)
    earlier = traj_iota[:, None] > traj_iota[None, :]
    rank_within = jnp.sum((target[:, None] == target[None, :]) & earlier, axis=1)
    place = target * capacity + rank_within
    slot_iota = jnp.arange(slots_total)
    hit = place[None, :] == slot_iota[:, None]
    occupied = jnp.any(hit, axis=1)
    source_traj = jnp.sum(jnp.where(hit, traj_iota[None, :], 0), axis=1)
    send_lengths = jnp.where(occupied, jnp.take(lengths, source_traj), 0).astype(jnp.bfloat16)
    send_tokens = jnp.where(occupied[:, None, None], jnp.take(tokens, source_traj, axis=0), bf_zero)
    send_cot = jnp.where(occupied[:, None, None], jnp.take(cotangent, source_traj, axis=0), bf_zero)
    recv_tokens, recv_cot, recv_len_wire = (
        lax.all_to_all(send_tokens, "group", split_axis=0, concat_axis=0, tiled=True),
        lax.all_to_all(send_cot, "group", split_axis=0, concat_axis=0, tiled=True),
        lax.all_to_all(send_lengths, "group", split_axis=0, concat_axis=0, tiled=True),
    )
    recv_lengths = recv_len_wire.astype(jnp.int32)
    recv_band = bucket_of(recv_lengths // 3)[0]
    filled = recv_lengths > 0
    is_short = filled & (recv_band < group_size)
    is_long = filled & (recv_band >= group_size)
    before = slot_iota[:, None] > slot_iota[None, :]
    rank_short = jnp.sum(before & is_short[None, :], axis=1)
    rank_long = jnp.sum(before & is_long[None, :], axis=1)
    pair_iota = jnp.arange(pairs)
    short_slot = jnp.sum(
        jnp.where(
            is_short[None, :] & (rank_short[None, :] == pair_iota[:, None]), slot_iota[None, :], 0
        ),
        axis=1,
    )
    long_slot = jnp.sum(
        jnp.where(
            is_long[None, :] & (rank_long[None, :] == pair_iota[:, None]), slot_iota[None, :], 0
        ),
        axis=1,
    )
    short_len = jnp.take(recv_lengths, short_slot)[:, None]
    long_len = jnp.take(recv_lengths, long_slot)[:, None]
    row_iota = jnp.arange(PAIR)[None, :]
    in_short = row_iota < short_len
    in_long = (row_iota >= short_len) & (row_iota < short_len + long_len)
    live = in_short | in_long
    source_row = jnp.where(
        in_short,
        short_slot[:, None] * slot_rows + row_iota,
        jnp.where(in_long, long_slot[:, None] * slot_rows + row_iota - short_len, 0),
    ).reshape(-1)
    segment = jnp.where(in_short, 0, jnp.where(in_long, 1, 2)).reshape(-1)
    position = jnp.where(in_short, row_iota, row_iota - short_len)
    live_flat = live.reshape(-1)
    flat_tokens = recv_tokens.reshape(slots_total * slot_rows, width)
    flat_cot = recv_cot.reshape(slots_total * slot_rows, width)
    packed_tokens = jnp.where(
        live_flat[:, None], jnp.take(flat_tokens, source_row, axis=0), bf_zero
    )
    packed_cot = jnp.where(live_flat[:, None], jnp.take(flat_cot, source_row, axis=0), bf_zero)
    factor = (
        jnp.where(live & (position % 3 == 0), rtg_factor, 1.0).astype(jnp.float32).reshape(-1, 1)
    )
    stream = packed_tokens.astype(jnp.float32) * factor
    shape = (slots_per_block, PAIR)
    stream, stream_grad, stacked = run_layers(
        stream, packed_cot.astype(jnp.float32), weights, segment, shape
    )
    out_rows = jnp.where(live_flat[:, None], stream, 0.0).astype(jnp.bfloat16)
    grad_rows = (stream_grad * factor).astype(jnp.bfloat16)
    pair_of = jnp.minimum(jnp.where(is_short, rank_short, rank_long), pairs - 1)
    offset_of = jnp.where(is_short, 0, jnp.take(short_len[:, 0], pair_of))
    slot_row = jnp.arange(slot_rows)[None, :]
    valid = slot_row < recv_lengths[:, None]
    back_index = jnp.where(
        valid, pair_of[:, None] * PAIR + offset_of[:, None] + slot_row, 0
    ).reshape(-1)
    valid_flat = valid.reshape(-1)[:, None]
    out_slots = jnp.where(valid_flat, jnp.take(out_rows, back_index, axis=0), bf_zero).reshape(
        slots_total, slot_rows, width
    )
    grad_slots = jnp.where(valid_flat, jnp.take(grad_rows, back_index, axis=0), bf_zero).reshape(
        slots_total, slot_rows, width
    )
    home_out, home_grad = (
        lax.all_to_all(out_slots, "group", split_axis=0, concat_axis=0, tiled=True),
        lax.all_to_all(grad_slots, "group", split_axis=0, concat_axis=0, tiled=True),
    )
    output = jnp.take(home_out, place, axis=0)
    grad_tokens = jnp.take(home_grad, place, axis=0)
    return (
        output,
        grad_tokens,
        stacked[0],
        stacked[1],
        stacked[2],
        stacked[3],
        stacked[4],
        stacked[5],
        stacked[6],
        stacked[7],
        stacked[8],
    )


def solution(mesh):
    in_specs = (
        P(("dp", "group"), None, None),
        P(("dp", "group")),
        P(),
        P(),
        P(),
        P(),
        P(),
        P(),
        P(),
        P(),
        P(),
        P(("dp", "group"), None, None),
    )
    out_specs = (
        P(("dp", "group"), None, None),
        P(("dp", "group"), None, None),
        P(),
        P(),
        P(),
        P(),
        P(),
        P(),
        P(),
        P(),
        P(),
    )
    return jax.shard_map(
        per_device, mesh=mesh, in_specs=in_specs, out_specs=out_specs, check_vma=False
    )
```

profile of v0, /device:TPU:0, one launch (start us, length us, event | category | flops | bytes accessed | tf_op | source)
XLA Modules:
  0.0 470.5 jit_solution(1357225669270662656)
XLA Ops:
  11.3 4.2 all-to-all-start
  20.8 1.9 gather_fusion.4
  25.1 3.5 all-to-all-start.1
  32.7 11.7 %all-to-all-done.1 = bf16[48,96,128]{2,1,0:T(8,128)(2,1)S(1)} async-done(((bf16[48,96,128]{2,1,0:T(8,128)(2,1)}), bf16[48,96,128]{2,1,0:T(8,128)(2,1)S(1)}, u32[]{:S(2)}, u32[]{:S(2)}) %all-to-all-start.1) | async-done | bytes 1179680 | tf_op jit(solution)/shard_map/all_to_all | solution.py:251
  44.5 3.5 all-to-all-start.3
  48.9 6.2 %gather_fusion.5 = bf16[2048,128]{1,0:T(8,128)(2,1)S(1)} fusion(bf16[4608,128]{1,0:T(8,128)(2,1)S(1)} %bitcast.570, s32[2048]{0:T(1024)S(1)} %fusion.167), kind=kCustom, calls=%fused_computation.2.clone | custom fusion | bytes 1056768 | tf_op jit(solution)/shard_map/jit(_take)/gather | solution.py:293
  55.6 8.2 %all-to-all-done.3 = bf16[48,96,128]{2,1,0:T(8,128)(2,1)S(1)} async-done(((bf16[48,96,128]{2,1,0:T(8,128)(2,1)}), bf16[48,96,128]{2,1,0:T(8,128)(2,1)S(1)}, u32[]{:S(2)}, u32[]{:S(2)}) %all-to-all-start.3) | async-done | bytes 1179680 | tf_op jit(solution)/shard_map/all_to_all | solution.py:252
  63.8 6.2 %gather_fusion.9 = bf16[2048,128]{1,0:T(8,128)(2,1)S(1)} fusion(bf16[4608,128]{1,0:T(8,128)(2,1)S(1)} %bitcast.571, s32[2048]{0:T(1024)S(1)} %fusion.167), kind=kCustom, calls=%fused_computation.7.clone | custom fusion | bytes 1056768 | tf_op jit(solution)/shard_map/jit(_take)/gather | solution.py:295
  74.6 8.0 %while.52 = (s32[]{:T(128)}, bf16[4,4,128,8,16]{2,4,3,1,0:T(8,128)(2,1)S(1)}, f32[4,4,8,128]{3,2,1,0:T(8,128)S(1)}, bf16[4,4,128,8,16]{2,4,3,1,0:T(8,128)(2,1)S(...) while((s32[]{:T(128)}, ...), condition=%wide.region_14.18_spmd, body=%wide.region_11.17_spmd.sunk | while | flops 39989248 | bytes 7381093 | solution.py:82
  86.0 3.6 multiply_convert_fusion.3
  96.4 2.0 copy.185
  98.4 2.2 reshape.789
  100.6 2.0 copy.188
  102.5 2.0 copy.183
  104.6 2.2 reshape.787
  106.8 2.0 copy.186
  109.7 18.2 %while.53 = (s32[]{:T(128)}, bf16[4,4,128,8,16]{2,4,3,1,0:T(8,128)(2,1)}, f32[4,4,8,128]{3,2,1,0:T(8,128)S(1)}, bf16[4,4,128,8,16]{2,4,3,1,0:T(8,128)(2,1)}, s32...) while((s32[]{:T(128)}, ...), condition=%wide.region_22.26_spmd, body=%wide.region_19.25_spmd.sunk | while | flops 39989248 | bytes 11575453 | solution.py:82
  127.9 2.4 copy.189
  130.3 2.2 convert_element_type.202
  134.8 3.1 multiply_convert_fusion.2
  137.9 4.2 convert_reduce_fusion
  143.3 2.2 fusion.188
  145.5 2.5 copy.194
  148.1 2.1 multiply_reduce_fusion.2
  154.5 2.0 copy.195
  156.6 2.2 reshape.792
  161.4 39.6 %while.54 = (s32[]{:T(128)}, bf16[4,4,128,8,16]{2,4,3,1,0:T(8,128)(2,1)}, bf16[4,4,128,8,16]{2,4,3,1,0:T(8,128)(2,1)}, bf16[4,4,128,8,16]{2,4,3,1,0:T(8,128)(2,1...) while((s32[]{:T(128)}, ...), condition=%wide.region_29.35_spmd, body=%wide.region_27.34_spmd.sunk | while | flops 88879104 | bytes 30532912 | solution.py:142
  201.1 2.2 copy.202
  203.3 2.2 reshape.795
  205.5 2.2 copy.200
  207.8 2.2 reshape.793
  210.0 2.2 copy.201
  212.2 2.2 reshape.794
  219.0 2.2 fusion.189
  221.2 2.5 copy.203
  230.1 4.0 convert_reduce_fusion.1
  235.3 2.2 fusion.190
  245.6 25.5 %while.55 = (s32[]{:T(128)}, bf16[4,4,128,8,16]{2,4,3,1,0:T(8,128)(2,1)}, bf16[4,4,128,8,16]{2,4,3,1,0:T(8,128)(2,1)}, bf16[4,4,128,8,16]{2,4,3,1,0:T(8,128)(2,1...) while((s32[]{:T(128)}, ...), condition=%wide.region_36.42_spmd, body=%wide.region_34.41_spmd.sunk | while | flops 88879104 | bytes 26338552 | solution.py:142
  288.3 8.8 %gather_fusion.6 = bf16[4608,128]{1,0:T(8,128)(2,1)S(1)} fusion(bf16[2048,128]{1,0:T(8,128)(2,1)S(1)} %copy.192, s32[5120]{0:T(1024)S(1)} %copy-done.63), kind=kCustom, calls=%fused_computation.3.clone | custom fusion | bytes 2377728 | tf_op jit(solution)/shard_map/jit(_take)/gather | solution.py:314
  297.1 8.8 %gather_fusion.10 = bf16[4608,128]{1,0:T(8,128)(2,1)S(1)} fusion(bf16[2048,128]{1,0:T(8,128)(2,1)S(1)} %copy.214, s32[5120]{0:T(1024)S(1)} %copy-done.63), kind=kCustom, calls=%fused_computation.8.clone | custom fusion | bytes 2377728 | tf_op jit(solution)/shard_map/jit(_take)/gather | solution.py:317
  305.9 4.3 select_select_fusion
  310.3 3.7 all-to-all-start.2
  319.5 10.3 %all-to-all-done.2 = bf16[48,96,128]{2,1,0:T(8,128)(2,1)S(1)} async-done(((bf16[48,96,128]{2,1,0:T(8,128)(2,1)}), bf16[48,96,128]{2,1,0:T(8,128)(2,1)S(1)}, u32[]{:S(2)}, u32[]{:S(2)}) %all-to-all-start.2) | async-done | bytes 1179680 | tf_op jit(solution)/shard_map/all_to_all | solution.py:321
  329.8 3.5 all-to-all-start.4
  333.5 51.8 %all-reduce = (f32[2,2,128]{2,1,0:T(2,128)}, f32[2,2,128]{2,1,0:T(2,128)}, f32[2,2,128]{2,1,0:T(2,128)}, f32[2,2,128]{2,1,0:T(2,128)}, f32[2,512]{1,0:T(2,128)}) all-reduce(f32[2,2,128]{2,1,0:T(2,128)S(1)} %pad_maximum_fusion.5, f32[2,2,128]{2,1,0:T(2,128)S(1)} %pad_maximum_fusion.6, ...), channel_id=1, replica_groups=mesh['dp'=8,'group'=4] {'dp','group'}, use_global_device_ids=true, to_apply=%region_43.49 | all-reduce | flops 3072 | bytes 24576 | tf_op jit(solution)/shard_map/psum | solution.py:193
  388.4 68.7 %all-reduce.4.cloned.1.call-done = (f32[2,128,384]{2,1,0:T(8,128)}, f32[2,128,128]{2,1,0:T(8,128)}, f32[2,128,512]{2,1,0:T(8,128)}, f32[2,512,128]{2,1,0:T(8,128)}) async-done(((f32[2,128,384]{2,1,0:T(8,128)}, f32[2,128,128]{2,1,0:T(8,128)}, f32[2,128,512]{2,1,0:T(8,128)}, f32[2,512,128]{2,1,0:T(8,128)}), (f32[2,128,384]{2,1,0:T(8,128)}, f32[2,128,128]{2,1,0:T(8,128)}, f32[2,128,512]{2,1,0:T(8,128)}, ...) | async-done | bytes 1572880 | tf_op jit(solution)/shard_map/psum | solution.py:193
  457.1 1.8 copy.314
  460.5 1.9 copy.316
  (647 shorter events, 179.7 us)
Async XLA Ops:
  7.2 12.9 %copy-start = (bf16[32,96,128]{2,1,0:T(8,128)(2,1)S(1)}, bf16[32,96,128]{2,1,0:T(8,128)(2,1)}, u32[]{:S(2)}) copy-start(bf16[32,96,128]{2,1,0:T(8,128)(2,1)} %param.41) | copy-start | bytes 2359300
  11.3 13.8 %all-to-all-start = ((bf16[4,12,1]{1,2,0:T(2,128)(2,1)}), bf16[4,12,1]{1,2,0:T(2,128)(2,1)S(1)}, u32[]{:S(2)}, u32[]{:S(2)}) async-start(bf16[4,12,1]{1,2,0:T(2,128)(2,1)} %copy.173), calls=%async_computation | async-start | bytes 4096 | tf_op jit(solution)/shard_map/all_to_all | solution.py:253
  23.3 48.0 %copy-start.80 = (f32[128]{0:T(128)}, f32[128]{0:T(128)S(1)}, u32[]{:S(2)}) copy-start(f32[128]{0:T(128)S(1)} %get-tuple-element.520) | copy-start | bytes 1540
  23.3 48.0 %copy-start.89 = (f32[128]{0:T(128)}, f32[128]{0:T(128)S(1)}, u32[]{:S(2)}) copy-start(f32[128]{0:T(128)S(1)} %get-tuple-element.479) | copy-start | bytes 1540
  23.3 62.7 %copy-start.82 = (f32[128]{0:T(128)}, f32[128]{0:T(128)S(1)}, u32[]{:S(2)}) copy-start(f32[128]{0:T(128)S(1)} %get-tuple-element.521) | copy-start | bytes 1540
  23.3 62.7 %copy-start.91 = (f32[128]{0:T(128)}, f32[128]{0:T(128)S(1)}, u32[]{:S(2)}) copy-start(f32[128]{0:T(128)S(1)} %get-tuple-element.478) | copy-start | bytes 1540
  25.1 19.4 %all-to-all-start.1 = ((bf16[48,96,128]{2,1,0:T(8,128)(2,1)}), bf16[48,96,128]{2,1,0:T(8,128)(2,1)S(1)}, u32[]{:S(2)}, u32[]{:S(2)}) async-start(bf16[48,96,128]{2,1,0:T(8,128)(2,1)} %get-tuple-element.485), calls=%async_computation.1 | async-start | bytes 2359296 | tf_op jit(solution)/shard_map/all_to_all | solution.py:251
  30.3 24.8 %copy-start.75 = (pred[4608]{0:T(1024)(128)(4,1)}, pred[4608]{0:T(1024)(128)(4,1)S(1)}, u32[]{:S(2)}) copy-start(pred[4608]{0:T(1024)(128)(4,1)S(1)} %lt.257) | copy-start | bytes 13828
  44.5 19.4 %all-to-all-start.3 = ((bf16[48,96,128]{2,1,0:T(8,128)(2,1)}), bf16[48,96,128]{2,1,0:T(8,128)(2,1)S(1)}, u32[]{:S(2)}, u32[]{:S(2)}) async-start(bf16[48,96,128]{2,1,0:T(8,128)(2,1)} %get-tuple-element.486), calls=%async_computation.3 | async-start | bytes 2359296 | tf_op jit(solution)/shard_map/all_to_all | solution.py:252
  55.4 28.9 %copy-start.2 = (bf16[2048,128]{0,1:T(8,128)(2,1)}, bf16[2048,128]{0,1:T(8,128)(2,1)S(1)}, u32[]{:S(2)}) copy-start(bf16[2048,128]{0,1:T(8,128)(2,1)S(1)} %copy.175) | copy-start | bytes 1572868
  55.6 15.7 %copy-start.52 = (f32[2048]{0:T(1024)}, f32[2048]{0:T(1024)S(1)}, u32[]{:S(2)}) copy-start(f32[2048]{0:T(1024)S(1)} %broadcast_multiply_fusion.3) | copy-start | bytes 24580
  86.0 3.7 copy-start.57
  86.0 3.6 copy-start.104
  127.8 4.7 copy-start.26
  127.8 4.7 copy-start.101
  221.2 4.2 copy-start.72
  230.1 4.0 copy-start.83
  230.1 4.0 copy-start.92
  271.1 3.4 copy-start.34
  297.1 8.8 %copy-start.76 = (pred[4608]{0:T(1024)(128)(4,1)S(1)}, pred[4608]{0:T(1024)(128)(4,1)}, u32[]{:S(2)}) copy-start(pred[4608]{0:T(1024)(128)(4,1)} %copy-done.75) | copy-start | bytes 13828
  297.1 8.8 %copy-start.77 = (pred[4608]{0:T(1024)(128)(4,1)S(1)}, pred[4608]{0:T(1024)(128)(4,1)}, u32[]{:S(2)}) copy-start(pred[4608]{0:T(1024)(128)(4,1)} %get-tuple-element.445) | copy-start | bytes 13828
  310.2 3.8 copy-start.47
  310.3 3.8 copy-start.62
  310.3 4.6 copy-start.46
  310.3 4.6 copy-start.48
  310.3 5.5 %copy-start.61 = (f32[1,128,128]{2,1,0:T(8,128)S(1)}, f32[1,128,128]{2,1,0:T(8,128)}, u32[]{:S(2)}) copy-start(f32[1,128,128]{2,1,0:T(8,128)} %convolution_bitcast_fusion.10) | copy-start | bytes 196612
  310.3 7.0 %copy-start.50 = (f32[1,128,384]{2,1,0:T(8,128)S(1)}, f32[1,128,384]{2,1,0:T(8,128)}, u32[]{:S(2)}) copy-start(f32[1,128,384]{2,1,0:T(8,128)} %convolution_bitcast_fusion.8) | copy-start | bytes 589828
  310.3 19.5 %all-to-all-start.2 = ((bf16[48,96,128]{2,1,0:T(8,128)(2,1)}), bf16[48,96,128]{2,1,0:T(8,128)(2,1)S(1)}, u32[]{:S(2)}, u32[]{:S(2)}) async-start(bf16[48,96,128]{2,1,0:T(8,128)(2,1)} %bitcast.572), calls=%async_computation.2 | async-start | bytes 2359296 | tf_op jit(solution)/shard_map/all_to_all | solution.py:321
  314.0 5.0 %copy-start.94 = (f32[128]{0:T(128)S(1)}, f32[128]{0:T(128)}, u32[]{:S(2)}) copy-start(f32[128]{0:T(128)} %get-tuple-element.354) | copy-start | bytes 1540
  314.0 5.0 %copy-start.95 = (f32[128]{0:T(128)S(1)}, f32[128]{0:T(128)}, u32[]{:S(2)}) copy-start(f32[128]{0:T(128)} %get-tuple-element.437) | copy-start | bytes 1540
  314.0 143.1 %all-reduce.4.cloned.1.call-start = ((), (), s32[]{:S(2)}) async-start(), calls=%async_computation.5 | async-start | bytes 3145728 | tf_op jit(solution)/shard_map/psum | solution.py:193
  314.9 4.2 copy-start.96
  314.9 4.3 copy-start.97
  314.9 4.3 copy-start.16
  315.7 3.4 copy-start.115
  315.7 3.4 copy-start.116
  315.8 3.4 copy-start.119
  315.8 3.4 copy-start.120
  319.0 14.3 %copy-start.98 = (f32[128]{0:T(128)S(1)}, f32[128]{0:T(128)}, u32[]{:S(2)}) copy-start(f32[128]{0:T(128)} %get-tuple-element.511) | copy-start | bytes 1540
  319.0 14.3 %copy-start.118 = (f32[128]{0:T(128)S(1)}, f32[128]{0:T(128)}, u32[]{:S(2)}) copy-start(f32[128]{0:T(128)} %get-tuple-element.509) | copy-start | bytes 1540
  319.0 14.4 %copy-start.99 = (f32[128]{0:T(128)S(1)}, f32[128]{0:T(128)}, u32[]{:S(2)}) copy-start(f32[128]{0:T(128)} %get-tuple-element.352) | copy-start | bytes 1540
  319.1 14.4 %copy-start.117 = (f32[128]{0:T(128)S(1)}, f32[128]{0:T(128)}, u32[]{:S(2)}) copy-start(f32[128]{0:T(128)} %get-tuple-element.348) | copy-start | bytes 1540
  319.1 14.4 %copy-start.109 = (f32[512]{0:T(512)S(1)}, f32[512]{0:T(512)}, u32[]{:S(2)}) copy-start(f32[512]{0:T(512)} %get-tuple-element.513) | copy-start | bytes 6148
  319.1 14.4 %copy-start.111 = (f32[512]{0:T(512)S(1)}, f32[512]{0:T(512)}, u32[]{:S(2)}) copy-start(f32[512]{0:T(512)} %get-tuple-element.515) | copy-start | bytes 6148
  329.8 56.4 %all-to-all-start.4 = ((bf16[48,96,128]{2,1,0:T(8,128)(2,1)}), bf16[48,96,128]{2,1,0:T(8,128)(2,1)S(1)}, u32[]{:S(2)}, u32[]{:S(2)}) async-start(bf16[48,96,128]{2,1,0:T(8,128)(2,1)} %bitcast.78), calls=%async_computation.4 | async-start | bytes 2359296 | tf_op jit(solution)/shard_map/all_to_all | solution.py:322
  333.3 53.7 %copy-start.114 = (pred[32]{0:T(512)(128)(4,1)S(1)}, pred[32]{0:T(512)(128)(4,1)}, u32[]{:S(2)}) copy-start(pred[32]{0:T(512)(128)(4,1)} %get-tuple-element.443) | copy-start | bytes 100
  387.0 76.2 %copy-start.1 = (bf16[32,96,128]{2,1,0:T(8,128)(2,1)S(1)}, bf16[32,96,128]{2,1,0:T(8,128)(2,1)}, u32[]{:S(2)}) copy-start(bf16[32,96,128]{2,1,0:T(8,128)(2,1)} %param.41) | copy-start | bytes 2359300
  457.1 5.3 %copy-start.51 = (f32[2,512,128]{2,1,0:T(8,128)S(1)}, f32[2,512,128]{2,1,0:T(8,128)}, u32[]{:S(2)}) copy-start(f32[2,512,128]{2,1,0:T(8,128)} %get-tuple-element.871) | copy-start | bytes 1572868
  (116 other events, 204.7 us)
Sparse Core Ops, SparseCore 0:
  321.7 135.3 all-reduce.3
where the time goes:
time: 480 us; the launch traced here: 470 us
  local copies, waits for them, and re-layouts  140 us (29%)
  matrix products  100 us (21%)
  waiting for transfers between devices  99 us (21%)
  blocking collectives  51.8 us (11%)
  other arithmetic  42.7 us (9%)
  starting transfers between devices  18.5 us (4%)
  between operations  16.2 us (3%)
    psum x1, waiting for transfers between devices, run_layers(): lax.psum((stacked[0], stacked[1], stacked[2], stacked[3], stacked[4], sta...  68.7 us
    psum x1, blocking collectives, run_layers(): lax.psum((stacked[0], stacked[1], stacked[2], stacked[3], stacked[4], sta...  51.8 us
    while x96, local copies, waits for them, and re-layouts  15.8 us
    another operation x16, local copies, waits for them, and re-layouts  15.1 us
    unnamed x228, local copies, waits for them, and re-layouts  12.7 us
    dot_general x8, matrix products, attend_back(): jnp.einsum('bqhd,bkhd->bhqk', d_mixed, values, preferred_element_type=jnp...  11.9 us
    all_to_all x1, waiting for transfers between devices, per_device(): lax.all_to_all(send_tokens, 'group', split_axis=0, concat_axis=0, tiled=T...  11.7 us
    all_to_all x1, waiting for transfers between devices, per_device(): lax.all_to_all(out_slots, 'group', split_axis=0, concat_axis=0, tiled=True)  10.3 us
  transfers between devices with their start and end apart: 6, of which 4 were waited for; matrix products, arithmetic and copies ran while one was open for 6% of the time, Pallas kernels for 0%

commit v1 on v0

v1 whole, which is shorter than its diff:
```python
import functools
import jax
import jax.numpy as jnp
from jax import lax
from jax.sharding import PartitionSpec as P
from jax.experimental import pallas as pl
from jax.experimental.pallas import tpu as pltpu

STEPS = 30
HEAD = 16
LAYERS = 2
BIN = 128
MEMBERS = 3
UNIT_BINS = 2
eps = 1e-05
dead_score = -1e30
LOG2E = 1.4426950408889634
LN2 = 0.6931471805599453
GELU_C = 0.7978845608
GELU_K = 0.044715
bf16 = jnp.bfloat16
f32 = jnp.float32


def dot(a, b):
    return lax.dot_general(a, b, (((1,), (0,)), ((), ())), preferred_element_type=f32)


def dot_nt(a, b):
    return lax.dot_general(a, b, (((1,), (1,)), ((), ())), preferred_element_type=f32)


def plan(lengths, order, count, room, used, mem_traj, mem_off, mem_len, steps_top, nbins_ref):
    trajs = lengths.shape[0]

    def clear(i, c):
        count[i] = 0
        return c

    lax.fori_loop(0, steps_top + 1, clear, 0)

    def tally(t, c):
        s = lengths[t] // 3
        count[s] = count[s] + 1
        return c

    lax.fori_loop(0, trajs, tally, 0)

    def prefix(i, total):
        s = steps_top - i
        n = count[s]
        count[s] = total
        return total + n

    lax.fori_loop(0, steps_top + 1, prefix, 0)

    def rank(t, c):
        s = lengths[t] // 3
        p = count[s]
        order[p] = t
        count[s] = p + 1
        return c

    lax.fori_loop(0, trajs, rank, 0)

    def blank(b):
        room[b] = BIN
        used[b] = 0
        for m in range(MEMBERS):
            mem_traj[b * MEMBERS + m] = 0
            mem_off[b * MEMBERS + m] = BIN
            mem_len[b * MEMBERS + m] = 0

    def put(i, nbins):
        t = order[i]
        length = lengths[t]

        def misfit(b):
            return (b < nbins) & ((room[b] < length) | (used[b] >= MEMBERS))

        b = lax.while_loop(misfit, lambda b: b + 1, 0)

        @pl.when(b == nbins)
        def _():
            blank(b)

        slot = b * MEMBERS + used[b]
        mem_traj[slot] = t
        mem_off[slot] = BIN - room[b]
        mem_len[slot] = length
        used[b] = used[b] + 1
        room[b] = room[b] - length
        return jnp.maximum(nbins, b + 1)

    nbins = lax.fori_loop(0, trajs, put, 0)
    for extra in range(UNIT_BINS - 1):
        blank(nbins + extra)
    nbins_ref[0] = nbins
    return nbins


def norm_parts(x):
    c = x - jnp.mean(x, -1, keepdims=True)
    rstd = lax.rsqrt(jnp.mean(c * c, -1, keepdims=True) + eps)
    return c * rstd, rstd


def norm_back(dy, normed, rstd, gain):
    dg = dy * gain
    return (dg - jnp.mean(dg, -1, keepdims=True) - normed * jnp.mean(dg * normed, -1, keepdims=True)) * rstd


def head_masks(width):
    lane = lax.broadcasted_iota(jnp.int32, (1, width), 1) // HEAD
    return [jnp.where(lane == h, 1.0, 0.0).astype(bf16) for h in range(width // HEAD)]


def row_sum(x):
    return jnp.sum(x, 0, keepdims=True)


def main_kernel(
    lengths, tok, cot, gains, shifts, wqkv, qvb, wout, outb, wup, upb, wdown,
    out, gtok, gsum,
    a_qkv, a_out, a_up, a_down, a_small, e_scr, act_scr, gp_scr,
    order, count, room, used, mem_traj, mem_off, mem_len, nbins_ref,
    *, steps_top,
):
    slot_rows, width = tok.shape[1:]
    hidden = wup.shape[2]
    heads = width // HEAD
    pairs = heads // 2
    unit = BIN * UNIT_BINS
    nbins = plan(lengths, order, count, room, used, mem_traj, mem_off, mem_len, steps_top, nbins_ref)
    units = (nbins + UNIT_BINS - 1) // UNIT_BINS
    for ref in (a_qkv, a_out, a_up, a_down, a_small):
        ref[...] = jnp.zeros_like(ref)

    masks = head_masks(width)
    mask_pairs = [
        jnp.concatenate([jnp.broadcast_to(masks[2 * j], (BIN, width)), jnp.broadcast_to(masks[2 * j + 1], (BIN, width))], 0)
        for j in range(pairs)
    ]

    def pair_rows(x, j):
        return jnp.concatenate([x * masks[2 * j], x * masks[2 * j + 1]], 0)

    def body(u, carry):
        r_iota = lax.broadcasted_iota(jnp.int32, (BIN, slot_rows), 0)
        c_iota = lax.broadcasted_iota(jnp.int32, (BIN, slot_rows), 1)
        q_iota = lax.broadcasted_iota(jnp.int32, (BIN, BIN), 0)
        k_iota = lax.broadcasted_iota(jnp.int32, (BIN, BIN), 1)
        toks, cots, biases = [], [], []
        for b in range(UNIT_BINS):
            x = None
            start = jnp.zeros((BIN, BIN), jnp.int32)
            for m in range(MEMBERS):
                slot = (u * UNIT_BINS + b) * MEMBERS + m
                t, o, n = mem_traj[slot], mem_off[slot], mem_len[slot]
                pick = jnp.where((r_iota - o == c_iota) & (c_iota < n), 1.0, 0.0).astype(bf16)
                both = jnp.concatenate([tok[t], cot[t]], axis=1)
                part = dot(pick, both)
                x = part if x is None else x + part
                start = jnp.where(q_iota >= o + n, o + n, start)
            toks.append(x[:, :width])
            cots.append(x[:, width:])
            biases.append(jnp.where((k_iota <= q_iota) & (k_iota >= start), 0.0, dead_score))
        x = jnp.concatenate(toks, 0)
        g = jnp.concatenate(cots, 0)
        row = lax.broadcasted_iota(jnp.int32, (unit, 1), 0) % BIN
        factor = jnp.where(row % 3 == 0, 0.5, 1.0)
        x = x * factor

        saved = []
        for l in range(LAYERS):
            n1, rstd1 = norm_parts(x)
            h1 = (n1 * gains[l, 0:1, :] + shifts[l, 0:1, :]).astype(bf16)
            joint = dot(h1, wqkv[l])
            q = ((joint[:, :width] + qvb[l, 0:1, :]) * (LOG2E * HEAD ** -0.5)).astype(bf16)
            k = joint[:, width:2 * width].astype(bf16)
            v = (joint[:, 2 * width:] + qvb[l, 1:2, :]).astype(bf16)
            mixed_bins, rl_bins = [], []
            for b in range(UNIT_BINS):
                rows = slice(b * BIN, (b + 1) * BIN)
                qb, kb, vb = q[rows], k[rows], v[rows]
                acc = None
                for j in range(pairs):
                    s = dot_nt(qb, pair_rows(kb, j))
                    es = []
                    for half in range(2):
                        sh = s[:, half * BIN:(half + 1) * BIN] + biases[b]
                        es.append(jnp.exp2(sh - jnp.max(sh, -1, keepdims=True)).astype(bf16))
                    e = jnp.concatenate(es, 1)
                    e_scr[l, rows, 2 * j * BIN:(2 * j + 2) * BIN] = e
                    r = jnp.concatenate([pair_rows(vb, j), mask_pairs[j]], 1)
                    part = dot(e, r)
                    acc = part if acc is None else acc + part
                rl = 1.0 / acc[:, width:]
                mixed_bins.append((acc[:, :width] * rl).astype(bf16))
                rl_bins.append(rl)
            mixed = jnp.concatenate(mixed_bins, 0)
            rl = jnp.concatenate(rl_bins, 0)
            x1 = x + dot(mixed, wout[l]) + outb[l, 0:1, :]
            n2, rstd2 = norm_parts(x1)
            h2 = (n2 * gains[l, 1:2, :] + shifts[l, 1:2, :]).astype(bf16)
            hid = dot(h2, wup[l]) + upb[l:l + 1, :]
            sq = hid * hid
            w = 0.5 * jnp.tanh(hid * (GELU_C + (GELU_C * GELU_K) * sq)) + 0.5
            act = hid * w
            gp = w + (act * (1.0 - w)) * (2 * GELU_C + (6 * GELU_C * GELU_K) * sq)
            act_b = act.astype(bf16)
            act_scr[l] = act_b
            gp_scr[l] = gp.astype(bf16)
            saved.append((n1, rstd1, h1, q, k, v, mixed, rl, n2, rstd2, h2))
            x = x1 + dot(act_b, wdown[l]) + outb[l, 1:2, :]

        out_b = x.astype(bf16)
        for l in reversed(range(LAYERS)):
            n1, rstd1, h1, q, k, v, mixed, rl, n2, rstd2, h2 = saved[l]
            e2 = g.astype(bf16)
            a_down[l] += dot(e2.T, act_scr[l])
            a_small[l, 7:8, :] += row_sum(e2.astype(f32))
            da = dot_nt(e2, wdown[l])
            du = (da * gp_scr[l].astype(f32)).astype(bf16)
            a_up[l] += dot(h2.T, du)
            dus = row_sum(du.astype(f32))
            for c in range(hidden // width):
                a_small[l, 8 + c:9 + c, :] += dus[:, c * width:(c + 1) * width]
            dh2 = dot_nt(du, wup[l])
            a_small[l, 1:2, :] += row_sum(dh2 * n2)
            a_small[l, 3:4, :] += row_sum(dh2)
            g1 = g + norm_back(dh2, n2, rstd2, gains[l, 1:2, :])
            e1 = g1.astype(bf16)
            a_out[l] += dot(mixed.T, e1)
            a_small[l, 6:7, :] += row_sum(e1.astype(f32))
            dm = dot_nt(e1, wout[l])
            dm1 = dm * rl
            dmo = -(dm1 * mixed.astype(f32))
            dm1 = dm1.astype(bf16)
            dmo = dmo.astype(bf16)
            dqkv_bins = []
            for b in range(UNIT_BINS):
                rows = slice(b * BIN, (b + 1) * BIN)
                qb, kb, vb = q[rows], k[rows], v[rows]
                lhs = jnp.concatenate([dm1[rows], dmo[rows]], 1)
                dm_t = dm1[rows].T
                q_t = qb.T
                dq = None
                dv_t, dk_t = [], []
                for j in range(pairs):
                    e = e_scr[l, rows, 2 * j * BIN:(2 * j + 2) * BIN]
                    r = jnp.concatenate([pair_rows(vb, j), mask_pairs[j]], 1)
                    ds = e * dot_nt(lhs, r).astype(bf16)
                    part = dot(ds, pair_rows(kb, j))
                    dq = part if dq is None else dq + part
                    top, mid, low = 2 * j * HEAD, (2 * j + 1) * HEAD, (2 * j + 2) * HEAD
                    pv = dot(dm_t[top:low], e)
                    dv_t += [pv[:HEAD, :BIN], pv[HEAD:, BIN:]]
                    pk = dot(q_t[top:low], ds)
                    dk_t += [pk[:HEAD, :BIN], pk[HEAD:, BIN:]]
                dv = jnp.concatenate(dv_t, 0).T
                dk = jnp.concatenate(dk_t, 0).T * LN2
                dqkv_bins.append(jnp.concatenate([(dq * HEAD ** -0.5).astype(bf16), dk.astype(bf16), dv.astype(bf16)], 1))
            dqkv = jnp.concatenate(dqkv_bins, 0)
            a_qkv[l] += dot(h1.T, dqkv)
            sums = row_sum(dqkv.astype(f32))
            a_small[l, 4:5, :] += sums[:, :width]
            a_small[l, 5:6, :] += sums[:, 2 * width:]
            dh = dot_nt(dqkv, wqkv[l])
            a_small[l, 0:1, :] += row_sum(dh * n1)
            a_small[l, 2:3, :] += row_sum(dh)
            g = g1 + norm_back(dh, n1, rstd1, gains[l, 0:1, :])

        grad_b = (g * factor).astype(bf16)
        s_iota = lax.broadcasted_iota(jnp.int32, (slot_rows, BIN), 0)
        p_iota = lax.broadcasted_iota(jnp.int32, (slot_rows, BIN), 1)
        both = jnp.concatenate([out_b, grad_b], 1)
        for b in range(UNIT_BINS):
            for m in range(MEMBERS):
                slot = (u * UNIT_BINS + b) * MEMBERS + m
                t, o, n = mem_traj[slot], mem_off[slot], mem_len[slot]
                pick = jnp.where((p_iota - o == s_iota) & (s_iota < n), 1.0, 0.0).astype(bf16)
                rows = dot(pick, both[b * BIN:(b + 1) * BIN]).astype(bf16)

                @pl.when(n > 0)
                def _():
                    out[t] = rows[:, :width]
                    gtok[t] = rows[:, width:]
        return carry

    lax.fori_loop(0, units, body, 0)

    per_layer = gsum.shape[0] // LAYERS
    for l in range(LAYERS):
        at = l * per_layer
        for c in range(3):
            gsum[at:at + width, :] = a_qkv[l, :, c * width:(c + 1) * width].astype(gsum.dtype)
            at += width
        gsum[at:at + width, :] = a_out[l].astype(gsum.dtype)
        at += width
        for c in range(hidden // width):
            gsum[at:at + width, :] = a_up[l, :, c * width:(c + 1) * width].astype(gsum.dtype)
            at += width
        for c in range(hidden // width):
            gsum[at:at + width, :] = a_down[l, :, c * width:(c + 1) * width].T.astype(gsum.dtype)
            at += width
        gsum[at:at + 64, :] = a_small[l].astype(gsum.dtype)


def main_call(args, steps_top):
    tokens, lengths, gains, shifts, wqkv, qvb, wout, outb, wup, upb, wdown, cot = args
    trajs, slot_rows, width = tokens.shape
    hidden = wup.shape[2]
    unit = BIN * UNIT_BINS
    bins = trajs + UNIT_BINS
    per_layer = 4 * width + 2 * hidden + 64
    vm = pl.BlockSpec(memory_space=pltpu.VMEM)
    sm = pl.BlockSpec(memory_space=pltpu.SMEM)
    return pl.pallas_call(
        functools.partial(main_kernel, steps_top=steps_top),
        out_shape=(
            jax.ShapeDtypeStruct(tokens.shape, bf16),
            jax.ShapeDtypeStruct(tokens.shape, bf16),
            jax.ShapeDtypeStruct((LAYERS * per_layer, width), bf16),
        ),
        in_specs=[sm] + [vm] * 11,
        out_specs=(vm, vm, vm),
        scratch_shapes=[
            pltpu.VMEM((LAYERS, width, 3 * width), f32),
            pltpu.VMEM((LAYERS, width, width), f32),
            pltpu.VMEM((LAYERS, width, hidden), f32),
            pltpu.VMEM((LAYERS, width, hidden), f32),
            pltpu.VMEM((LAYERS, 64, width), f32),
            pltpu.VMEM((LAYERS, unit, width // HEAD * BIN), bf16),
            pltpu.VMEM((LAYERS, unit, hidden), bf16),
            pltpu.VMEM((LAYERS, unit, hidden), bf16),
            pltpu.SMEM((trajs,), jnp.int32),
            pltpu.SMEM((steps_top + 1,), jnp.int32),
            pltpu.SMEM((bins,), jnp.int32),
            pltpu.SMEM((bins,), jnp.int32),
            pltpu.SMEM((bins * MEMBERS,), jnp.int32),
            pltpu.SMEM((bins * MEMBERS,), jnp.int32),
            pltpu.SMEM((bins * MEMBERS,), jnp.int32),
            pltpu.SMEM((1,), jnp.int32),
        ],
        compiler_params=pltpu.CompilerParams(vmem_limit_bytes=56 * 1024 * 1024),
        name="layers",
    )(lengths, tokens, cot, gains, shifts, wqkv, qvb, wout, outb, wup, upb, wdown)


AXES = ("dp", "group")
SPLIT_BITS = 3


def exchange(x, bit, devices):
    return lax.ppermute(x, AXES, [(i, i ^ bit) for i in range(devices)])


def all_sum(x, mesh_shape):
    devices = mesh_shape["dp"] * mesh_shape["group"]
    index = lax.axis_index("dp") * mesh_shape["group"] + lax.axis_index("group")
    bits = [1 << i for i in range(devices.bit_length() - 1)]
    kept = []
    for bit in bits[:SPLIT_BITS]:
        half = x.shape[0] // 2
        low = (index // bit) % 2 == 0
        mine = jnp.where(low, x[:half], x[half:])
        other = jnp.where(low, x[half:], x[:half])
        x = (mine.astype(f32) + exchange(other, bit, devices).astype(f32)).astype(bf16)
        kept.append((bit, low))
    for bit in bits[SPLIT_BITS:]:
        x = (x.astype(f32) + exchange(x, bit, devices).astype(f32)).astype(bf16)
    for bit, low in reversed(kept):
        other = exchange(x, bit, devices)
        x = jnp.where(low, jnp.concatenate([x, other]), jnp.concatenate([other, x]))
    return x


def solution(mesh):
    mesh_shape = dict(mesh.shape)

    def per_device(*args):
        width = args[0].shape[2]
        hidden = args[8].shape[2]
        output, grad_tokens, sums = main_call(args, STEPS)
        total = all_sum(sums, mesh_shape).astype(f32).reshape(LAYERS, -1, width)

        def wide(first, parts):
            return jnp.concatenate([total[:, first + i * width:first + (i + 1) * width] for i in range(parts)], 2)

        up_at = 4 * width
        down_at = up_at + hidden
        small = total[:, down_at + hidden:]
        return (
            output,
            grad_tokens,
            small[:, 0:2],
            small[:, 2:4],
            wide(0, 3),
            small[:, 4:6],
            total[:, 3 * width:4 * width],
            small[:, 6:8],
            wide(up_at, hidden // width),
            small[:, 8:8 + hidden // width].reshape(LAYERS, hidden),
            total[:, down_at:down_at + hidden],
        )

    rows = P(AXES, None, None)
    return jax.shard_map(
        per_device,
        mesh=mesh,
        in_specs=(rows, P(AXES)) + (P(),) * 9 + (rows,),
        out_specs=(rows, rows) + (P(),) * 9,
        check_vma=False,
    )
```

time: 480 us -> 127 us (0.26); the launches traced: 470 us -> 127 us
  local copies, waits for them, and re-layouts: 140 us -> 2.79 us
  matrix products: 100 us -> 0 us
  Pallas kernels: 0 us -> 71.2 us
  waiting for transfers between devices: 99 us -> 29.9 us
  blocking collectives: 51.8 us -> 0 us
  other arithmetic: 42.7 us -> 3.72 us
  between operations: 16.2 us -> 0.75 us
    dot_general x80 -> x0, matrix products: 100 us -> none  [the longest x8 11.9 us: attend_back(): jnp.einsum('bqhd,bkhd->bhqk', d_mixed, values, preferred_element_type=jnp...]
    pallas_call x0 -> x1, Pallas kernels: none -> 71.2 us  [main_call(): pl.pallas_call(functools.partial(main_kernel, steps_top=steps_top), out_s...]
    psum x1 -> x0, waiting for transfers between devices: 68.7 us -> none  [run_layers(): lax.psum((stacked[0], stacked[1], stacked[2], stacked[3], stacked[4], sta...]
    psum x1 -> x0, blocking collectives: 51.8 us -> none  [run_layers(): lax.psum((stacked[0], stacked[1], stacked[2], stacked[3], stacked[4], sta...]
    gather x15 -> x0, local copies, waits for them, and re-layouts: 38.3 us -> none  [the longest x1 8.79 us: per_device(): jnp.take(out_rows, back_index, axis=0)]
    all_to_all x5 -> x0, waiting for transfers between devices: 30.2 us -> none  [the longest x1 11.7 us: per_device(): lax.all_to_all(send_tokens, 'group', split_axis=0, concat_axis=0, tiled=T...]
    ppermute x0 -> x8, waiting for transfers between devices: none -> 29.9 us  [exchange(): return lax.ppermute(x, AXES, [(i, i ^ bit) for i in range(devices)])]
    while x102 -> x0, local copies, waits for them, and re-layouts: 21.4 us -> none
  transfers between devices with their start and end apart: 6 -> 8, of which waited for: 4 -> 8; matrix products, arithmetic and copies ran while one was open for 6% -> 0% of each run, Pallas kernels for 0% -> 0%
where the time goes in v1:
time: 127 us
  Pallas kernels  71.2 us (56%)
  waiting for transfers between devices  29.9 us (24%)
  starting transfers between devices  18.4 us (14%)
  other arithmetic  3.72 us (3%)
  local copies, waits for them, and re-layouts  2.79 us (2%)
    pallas_call x1, Pallas kernels, main_call(): pl.pallas_call(functools.partial(main_kernel, steps_top=steps_top), out_s...  71.2 us
    ppermute x8, waiting for transfers between devices, exchange(): return lax.ppermute(x, AXES, [(i, i ^ bit) for i in range(devices)])  29.9 us
    ppermute x8, starting transfers between devices, exchange(): return lax.ppermute(x, AXES, [(i, i ^ bit) for i in range(devices)])  18.4 us
  transfers between devices with their start and end apart: 8, of which 8 were waited for; matrix products, arithmetic and copies ran while one was open for 0% of the time, Pallas kernels for 0%

profile of v1, /device:TPU:0, one launch (start us, length us, event | category | flops | bytes accessed | tf_op | source)
XLA Modules:
  0.0 126.8 jit_solution(12742522214463690309)
XLA Ops:
  0.7 71.2 %layers.1 = (bf16[32,96,128]{2,1,0:T(8,128)(2,1)}, bf16[32,96,128]{2,1,0:T(8,128)(2,1)}, bf16[3200,128]{1,0:T(8,128)(2,1)}) custom-call(s32[32]{0:T(128)} %lengths.1, bf16[32,96,128]{2,1,0:T(8,128)(2,1)} %tok.1, bf16[32,96,128]{2,1,0:T(8,128)(2,1)} %cot.1, f32[2,2,128]{2,1,0:T(2,128)} %gains.1, f32[2,2,128]{2,1,0:T(2,128)} %shifts.1, ...), custom_call_target="tpu_custom_call" | custom-call | tf_op jit(solution)/shard_map/layers/pallas_call | solution.py:319
  71.9 0.0 copy-start
  71.9 1.2 broadcast_select_fusion
  73.1 0.8 collective-permute-start
  73.9 1.4 %collective-permute-done = bf16[1600,128]{1,0:T(8,128)(2,1)S(1)} collective-permute-done((bf16[1600,128]{1,0:T(8,128)(2,1)S(1)}, bf16[1600,128]{1,0:T(8,128)(2,1)S(1)}, u32[]{:S(2)}, u32[]{:S(2)}) %collective-permute-start) | collective-permute-done | bytes 409632 | tf_op jit(solution)/shard_map/ppermute | solution.py:356
  75.3 0.0 copy-done
  75.3 0.2 add_convert_fusion
  75.5 11.6 %collective-permute-start.1 = (bf16[800,128]{1,0:T(8,128)(2,1)S(1)}, bf16[800,128]{1,0:T(8,128)(2,1)S(1)}, u32[]{:S(2)}, u32[]{:S(2)}) collective-permute-start(bf16[800,128]{1,0:T(8,128)(2,1)S(1)} %broadcast_select_fusion.1), channel_id=1, source_target_pairs={{0,2},{1,3},{2,0},{3,1},{4,6},{5,7},{6,4},{7,5},{8,10},{9,11},{10,... | collective-permute-start | bytes 614408 | tf_op jit(solution)/shard_map/ppermute | solution.py:356
  87.1 5.6 %collective-permute-done.1 = bf16[800,128]{1,0:T(8,128)(2,1)S(1)} collective-permute-done((bf16[800,128]{1,0:T(8,128)(2,1)S(1)}, bf16[800,128]{1,0:T(8,128)(2,1)S(1)}, u32[]{:S(2)}, u32[]{:S(2)}) %collective-permute-start.1) | collective-permute-done | bytes 204832 | tf_op jit(solution)/shard_map/ppermute | solution.py:356
  92.7 0.1 add_convert_fusion.1
  92.8 0.1 collective-permute-start.2
  92.9 4.6 %collective-permute-done.2 = bf16[400,128]{1,0:T(8,128)(2,1)S(1)} collective-permute-done((bf16[400,128]{1,0:T(8,128)(2,1)S(1)}, bf16[400,128]{1,0:T(8,128)(2,1)S(1)}, u32[]{:S(2)}, u32[]{:S(2)}) %collective-permute-start.2) | collective-permute-done | bytes 102432 | tf_op jit(solution)/shard_map/ppermute | solution.py:356
  97.6 1.5 %collective-permute-start.3 = (bf16[400,128]{1,0:T(8,128)(2,1)S(1)}, bf16[400,128]{1,0:T(8,128)(2,1)S(1)}, u32[]{:S(2)}, u32[]{:S(2)}) collective-permute-start(bf16[400,128]{1,0:T(8,128)(2,1)S(1)} %add_convert_fusion.4), channel_id=1, source_target_pairs={{0,8},{1,9},{2,10},{3,11},{4,12},{5,13},{6,14},{7,15},{8,0},{9,1},... | collective-permute-start | bytes 307208 | tf_op jit(solution)/shard_map/ppermute | solution.py:356
  99.1 3.2 %collective-permute-done.3 = bf16[400,128]{1,0:T(8,128)(2,1)S(1)} collective-permute-done((bf16[400,128]{1,0:T(8,128)(2,1)S(1)}, bf16[400,128]{1,0:T(8,128)(2,1)S(1)}, u32[]{:S(2)}, u32[]{:S(2)}) %collective-permute-start.3) | collective-permute-done | bytes 102432 | tf_op jit(solution)/shard_map/ppermute | solution.py:356
  102.3 3.4 %collective-permute-start.4 = (bf16[400,128]{1,0:T(8,128)(2,1)S(1)}, bf16[400,128]{1,0:T(8,128)(2,1)S(1)}, u32[]{:S(2)}, u32[]{:S(2)}) collective-permute-start(bf16[400,128]{1,0:T(8,128)(2,1)S(1)} %add_convert_fusion.3), channel_id=1, source_target_pairs={{0,16},{1,17},{2,18},{3,19},{4,20},{5,21},{6,22},{7,23},{8,24},{9,... | collective-permute-start | bytes 307208 | tf_op jit(solution)/shard_map/ppermute | solution.py:356
  105.7 3.7 %collective-permute-done.4 = bf16[400,128]{1,0:T(8,128)(2,1)S(1)} collective-permute-done((bf16[400,128]{1,0:T(8,128)(2,1)S(1)}, bf16[400,128]{1,0:T(8,128)(2,1)S(1)}, u32[]{:S(2)}, u32[]{:S(2)}) %collective-permute-start.4) | collective-permute-done | bytes 102432 | tf_op jit(solution)/shard_map/ppermute | solution.py:356
  109.5 0.1 collective-permute-start.5
  109.6 4.6 %collective-permute-done.5 = bf16[400,128]{1,0:T(8,128)(2,1)S(1)} collective-permute-done((bf16[400,128]{1,0:T(8,128)(2,1)S(1)}, bf16[400,128]{1,0:T(8,128)(2,1)S(1)}, u32[]{:S(2)}, u32[]{:S(2)}) %collective-permute-start.5) | collective-permute-done | bytes 102432 | tf_op jit(solution)/shard_map/ppermute | solution.py:356
  114.2 0.1 maximum_select_fusion.2
  114.3 0.9 collective-permute-start.6
  115.2 4.9 %collective-permute-done.6 = bf16[800,128]{1,0:T(8,128)(2,1)S(1)} collective-permute-done((bf16[800,128]{1,0:T(8,128)(2,1)S(1)}, bf16[800,128]{1,0:T(8,128)(2,1)S(1)}, u32[]{:S(2)}, u32[]{:S(2)}) %collective-permute-start.6) | collective-permute-done | bytes 204832 | tf_op jit(solution)/shard_map/ppermute | solution.py:356
  120.1 0.1 maximum_select_fusion.1
  120.2 0.1 collective-permute-start.7
  120.3 1.7 %collective-permute-done.7 = bf16[1600,128]{1,0:T(8,128)(2,1)S(1)} collective-permute-done((bf16[1600,128]{1,0:T(8,128)(2,1)S(1)}, bf16[1600,128]{1,0:T(8,128)(2,1)S(1)}, u32[]{:S(2)}, u32[]{:S(2)}) %collective-permute-start.7) | collective-permute-done | bytes 409632 | tf_op jit(solution)/shard_map/ppermute | solution.py:356
  122.1 0.2 maximum_select_fusion
  122.3 0.8 fusion
  123.0 0.1 convert.1
  123.1 0.8 slice.109
  124.0 0.6 fusion.1
  124.6 0.6 copy.25
  125.2 0.8 pad_maximum_fusion.1
  125.9 0.8 pad_maximum_fusion
  (6 shorter events, 0.1 us)
Async XLA Ops:
  71.9 3.4 %copy-start = (bf16[3200,128]{1,0:T(8,128)(2,1)S(1)}, bf16[3200,128]{1,0:T(8,128)(2,1)}, u32[]{:S(2)}) copy-start(bf16[3200,128]{1,0:T(8,128)(2,1)} %get-tuple-element.16) | copy-start | bytes 2457604
  73.1 2.2 %collective-permute-start = (bf16[1600,128]{1,0:T(8,128)(2,1)S(1)}, bf16[1600,128]{1,0:T(8,128)(2,1)S(1)}, u32[]{:S(2)}, u32[]{:S(2)}) collective-permute-start(bf16[1600,128]{1,0:T(8,128)(2,1)S(1)} %broadcast_select_fusion), channel_id=1, source_target_pairs={{0,1},{1,0},{2,3},{3,2},{4,5},{5,4},{6,7},{7,6},{8,9},{9,8},{10,11... | collective-permute-start | bytes 1228808 | tf_op jit(solution)/shard_map/ppermute | solution.py:356
  75.5 17.2 %collective-permute-start.1 = (bf16[800,128]{1,0:T(8,128)(2,1)S(1)}, bf16[800,128]{1,0:T(8,128)(2,1)S(1)}, u32[]{:S(2)}, u32[]{:S(2)}) collective-permute-start(bf16[800,128]{1,0:T(8,128)(2,1)S(1)} %broadcast_select_fusion.1), channel_id=1, source_target_pairs={{0,2},{1,3},{2,0},{3,1},{4,6},{5,7},{6,4},{7,5},{8,10},{9,11},{10,... | collective-permute-start | bytes 614408 | tf_op jit(solution)/shard_map/ppermute | solution.py:356
  92.8 4.7 %collective-permute-start.2 = (bf16[400,128]{1,0:T(8,128)(2,1)S(1)}, bf16[400,128]{1,0:T(8,128)(2,1)S(1)}, u32[]{:S(2)}, u32[]{:S(2)}) collective-permute-start(bf16[400,128]{1,0:T(8,128)(2,1)S(1)} %broadcast_select_fusion.2), channel_id=1, source_target_pairs={{0,4},{1,5},{2,6},{3,7},{4,0},{5,1},{6,2},{7,3},{8,12},{9,13},{10,... | collective-permute-start | bytes 307208 | tf_op jit(solution)/shard_map/ppermute | solution.py:356
  97.6 4.7 %collective-permute-start.3 = (bf16[400,128]{1,0:T(8,128)(2,1)S(1)}, bf16[400,128]{1,0:T(8,128)(2,1)S(1)}, u32[]{:S(2)}, u32[]{:S(2)}) collective-permute-start(bf16[400,128]{1,0:T(8,128)(2,1)S(1)} %add_convert_fusion.4), channel_id=1, source_target_pairs={{0,8},{1,9},{2,10},{3,11},{4,12},{5,13},{6,14},{7,15},{8,0},{9,1},... | collective-permute-start | bytes 307208 | tf_op jit(solution)/shard_map/ppermute | solution.py:356
  102.3 7.2 %collective-permute-start.4 = (bf16[400,128]{1,0:T(8,128)(2,1)S(1)}, bf16[400,128]{1,0:T(8,128)(2,1)S(1)}, u32[]{:S(2)}, u32[]{:S(2)}) collective-permute-start(bf16[400,128]{1,0:T(8,128)(2,1)S(1)} %add_convert_fusion.3), channel_id=1, source_target_pairs={{0,16},{1,17},{2,18},{3,19},{4,20},{5,21},{6,22},{7,23},{8,24},{9,... | collective-permute-start | bytes 307208 | tf_op jit(solution)/shard_map/ppermute | solution.py:356
  109.5 4.7 %collective-permute-start.5 = (bf16[400,128]{1,0:T(8,128)(2,1)S(1)}, bf16[400,128]{1,0:T(8,128)(2,1)S(1)}, u32[]{:S(2)}, u32[]{:S(2)}) collective-permute-start(bf16[400,128]{1,0:T(8,128)(2,1)S(1)} %add_convert_fusion.2), channel_id=1, source_target_pairs={{0,4},{1,5},{2,6},{3,7},{4,0},{5,1},{6,2},{7,3},{8,12},{9,13},{10,... | collective-permute-start | bytes 307208 | tf_op jit(solution)/shard_map/ppermute | solution.py:356
  114.3 5.8 %collective-permute-start.6 = (bf16[800,128]{1,0:T(8,128)(2,1)S(1)}, bf16[800,128]{1,0:T(8,128)(2,1)S(1)}, u32[]{:S(2)}, u32[]{:S(2)}) collective-permute-start(bf16[800,128]{1,0:T(8,128)(2,1)S(1)} %maximum_select_fusion.2), channel_id=1, source_target_pairs={{0,2},{1,3},{2,0},{3,1},{4,6},{5,7},{6,4},{7,5},{8,10},{9,11},{10,... | collective-permute-start | bytes 614408 | tf_op jit(solution)/shard_map/ppermute | solution.py:356
  120.2 1.8 %collective-permute-start.7 = (bf16[1600,128]{1,0:T(8,128)(2,1)S(1)}, bf16[1600,128]{1,0:T(8,128)(2,1)S(1)}, u32[]{:S(2)}, u32[]{:S(2)}) collective-permute-start(bf16[1600,128]{1,0:T(8,128)(2,1)S(1)} %maximum_select_fusion.1), channel_id=1, source_target_pairs={{0,1},{1,0},{2,3},{3,2},{4,5},{5,4},{6,7},{7,6},{8,9},{9,8},{10,11... | collective-permute-start | bytes 1228808 | tf_op jit(solution)/shard_map/ppermute | solution.py:356

commit v2 on v1

v2 whole, which is shorter than its diff:
```python
import functools
import jax
import jax.numpy as jnp
from jax import lax
from jax.sharding import PartitionSpec as P
from jax.experimental import pallas as pl
from jax.experimental.pallas import tpu as pltpu

STEPS = 30
HEAD = 16
LAYERS = 2
BIN = 128
SMALL = 64
MEMBERS = 2
UNIT_BINS = 8
eps = 1e-05
dead_score = -1e30
LOG2E = 1.4426950408889634
LN2 = 0.6931471805599453
GELU_C = 0.7978845608
GELU_K = 0.044715
bf16 = jnp.bfloat16
f32 = jnp.float32


def dot(a, b):
    return lax.dot_general(a, b, (((1,), (0,)), ((), ())), preferred_element_type=f32)


def dot_nt(a, b):
    return lax.dot_general(a, b, (((1,), (1,)), ((), ())), preferred_element_type=f32)


def plan(lengths, order, count, mem_traj, mem_off, mem_len, steps_top):
    trajs = lengths.shape[0]
    pairs = trajs // 2

    def clear(i, c):
        count[i] = 0
        return c

    lax.fori_loop(0, steps_top + 1, clear, 0, unroll=True)

    def tally(t, c):
        s = lengths[t] // 3
        count[s] = count[s] + 1
        return c

    lax.fori_loop(0, trajs, tally, 0, unroll=4)

    def prefix(i, total):
        s = steps_top - i
        n = count[s]
        count[s] = total
        return total + n

    lax.fori_loop(0, steps_top + 1, prefix, 0, unroll=True)

    def rank(t, c):
        s = lengths[t] // 3
        p = count[s]
        order[p] = t
        count[s] = p + 1
        return c

    lax.fori_loop(0, trajs, rank, 0, unroll=4)

    def member(slot, t, offset, length):
        mem_traj[slot] = t
        mem_off[slot] = offset
        mem_len[slot] = length

    def pair(p, nbins):
        long, short = order[p], order[trajs - 1 - p]
        length, length_two = lengths[long], lengths[short]
        fits = length + length_two <= BIN
        member(2 * p, long, 0, length)
        member(2 * p + 1, short, length, jnp.where(fits, length_two, 0))
        member(2 * nbins, short, 0, length_two)
        member(2 * nbins + 1, short, length_two, 0)
        return nbins + jnp.where(fits, 0, 1)

    nbins = lax.fori_loop(0, pairs, pair, pairs)
    units = (nbins + UNIT_BINS - 1) // UNIT_BINS

    def pad(i, c):
        member(i, 0, BIN, 0)
        return c

    lax.fori_loop(2 * nbins, 2 * UNIT_BINS * units, pad, 0)
    return units


def norm_parts(x):
    c = x - jnp.mean(x, -1, keepdims=True)
    rstd = lax.rsqrt(jnp.mean(c * c, -1, keepdims=True) + eps)
    return c * rstd, rstd


def norm_back(dy, normed, rstd, gain):
    dg = dy * gain
    return (dg - jnp.mean(dg, -1, keepdims=True) - normed * jnp.mean(dg * normed, -1, keepdims=True)) * rstd


def head_masks(width):
    lane = lax.broadcasted_iota(jnp.int32, (1, width), 1) // HEAD
    return [jnp.where(lane == h, 1.0, 0.0).astype(bf16) for h in range(width // HEAD)]


def row_sum(x):
    return jnp.sum(x, 0, keepdims=True)


def main_kernel(
    lengths, parity, tok_hbm, cot_hbm, gains, shifts, wqkv, qvb, wout, outb, wup, upb, wdown,
    out_hbm, gtok_hbm, mine_hbm, other_hbm,
    tok, cot, out, gtok, gsum,
    a_qkv, a_out, a_up, a_down, a_small, e_scr, act_scr, gp_scr,
    order, count, mem_traj, mem_off, mem_len, sems,
    *, steps_top,
):
    trajs, slot_rows, width = tok.shape
    hidden = wup.shape[2]
    heads = width // HEAD
    pairs = heads // 2
    unit = BIN * UNIT_BINS
    loads = [pltpu.make_async_copy(tok_hbm, tok, sems.at[0]), pltpu.make_async_copy(cot_hbm, cot, sems.at[1])]
    for copy in loads:
        copy.start()
    for ref in (a_qkv, a_out, a_up, a_down, a_small):
        ref[...] = jnp.zeros_like(ref)
    units = plan(lengths, order, count, mem_traj, mem_off, mem_len, steps_top)
    for copy in loads:
        copy.wait()

    masks = head_masks(width)
    mask_pairs = [
        jnp.concatenate([jnp.broadcast_to(masks[2 * j], (BIN, width)), jnp.broadcast_to(masks[2 * j + 1], (BIN, width))], 0)
        for j in range(pairs)
    ]

    def pair_rows(x, j):
        return jnp.concatenate([x * masks[2 * j], x * masks[2 * j + 1]], 0)

    blank = jnp.zeros((HEAD, BIN), bf16)
    ones = jnp.ones((HEAD, BIN), bf16)

    def pair_columns(xt, j):
        lo, mid, hi = 2 * j * HEAD, (2 * j + 1) * HEAD, (2 * j + 2) * HEAD
        parts = [
            jnp.concatenate([xt[lo:mid], blank], 1),
            jnp.concatenate([blank, xt[mid:hi]], 1),
        ]
        if j > 0:
            parts = [jnp.zeros((lo, 2 * BIN), bf16)] + parts
        if hi < width:
            parts = parts + [jnp.zeros((width - hi, 2 * BIN), bf16)]
        return jnp.concatenate(parts, 0)

    ones_t = jnp.ones((width, BIN), bf16)
    mask_columns = [pair_columns(ones_t, j) for j in range(pairs)]

    def body(u, carry):
        r_iota = lax.broadcasted_iota(jnp.int32, (BIN, slot_rows), 0)
        c_iota = lax.broadcasted_iota(jnp.int32, (BIN, slot_rows), 1)
        q_iota = lax.broadcasted_iota(jnp.int32, (BIN, BIN), 0)
        k_iota = lax.broadcasted_iota(jnp.int32, (BIN, BIN), 1)
        toks, cots, biases = [], [], []
        for b in range(UNIT_BINS):
            x = None
            start = jnp.zeros((BIN, BIN), jnp.int32)
            for m in range(MEMBERS):
                slot = (u * UNIT_BINS + b) * MEMBERS + m
                t, o, n = mem_traj[slot], mem_off[slot], mem_len[slot]
                pick = jnp.where((r_iota - o == c_iota) & (c_iota < n), 1.0, 0.0).astype(bf16)
                both = jnp.concatenate([tok[t], cot[t]], axis=1)
                part = dot(pick, both)
                x = part if x is None else x + part
                start = jnp.where(q_iota >= o + n, o + n, start)
            toks.append(x[:, :width])
            cots.append(x[:, width:])
            biases.append(jnp.where((k_iota <= q_iota) & (k_iota >= start), 0.0, dead_score))
        x = jnp.concatenate(toks, 0)
        g = jnp.concatenate(cots, 0)
        row = lax.broadcasted_iota(jnp.int32, (unit, 1), 0) % BIN
        factor = jnp.where(row % 3 == 0, 0.5, 1.0)
        x = x * factor

        saved = []
        for l in range(LAYERS):
            n1, rstd1 = norm_parts(x)
            h1 = (n1 * gains[l, 0:1, :] + shifts[l, 0:1, :]).astype(bf16)
            joint = dot(h1, wqkv[l])
            q = ((joint[:, :width] + qvb[l, 0:1, :]) * (LOG2E * HEAD ** -0.5)).astype(bf16)
            k = joint[:, width:2 * width].astype(bf16)
            v = (joint[:, 2 * width:] + qvb[l, 1:2, :]).astype(bf16)
            bins = range(UNIT_BINS)
            rows_of = [slice(b * BIN, (b + 1) * BIN) for b in bins]
            acc = [None] * UNIT_BINS

            def scores(j):
                return [dot_nt(q[rows_of[b]], pair_rows(k[rows_of[b]], j)) for b in bins]

            ahead = scores(0)
            for j in range(pairs):
                s = ahead
                if j + 1 < pairs:
                    ahead = scores(j + 1)
                es = []
                for b in bins:
                    halves = []
                    for half in range(2):
                        sh = s[b][:, half * BIN:(half + 1) * BIN] + biases[b]
                        halves.append(jnp.exp2(sh - jnp.max(sh, -1, keepdims=True)).astype(bf16))
                    e = jnp.concatenate(halves, 1)
                    e_scr[l, rows_of[b], 2 * j * BIN:(2 * j + 2) * BIN] = e
                    es.append(e)
                for b in bins:
                    r = jnp.concatenate([pair_rows(v[rows_of[b]], j), mask_pairs[j]], 1)
                    part = dot(es[b], r)
                    acc[b] = part if acc[b] is None else acc[b] + part
            mixed_bins, rl_bins = [], []
            for b in bins:
                rl = 1.0 / acc[b][:, width:]
                mixed_bins.append((acc[b][:, :width] * rl).astype(bf16))
                rl_bins.append(rl)
            mixed = jnp.concatenate(mixed_bins, 0)
            rl = jnp.concatenate(rl_bins, 0)
            x1 = x + dot(mixed, wout[l]) + outb[l, 0:1, :]
            n2, rstd2 = norm_parts(x1)
            h2 = (n2 * gains[l, 1:2, :] + shifts[l, 1:2, :]).astype(bf16)
            hid = dot(h2, wup[l]) + upb[l:l + 1, :]
            sq = hid * hid
            w = 0.5 * jnp.tanh(hid * (GELU_C + (GELU_C * GELU_K) * sq)) + 0.5
            act = hid * w
            gp = w + (act * (1.0 - w)) * (2 * GELU_C + (6 * GELU_C * GELU_K) * sq)
            act_b = act.astype(bf16)
            act_scr[l] = act_b
            gp_scr[l] = gp.astype(bf16)
            saved.append((n1, rstd1, h1, q, k, v, mixed, rl, n2, rstd2, h2))
            x = x1 + dot(act_b, wdown[l]) + outb[l, 1:2, :]

        out_b = x.astype(bf16)
        for l in reversed(range(LAYERS)):
            n1, rstd1, h1, q, k, v, mixed, rl, n2, rstd2, h2 = saved[l]
            e2 = g.astype(bf16)
            a_down[l] += dot(e2.T, act_scr[l])
            a_small[l, 7:8, :] += row_sum(e2.astype(f32))
            da = dot_nt(e2, wdown[l])
            du = (da * gp_scr[l].astype(f32)).astype(bf16)
            a_up[l] += dot(h2.T, du)
            dus = row_sum(du.astype(f32))
            for c in range(hidden // width):
                a_small[l, 8 + c:9 + c, :] += dus[:, c * width:(c + 1) * width]
            dh2 = dot_nt(du, wup[l])
            a_small[l, 1:2, :] += row_sum(dh2 * n2)
            a_small[l, 3:4, :] += row_sum(dh2)
            g1 = g + norm_back(dh2, n2, rstd2, gains[l, 1:2, :])
            e1 = g1.astype(bf16)
            a_out[l] += dot(mixed.T, e1)
            a_small[l, 6:7, :] += row_sum(e1.astype(f32))
            dm = dot_nt(e1, wout[l])
            dm1 = dm * rl
            dmo = -(dm1 * mixed.astype(f32))
            dm1 = dm1.astype(bf16)
            dmo = dmo.astype(bf16)
            lhs, dm_t, q_t, v_t, dq, dv_t, dk_t = [], [], [], [], [], [], []
            for b in range(UNIT_BINS):
                rows = slice(b * BIN, (b + 1) * BIN)
                lhs.append(jnp.concatenate([dm1[rows], dmo[rows]], 1))
                dm_t.append(dm1[rows].T)
                q_t.append(q[rows].T)
                v_t.append(v[rows].T)
                dq.append(None)
                dv_t.append([])
                dk_t.append([])
            bins = range(UNIT_BINS)
            rows_of = [slice(b * BIN, (b + 1) * BIN) for b in bins]

            def d_scores(j):
                return [dot(lhs[b], jnp.concatenate([pair_columns(v_t[b], j), mask_columns[j]], 0)) for b in bins]

            ahead = d_scores(0)
            for j in range(pairs):
                top, low = 2 * j * HEAD, (2 * j + 2) * HEAD
                z = ahead
                if j + 1 < pairs:
                    ahead = d_scores(j + 1)
                es = [e_scr[l, rows_of[b], 2 * j * BIN:(2 * j + 2) * BIN] for b in bins]
                for b in bins:
                    pv = dot(dm_t[b][top:low], es[b])
                    dv_t[b] += [pv[:HEAD, :BIN], pv[HEAD:, BIN:]]
                ds = [es[b] * z[b].astype(bf16) for b in bins]
                for b in bins:
                    part = dot(ds[b], pair_rows(k[rows_of[b]], j))
                    dq[b] = part if dq[b] is None else dq[b] + part
                for b in bins:
                    pk = dot(q_t[b][top:low], ds[b])
                    dk_t[b] += [pk[:HEAD, :BIN], pk[HEAD:, BIN:]]
            dqkv_bins = []
            for b in range(UNIT_BINS):
                dv = jnp.concatenate(dv_t[b], 0).T
                dk = jnp.concatenate(dk_t[b], 0).T * LN2
                dqkv_bins.append(jnp.concatenate([(dq[b] * HEAD ** -0.5).astype(bf16), dk.astype(bf16), dv.astype(bf16)], 1))
            dqkv = jnp.concatenate(dqkv_bins, 0)
            a_qkv[l] += dot(h1.T, dqkv)
            sums = row_sum(dqkv.astype(f32))
            a_small[l, 4:5, :] += sums[:, :width]
            a_small[l, 5:6, :] += sums[:, 2 * width:]
            dh = dot_nt(dqkv, wqkv[l])
            a_small[l, 0:1, :] += row_sum(dh * n1)
            a_small[l, 2:3, :] += row_sum(dh)
            g = g1 + norm_back(dh, n1, rstd1, gains[l, 0:1, :])

        grad_b = (g * factor).astype(bf16)
        s_iota = lax.broadcasted_iota(jnp.int32, (slot_rows, BIN), 0)
        p_iota = lax.broadcasted_iota(jnp.int32, (slot_rows, BIN), 1)
        both = jnp.concatenate([out_b, grad_b], 1)
        for b in range(UNIT_BINS):
            for m in range(MEMBERS):
                slot = (u * UNIT_BINS + b) * MEMBERS + m
                t, o, n = mem_traj[slot], mem_off[slot], mem_len[slot]
                pick = jnp.where((p_iota - o == s_iota) & (s_iota < n), 1.0, 0.0).astype(bf16)
                rows = dot(pick, both[b * BIN:(b + 1) * BIN]).astype(bf16)

                home = jnp.where(n > 0, t, trajs)
                out[home] = rows[:, :width]
                gtok[home] = rows[:, width:]
        return carry

    lax.fori_loop(0, units, body, 0)

    stores = [
        pltpu.make_async_copy(out.at[pl.ds(0, trajs)], out_hbm, sems.at[0]),
        pltpu.make_async_copy(gtok.at[pl.ds(0, trajs)], gtok_hbm, sems.at[1]),
    ]
    for copy in stores:
        copy.start()
    for l in range(LAYERS):
        at = 0
        for c in range(3):
            gsum[l, at:at + width, :] = a_qkv[l, :, c * width:(c + 1) * width].astype(bf16)
            at += width
        gsum[l, at:at + width, :] = a_out[l].astype(bf16)
        at += width
        for c in range(hidden // width):
            gsum[l, at:at + width, :] = a_up[l, :, c * width:(c + 1) * width].astype(bf16)
            at += width
        for c in range(hidden // width):
            gsum[l, at:at + width, :] = a_down[l, :, c * width:(c + 1) * width].T.astype(bf16)
            at += width
        gsum[l, at:at + SMALL, :] = a_small[l].astype(bf16)
    mine = parity[0]
    stores += [
        pltpu.make_async_copy(gsum.at[mine], mine_hbm, sems.at[2]),
        pltpu.make_async_copy(gsum.at[1 - mine], other_hbm, sems.at[3]),
    ]
    for copy in stores[2:]:
        copy.start()
    for copy in stores:
        copy.wait()


def main_call(args, steps_top, parity):
    tokens, lengths, gains, shifts, wqkv, qvb, wout, outb, wup, upb, wdown, cot = args
    trajs, slot_rows, width = tokens.shape
    hidden = wup.shape[2]
    unit = BIN * UNIT_BINS
    slots = 2 * (trajs + UNIT_BINS)
    per_layer = 4 * width + 2 * hidden + SMALL
    vm = pl.BlockSpec(memory_space=pltpu.VMEM)
    sm = pl.BlockSpec(memory_space=pltpu.SMEM)
    hbm = pl.BlockSpec(memory_space=pl.ANY)
    sums = jax.ShapeDtypeStruct((per_layer, width), bf16)
    return pl.pallas_call(
        functools.partial(main_kernel, steps_top=steps_top),
        out_shape=(
            jax.ShapeDtypeStruct(tokens.shape, bf16),
            jax.ShapeDtypeStruct(tokens.shape, bf16),
            sums,
            sums,
        ),
        in_specs=[sm, sm, hbm, hbm] + [vm] * 9,
        out_specs=(hbm, hbm, hbm, hbm),
        scratch_shapes=[
            pltpu.VMEM(tokens.shape, bf16),
            pltpu.VMEM(tokens.shape, bf16),
            pltpu.VMEM((trajs + 1, slot_rows, width), bf16),
            pltpu.VMEM((trajs + 1, slot_rows, width), bf16),
            pltpu.VMEM((LAYERS, per_layer, width), bf16),
            pltpu.VMEM((LAYERS, width, 3 * width), f32),
            pltpu.VMEM((LAYERS, width, width), f32),
            pltpu.VMEM((LAYERS, width, hidden), f32),
            pltpu.VMEM((LAYERS, width, hidden), f32),
            pltpu.VMEM((LAYERS, SMALL, width), f32),
            pltpu.VMEM((LAYERS, unit, width // HEAD * BIN), bf16),
            pltpu.VMEM((LAYERS, unit, hidden), bf16),
            pltpu.VMEM((LAYERS, unit, hidden), bf16),
            pltpu.SMEM((trajs,), jnp.int32),
            pltpu.SMEM((steps_top + 1,), jnp.int32),
            pltpu.SMEM((slots,), jnp.int32),
            pltpu.SMEM((slots,), jnp.int32),
            pltpu.SMEM((slots,), jnp.int32),
            pltpu.SemaphoreType.DMA((4,)),
        ],
        compiler_params=pltpu.CompilerParams(vmem_limit_bytes=56 * 1024 * 1024),
        name="layers",
    )(lengths, parity, tokens, cot, gains, shifts, wqkv, qvb, wout, outb, wup, upb, wdown)


AXES = ("dp", "group")


def finish_kernel(parity, mine, other, gains, shifts, qkv, qvb, out, outb, up, upb, down):
    width = mine.shape[1]
    hidden = up.shape[2]
    for p in range(LAYERS):

        @pl.when(parity[0] == p)
        def _():
            for l in range(LAYERS):
                src = mine if l == p else other
                at = 0
                for c in range(3):
                    qkv[l, :, c * width:(c + 1) * width] = src[at:at + width, :].astype(f32)
                    at += width
                out[l] = src[at:at + width, :].astype(f32)
                at += width
                for c in range(hidden // width):
                    up[l, :, c * width:(c + 1) * width] = src[at:at + width, :].astype(f32)
                    at += width
                down[l] = src[at:at + hidden, :].astype(f32)
                at += hidden
                small = src[at:at + SMALL, :].astype(f32)
                gains[l] = small[0:2]
                shifts[l] = small[2:4]
                qvb[l] = small[4:6]
                outb[l] = small[6:8]
                for c in range(hidden // width):
                    upb[l:l + 1, c * width:(c + 1) * width] = small[8 + c:9 + c]


def finish_call(parity, mine, other, args):
    vm = pl.BlockSpec(memory_space=pltpu.VMEM)
    sm = pl.BlockSpec(memory_space=pltpu.SMEM)
    return pl.pallas_call(
        finish_kernel,
        out_shape=tuple(jax.ShapeDtypeStruct(a.shape, f32) for a in args[2:11]),
        in_specs=[sm, vm, vm],
        out_specs=(vm,) * 9,
        compiler_params=pltpu.CompilerParams(vmem_limit_bytes=16 * 1024 * 1024),
        name="finish",
    )(parity, mine, other)


def exchange(x, bits, devices):
    return lax.ppermute(x, AXES, [(i, i ^ bits[i % 2]) for i in range(devices)])


def added(a, b):
    return (a.astype(f32) + b.astype(f32)).astype(bf16)


def all_sum(mine, other, index, devices):
    x = added(mine, exchange(other, (1, 1), devices))
    bits = [1 << i for i in range(1, devices.bit_length() - 1)]
    crossed = list(bits)
    for i in range(0, len(bits) - 1, 2):
        crossed[i], crossed[i + 1] = bits[i + 1], bits[i]
    steps = list(zip(bits, crossed))
    turn = len(steps) // 2
    orders = [steps, steps[turn:] + steps[:turn]]
    size = x.shape[0] // len(orders)
    parts = [x[i * size:(i + 1) * size] for i in range(len(orders))]
    lows = [(index // jnp.where(index % 2 == 0, order[0][0], order[0][1])) % 2 == 0 for order in orders]
    half = size // 2
    kept = [jnp.where(low, p[:half], p[half:]) for p, low in zip(parts, lows)]
    sent = [jnp.where(low, p[half:], p[:half]) for p, low in zip(parts, lows)]
    for step in range(len(steps)):
        got = [exchange(p, order[step], devices) for p, order in zip(sent, orders)]
        kept = [added(p, q) for p, q in zip(kept, got)]
        sent = kept
    got = [exchange(p, order[0], devices) for p, order in zip(kept, orders)]
    parts = [
        jnp.where(low, jnp.concatenate([p, q]), jnp.concatenate([q, p]))
        for p, q, low in zip(kept, got, lows)
    ]
    x = jnp.concatenate(parts)
    return x, exchange(x, (1, 1), devices)


def solution(mesh):
    mesh_shape = dict(mesh.shape)
    devices = mesh_shape["dp"] * mesh_shape["group"]

    def per_device(*args):
        index = lax.axis_index("dp") * mesh_shape["group"] + lax.axis_index("group")
        parity = (index % 2).astype(jnp.int32).reshape(1)
        output, grad_tokens, mine, other = main_call(args, STEPS, parity)
        mine, other = all_sum(mine, other, index, devices)
        return (output, grad_tokens) + tuple(finish_call(parity, mine, other, args))

    rows = P(AXES, None, None)
    return jax.shard_map(
        per_device,
        mesh=mesh,
        in_specs=(rows, P(AXES)) + (P(),) * 9 + (rows,),
        out_specs=(rows, rows) + (P(),) * 9,
        check_vma=False,
    )
```

time: 127 us -> 75.5 us (0.59)
  Pallas kernels: 71.2 us -> 37.5 us
  waiting for transfers between devices: 29.9 us -> 17.6 us
  local copies, waits for them, and re-layouts: 2.79 us -> 0 us
  other arithmetic: 3.72 us -> 1.55 us
    pallas_call x1, Pallas kernels: 71.2 us -> 36.2 us  [main_call(): pl.pallas_call(functools.partial(main_kernel, steps_top=steps_top), out_s...]
    ppermute x8 -> x12, waiting for transfers between devices: 29.9 us -> 17.6 us  [exchange(): return lax.ppermute(x, AXES, [(i, i ^ bits[i % 2]) for i in range(devices)])]
    slice x3 -> x0, local copies, waits for them, and re-layouts: 2.19 us -> none  [the longest x1 0.83 us: per_device(): total[:, down_at:down_at + hidden]]
    concatenate x2 -> x1, other arithmetic: 1.6 us -> 0.03 us  [all_sum(): x = jnp.concatenate(parts)]
    select_n x6 -> x3, other arithmetic: 1.66 us -> 0.14 us  [the longest x2 0.12 us: all_sum(): jnp.where(low, jnp.concatenate([p, q]), jnp.concatenate([q, p]))]
    pallas_call x0 -> x1, Pallas kernels: none -> 1.29 us  [finish_call(): pl.pallas_call(finish_kernel, out_shape=tuple((jax.ShapeDtypeStruct(a.sha...]
    ppermute x8 -> x12, starting transfers between devices: 18.4 us -> 17.9 us  [exchange(): return lax.ppermute(x, AXES, [(i, i ^ bits[i % 2]) for i in range(devices)])]
  transfers between devices with their start and end apart: 8 -> 12, of which waited for: 8 -> 10; matrix products, arithmetic and copies ran while one was open for 0% -> 0% of each run, Pallas kernels for 0% -> 0%
where the time goes in v2:
time: 75.5 us; the launch traced here: 75.3 us
  Pallas kernels  37.5 us (50%)
  starting transfers between devices  17.9 us (24%)
  waiting for transfers between devices  17.6 us (23%)
  other arithmetic  1.55 us (2%)
    pallas_call x1, Pallas kernels, main_call(): pl.pallas_call(functools.partial(main_kernel, steps_top=steps_top), out_s...  36.2 us
    ppermute x12, starting transfers between devices, exchange(): return lax.ppermute(x, AXES, [(i, i ^ bits[i % 2]) for i in range(devices)])  17.9 us
    ppermute x12, waiting for transfers between devices, exchange(): return lax.ppermute(x, AXES, [(i, i ^ bits[i % 2]) for i in range(devices)])  17.6 us
  transfers between devices with their start and end apart: 12, of which 10 were waited for; matrix products, arithmetic and copies ran while one was open for 0% of the time, Pallas kernels for 0%

profile of v2, /device:TPU:0, one launch (start us, length us, event | category | flops | bytes accessed | tf_op | source)
XLA Modules:
  0.0 75.3 jit_solution(1501377374904891399)
XLA Ops:
  0.7 36.2 %layers.1 = (bf16[32,96,128]{2,1,0:T(8,128)(2,1)}, bf16[32,96,128]{2,1,0:T(8,128)(2,1)}, bf16[1600,128]{1,0:T(8,128)(2,1)}, bf16[1600,128]{1,0:T(8,128)(2,1)}) custom-call(s32[32]{0:T(128)} %lengths.1, s32[1]{0:T(128)} %bitcast.parity, bf16[32,96,128]{2,1,0:T(8,128)(2,1)} %tok_hbm.1, bf16[32,96,128]{2,1,0:T(8,128)(2,1)} %cot_hbm.1, f32[2,2,128]{2,1,0:T(2,128)} %gains.1, ...), custom_call_target="tpu_custom_call" | custom-call | tf_op jit(solution)/shard_map/layers/pallas_call | solution.py:375
  36.9 0.5 collective-permute-start
  37.4 1.6 %collective-permute-done = bf16[1600,128]{1,0:T(8,128)(2,1)S(1)} collective-permute-done((bf16[1600,128]{1,0:T(8,128)(2,1)}, bf16[1600,128]{1,0:T(8,128)(2,1)S(1)}, u32[]{:S(2)}, u32[]{:S(2)}) %collective-permute-start) | collective-permute-done | bytes 409632 | tf_op jit(solution)/shard_map/ppermute | solution.py:457
  39.0 1.1 %add_convert_fusion = bf16[1600,128]{1,0:T(8,128)(2,1)S(1)} fusion(bf16[1600,128]{1,0:T(8,128)(2,1)S(1)} %collective-permute-done, bf16[1600,128]{1,0:T(8,128)(2,1)} %get-tuple-element.26), kind=kLoop, calls=%fused_computation | loop fusion | flops 819200 | bytes 1228800 | tf_op jit(solution)/shard_map/convert_element_type | solution.py:461
  40.1 3.0 %collective-permute-start.1 = (bf16[400,128]{1,0:T(8,128)(2,1)S(1)}, bf16[400,128]{1,0:T(8,128)(2,1)S(1)}, u32[]{:S(2)}, u32[]{:S(2)}) collective-permute-start(bf16[400,128]{1,0:T(8,128)(2,1)S(1)} %get-tuple-element.39), channel_id=1, source_target_pairs={{0,2},{1,5},{2,0},{3,7},{4,6},{5,1},{6,4},{7,3},{8,10},{9,13},{10,... | collective-permute-start | bytes 307208 | tf_op jit(solution)/shard_map/ppermute | solution.py:457
  43.1 1.6 %collective-permute-start.6 = (bf16[400,128]{1,0:T(8,128)(2,1)S(1)}, bf16[400,128]{1,0:T(8,128)(2,1)S(1)}, u32[]{:S(2)}, u32[]{:S(2)}) collective-permute-start(bf16[400,128]{1,0:T(8,128)(2,1)S(1)} %get-tuple-element.40), channel_id=1, source_target_pairs={{0,8},{1,17},{2,10},{3,19},{4,12},{5,21},{6,14},{7,23},{8,0},{9,25... | collective-permute-start | bytes 307208 | tf_op jit(solution)/shard_map/ppermute | solution.py:457
  44.6 1.1 %collective-permute-done.1 = bf16[400,128]{1,0:T(8,128)(2,1)S(1)} collective-permute-done((bf16[400,128]{1,0:T(8,128)(2,1)S(1)}, bf16[400,128]{1,0:T(8,128)(2,1)S(1)}, u32[]{:S(2)}, u32[]{:S(2)}) %collective-permute-start.1) | collective-permute-done | bytes 102432 | tf_op jit(solution)/shard_map/ppermute | solution.py:457
  45.7 2.9 %collective-permute-done.6 = bf16[400,128]{1,0:T(8,128)(2,1)S(1)} collective-permute-done((bf16[400,128]{1,0:T(8,128)(2,1)S(1)}, bf16[400,128]{1,0:T(8,128)(2,1)S(1)}, u32[]{:S(2)}, u32[]{:S(2)}) %collective-permute-start.6) | collective-permute-done | bytes 102432 | tf_op jit(solution)/shard_map/ppermute | solution.py:457
  48.6 0.1 add_convert_fusion.8
  48.7 0.7 collective-permute-start.2
  49.4 2.6 %collective-permute-start.7 = (bf16[400,128]{1,0:T(8,128)(2,1)S(1)}, bf16[400,128]{1,0:T(8,128)(2,1)S(1)}, u32[]{:S(2)}, u32[]{:S(2)}) collective-permute-start(bf16[400,128]{1,0:T(8,128)(2,1)S(1)} %get-tuple-element.38), channel_id=1, source_target_pairs={{0,16},{1,9},{2,18},{3,11},{4,20},{5,13},{6,22},{7,15},{8,24},{9,1... | collective-permute-start | bytes 307208 | tf_op jit(solution)/shard_map/ppermute | solution.py:457
  52.0 1.4 %collective-permute-done.2 = bf16[400,128]{1,0:T(8,128)(2,1)S(1)} collective-permute-done((bf16[400,128]{1,0:T(8,128)(2,1)S(1)}, bf16[400,128]{1,0:T(8,128)(2,1)S(1)}, u32[]{:S(2)}, u32[]{:S(2)}) %collective-permute-start.2) | collective-permute-done | bytes 102432 | tf_op jit(solution)/shard_map/ppermute | solution.py:457
  53.4 1.7 %collective-permute-start.3 = (bf16[400,128]{1,0:T(8,128)(2,1)S(1)}, bf16[400,128]{1,0:T(8,128)(2,1)S(1)}, u32[]{:S(2)}, u32[]{:S(2)}) collective-permute-start(bf16[400,128]{1,0:T(8,128)(2,1)S(1)} %add_convert_fusion.7), channel_id=1, source_target_pairs={{0,8},{1,17},{2,10},{3,19},{4,12},{5,21},{6,14},{7,23},{8,0},{9,25... | collective-permute-start | bytes 307208 | tf_op jit(solution)/shard_map/ppermute | solution.py:457
  55.2 0.0 collective-permute-done.7
  55.2 1.2 %collective-permute-start.8 = (bf16[400,128]{1,0:T(8,128)(2,1)S(1)}, bf16[400,128]{1,0:T(8,128)(2,1)S(1)}, u32[]{:S(2)}, u32[]{:S(2)}) collective-permute-start(bf16[400,128]{1,0:T(8,128)(2,1)S(1)} %add_convert_fusion.3), channel_id=1, source_target_pairs={{0,2},{1,5},{2,0},{3,7},{4,6},{5,1},{6,4},{7,3},{8,10},{9,13},{10,... | collective-permute-start | bytes 307208 | tf_op jit(solution)/shard_map/ppermute | solution.py:457
  56.5 2.7 %collective-permute-done.3 = bf16[400,128]{1,0:T(8,128)(2,1)S(1)} collective-permute-done((bf16[400,128]{1,0:T(8,128)(2,1)S(1)}, bf16[400,128]{1,0:T(8,128)(2,1)S(1)}, u32[]{:S(2)}, u32[]{:S(2)}) %collective-permute-start.3) | collective-permute-done | bytes 102432 | tf_op jit(solution)/shard_map/ppermute | solution.py:457
  59.2 1.8 %collective-permute-start.4 = (bf16[400,128]{1,0:T(8,128)(2,1)S(1)}, bf16[400,128]{1,0:T(8,128)(2,1)S(1)}, u32[]{:S(2)}, u32[]{:S(2)}) collective-permute-start(bf16[400,128]{1,0:T(8,128)(2,1)S(1)} %add_convert_fusion.6), channel_id=1, source_target_pairs={{0,16},{1,9},{2,18},{3,11},{4,20},{5,13},{6,22},{7,15},{8,24},{9,1... | collective-permute-start | bytes 307208 | tf_op jit(solution)/shard_map/ppermute | solution.py:457
  61.0 0.0 collective-permute-done.8
  61.0 3.6 %collective-permute-start.9 = (bf16[400,128]{1,0:T(8,128)(2,1)S(1)}, bf16[400,128]{1,0:T(8,128)(2,1)S(1)}, u32[]{:S(2)}, u32[]{:S(2)}) collective-permute-start(bf16[400,128]{1,0:T(8,128)(2,1)S(1)} %add_convert_fusion.2), channel_id=1, source_target_pairs={{0,4},{1,3},{2,6},{3,1},{4,0},{5,7},{6,2},{7,5},{8,12},{9,11},{10,... | collective-permute-start | bytes 307208 | tf_op jit(solution)/shard_map/ppermute | solution.py:457
  64.7 1.2 %collective-permute-done.4 = bf16[400,128]{1,0:T(8,128)(2,1)S(1)} collective-permute-done((bf16[400,128]{1,0:T(8,128)(2,1)S(1)}, bf16[400,128]{1,0:T(8,128)(2,1)S(1)}, u32[]{:S(2)}, u32[]{:S(2)}) %collective-permute-start.4) | collective-permute-done | bytes 102432 | tf_op jit(solution)/shard_map/ppermute | solution.py:457
  65.9 0.1 collective-permute-start.5
  66.0 1.3 %collective-permute-done.9 = bf16[400,128]{1,0:T(8,128)(2,1)S(1)} collective-permute-done((bf16[400,128]{1,0:T(8,128)(2,1)S(1)}, bf16[400,128]{1,0:T(8,128)(2,1)S(1)}, u32[]{:S(2)}, u32[]{:S(2)}) %collective-permute-start.9) | collective-permute-done | bytes 102432 | tf_op jit(solution)/shard_map/ppermute | solution.py:457
  67.3 1.0 %collective-permute-start.10 = (bf16[400,128]{1,0:T(8,128)(2,1)S(1)}, bf16[400,128]{1,0:T(8,128)(2,1)S(1)}, u32[]{:S(2)}, u32[]{:S(2)}) collective-permute-start(bf16[400,128]{1,0:T(8,128)(2,1)S(1)} %add_convert_fusion.1), channel_id=1, source_target_pairs={{0,8},{1,17},{2,10},{3,19},{4,12},{5,21},{6,14},{7,23},{8,0},{9,25... | collective-permute-start | bytes 307208 | tf_op jit(solution)/shard_map/ppermute | solution.py:457
  68.3 2.3 %collective-permute-done.5 = bf16[400,128]{1,0:T(8,128)(2,1)S(1)} collective-permute-done((bf16[400,128]{1,0:T(8,128)(2,1)S(1)}, bf16[400,128]{1,0:T(8,128)(2,1)S(1)}, u32[]{:S(2)}, u32[]{:S(2)}) %collective-permute-start.5) | collective-permute-done | bytes 102432 | tf_op jit(solution)/shard_map/ppermute | solution.py:457
  70.7 0.1 maximum_select_fusion
  70.7 1.3 %collective-permute-done.10 = bf16[400,128]{1,0:T(8,128)(2,1)S(1)} collective-permute-done((bf16[400,128]{1,0:T(8,128)(2,1)S(1)}, bf16[400,128]{1,0:T(8,128)(2,1)S(1)}, u32[]{:S(2)}, u32[]{:S(2)}) %collective-permute-start.10) | collective-permute-done | bytes 102432 | tf_op jit(solution)/shard_map/ppermute | solution.py:457
  72.1 0.1 maximum_select_fusion.1
  72.2 0.1 collective-permute-start.11
  72.2 1.7 %collective-permute-done.11.other = bf16[1600,128]{1,0:T(8,128)(2,1)S(1)} collective-permute-done((bf16[1600,128]{1,0:T(8,128)(2,1)S(1)}, bf16[1600,128]{1,0:T(8,128)(2,1)S(1)}, u32[]{:S(2)}, u32[]{:S(2)}) %collective-permute-start.11) | collective-permute-done | bytes 409632 | tf_op jit(solution)/shard_map/ppermute | solution.py:457
  74.0 1.3 %finish.1 = (f32[2,2,128]{2,1,0:T(2,128)}, f32[2,2,128]{2,1,0:T(2,128)}, f32[2,128,384]{2,1,0:T(8,128)}, f32[2,2,128]{2,1,0:T(2,128)}, f32[2,128,128]{2,1,0:T(8,...) custom-call(s32[1]{0:T(128)} %bitcast.parity, ...), custom_call_target="tpu_custom_call" | custom-call | tf_op jit(solution)/shard_map/finish/pallas_call | solution.py:446
  (8 shorter events, 0.2 us)
Async XLA Ops:
  36.9 2.1 %collective-permute-start = (bf16[1600,128]{1,0:T(8,128)(2,1)}, bf16[1600,128]{1,0:T(8,128)(2,1)S(1)}, u32[]{:S(2)}, u32[]{:S(2)}) collective-permute-start(bf16[1600,128]{1,0:T(8,128)(2,1)} %get-tuple-element.27), channel_id=1, source_target_pairs={{0,1},{1,0},{2,3},{3,2},{4,5},{5,4},{6,7},{7,6},{8,9},{9,8},{10,11... | collective-permute-start | bytes 1228808 | tf_op jit(solution)/shard_map/ppermute | solution.py:457
  40.1 5.6 %collective-permute-start.1 = (bf16[400,128]{1,0:T(8,128)(2,1)S(1)}, bf16[400,128]{1,0:T(8,128)(2,1)S(1)}, u32[]{:S(2)}, u32[]{:S(2)}) collective-permute-start(bf16[400,128]{1,0:T(8,128)(2,1)S(1)} %get-tuple-element.39), channel_id=1, source_target_pairs={{0,2},{1,5},{2,0},{3,7},{4,6},{5,1},{6,4},{7,3},{8,10},{9,13},{10,... | collective-permute-start | bytes 307208 | tf_op jit(solution)/shard_map/ppermute | solution.py:457
  43.1 5.5 %collective-permute-start.6 = (bf16[400,128]{1,0:T(8,128)(2,1)S(1)}, bf16[400,128]{1,0:T(8,128)(2,1)S(1)}, u32[]{:S(2)}, u32[]{:S(2)}) collective-permute-start(bf16[400,128]{1,0:T(8,128)(2,1)S(1)} %get-tuple-element.40), channel_id=1, source_target_pairs={{0,8},{1,17},{2,10},{3,19},{4,12},{5,21},{6,14},{7,23},{8,0},{9,25... | collective-permute-start | bytes 307208 | tf_op jit(solution)/shard_map/ppermute | solution.py:457
  48.7 4.7 %collective-permute-start.2 = (bf16[400,128]{1,0:T(8,128)(2,1)S(1)}, bf16[400,128]{1,0:T(8,128)(2,1)S(1)}, u32[]{:S(2)}, u32[]{:S(2)}) collective-permute-start(bf16[400,128]{1,0:T(8,128)(2,1)S(1)} %get-tuple-element.37), channel_id=1, source_target_pairs={{0,4},{1,3},{2,6},{3,1},{4,0},{5,7},{6,2},{7,5},{8,12},{9,11},{10,... | collective-permute-start | bytes 307208 | tf_op jit(solution)/shard_map/ppermute | solution.py:457
  49.4 5.8 %collective-permute-start.7 = (bf16[400,128]{1,0:T(8,128)(2,1)S(1)}, bf16[400,128]{1,0:T(8,128)(2,1)S(1)}, u32[]{:S(2)}, u32[]{:S(2)}) collective-permute-start(bf16[400,128]{1,0:T(8,128)(2,1)S(1)} %get-tuple-element.38), channel_id=1, source_target_pairs={{0,16},{1,9},{2,18},{3,11},{4,20},{5,13},{6,22},{7,15},{8,24},{9,1... | collective-permute-start | bytes 307208 | tf_op jit(solution)/shard_map/ppermute | solution.py:457
  53.4 5.7 %collective-permute-start.3 = (bf16[400,128]{1,0:T(8,128)(2,1)S(1)}, bf16[400,128]{1,0:T(8,128)(2,1)S(1)}, u32[]{:S(2)}, u32[]{:S(2)}) collective-permute-start(bf16[400,128]{1,0:T(8,128)(2,1)S(1)} %add_convert_fusion.7), channel_id=1, source_target_pairs={{0,8},{1,17},{2,10},{3,19},{4,12},{5,21},{6,14},{7,23},{8,0},{9,25... | collective-permute-start | bytes 307208 | tf_op jit(solution)/shard_map/ppermute | solution.py:457
  55.2 5.8 %collective-permute-start.8 = (bf16[400,128]{1,0:T(8,128)(2,1)S(1)}, bf16[400,128]{1,0:T(8,128)(2,1)S(1)}, u32[]{:S(2)}, u32[]{:S(2)}) collective-permute-start(bf16[400,128]{1,0:T(8,128)(2,1)S(1)} %add_convert_fusion.3), channel_id=1, source_target_pairs={{0,2},{1,5},{2,0},{3,7},{4,6},{5,1},{6,4},{7,3},{8,10},{9,13},{10,... | collective-permute-start | bytes 307208 | tf_op jit(solution)/shard_map/ppermute | solution.py:457
  59.2 6.7 %collective-permute-start.4 = (bf16[400,128]{1,0:T(8,128)(2,1)S(1)}, bf16[400,128]{1,0:T(8,128)(2,1)S(1)}, u32[]{:S(2)}, u32[]{:S(2)}) collective-permute-start(bf16[400,128]{1,0:T(8,128)(2,1)S(1)} %add_convert_fusion.6), channel_id=1, source_target_pairs={{0,16},{1,9},{2,18},{3,11},{4,20},{5,13},{6,22},{7,15},{8,24},{9,1... | collective-permute-start | bytes 307208 | tf_op jit(solution)/shard_map/ppermute | solution.py:457
  61.0 6.3 %collective-permute-start.9 = (bf16[400,128]{1,0:T(8,128)(2,1)S(1)}, bf16[400,128]{1,0:T(8,128)(2,1)S(1)}, u32[]{:S(2)}, u32[]{:S(2)}) collective-permute-start(bf16[400,128]{1,0:T(8,128)(2,1)S(1)} %add_convert_fusion.2), channel_id=1, source_target_pairs={{0,4},{1,3},{2,6},{3,1},{4,0},{5,7},{6,2},{7,5},{8,12},{9,11},{10,... | collective-permute-start | bytes 307208 | tf_op jit(solution)/shard_map/ppermute | solution.py:457
  65.9 4.7 %collective-permute-start.5 = (bf16[400,128]{1,0:T(8,128)(2,1)S(1)}, bf16[400,128]{1,0:T(8,128)(2,1)S(1)}, u32[]{:S(2)}, u32[]{:S(2)}) collective-permute-start(bf16[400,128]{1,0:T(8,128)(2,1)S(1)} %add_convert_fusion.5), channel_id=1, source_target_pairs={{0,2},{1,5},{2,0},{3,7},{4,6},{5,1},{6,4},{7,3},{8,10},{9,13},{10,... | collective-permute-start | bytes 307208 | tf_op jit(solution)/shard_map/ppermute | solution.py:457
  67.3 4.7 %collective-permute-start.10 = (bf16[400,128]{1,0:T(8,128)(2,1)S(1)}, bf16[400,128]{1,0:T(8,128)(2,1)S(1)}, u32[]{:S(2)}, u32[]{:S(2)}) collective-permute-start(bf16[400,128]{1,0:T(8,128)(2,1)S(1)} %add_convert_fusion.1), channel_id=1, source_target_pairs={{0,8},{1,17},{2,10},{3,19},{4,12},{5,21},{6,14},{7,23},{8,0},{9,25... | collective-permute-start | bytes 307208 | tf_op jit(solution)/shard_map/ppermute | solution.py:457
  72.2 1.8 %collective-permute-start.11 = (bf16[1600,128]{1,0:T(8,128)(2,1)S(1)}, bf16[1600,128]{1,0:T(8,128)(2,1)S(1)}, u32[]{:S(2)}, u32[]{:S(2)}) collective-permute-start(bf16[1600,128]{1,0:T(8,128)(2,1)S(1)} %pad_maximum_fusion.mine), channel_id=1, source_target_pairs={{0,1},{1,0},{2,3},{3,2},{4,5},{5,4},{6,7},{7,6},{8,9},{9,8},{10,11... | collective-permute-start | bytes 1228808 | tf_op jit(solution)/shard_map/ppermute | solution.py:457

commit v3 on v2

--- a/solution.py
+++ b/solution.py
@@ -11,6 +11,8 @@
 LAYERS = 2
 BIN = 128
 SMALL = 64
+FWD_GROUP = 1
+BWD_GROUP = 4
 MEMBERS = 2
 UNIT_BINS = 8
 eps = 1e-05
@@ -112,9 +114,9 @@
 
 
 def main_kernel(
-    lengths, parity, tok_hbm, cot_hbm, gains, shifts, wqkv, qvb, wout, outb, wup, upb, wdown,
-    out_hbm, gtok_hbm, mine_hbm, other_hbm,
-    tok, cot, out, gtok, gsum,
+    lengths, parity, tok_hbm, cot_hbm, gains_hbm, shifts_hbm, wqkv_hbm, qvb_hbm, wout_hbm, outb_hbm, wup_hbm, upb_hbm, wdown_hbm,
+    out_hbm, gtok_hbm, mine_a, mine_b, other_a, other_b,
+    tok, cot, gains, shifts, wqkv, qvb, wout, outb, wup, upb, wdown, out, gtok, gsum,
     a_qkv, a_out, a_up, a_down, a_small, e_scr, act_scr, gp_scr,
     order, count, mem_traj, mem_off, mem_len, sems,
     *, steps_top,
@@ -124,7 +126,9 @@
     heads = width // HEAD
     pairs = heads // 2
     unit = BIN * UNIT_BINS
-    loads = [pltpu.make_async_copy(tok_hbm, tok, sems.at[0]), pltpu.make_async_copy(cot_hbm, cot, sems.at[1])]
+    sources = (tok_hbm, cot_hbm, gains_hbm, shifts_hbm, wqkv_hbm, qvb_hbm, wout_hbm, outb_hbm, wup_hbm, upb_hbm, wdown_hbm)
+    targets = (tok, cot, gains, shifts, wqkv, qvb, wout, outb, wup, upb, wdown)
+    loads = [pltpu.make_async_copy(a, b, sems.at[i]) for i, (a, b) in enumerate(zip(sources, targets))]
     for copy in loads:
         copy.start()
     for ref in (a_qkv, a_out, a_up, a_down, a_small):
@@ -161,22 +165,19 @@
     mask_columns = [pair_columns(ones_t, j) for j in range(pairs)]
 
     def body(u, carry):
-        r_iota = lax.broadcasted_iota(jnp.int32, (BIN, slot_rows), 0)
-        c_iota = lax.broadcasted_iota(jnp.int32, (BIN, slot_rows), 1)
         q_iota = lax.broadcasted_iota(jnp.int32, (BIN, BIN), 0)
         k_iota = lax.broadcasted_iota(jnp.int32, (BIN, BIN), 1)
         toks, cots, biases = [], [], []
         for b in range(UNIT_BINS):
-            x = None
+            picks, rows_in = [], []
             start = jnp.zeros((BIN, BIN), jnp.int32)
             for m in range(MEMBERS):
                 slot = (u * UNIT_BINS + b) * MEMBERS + m
                 t, o, n = mem_traj[slot], mem_off[slot], mem_len[slot]
-                pick = jnp.where((r_iota - o == c_iota) & (c_iota < n), 1.0, 0.0).astype(bf16)
-                both = jnp.concatenate([tok[t], cot[t]], axis=1)
-                part = dot(pick, both)
-                x = part if x is None else x + part
+                picks.append(jnp.where((q_iota - o == k_iota) & (k_iota < n), 1.0, 0.0).astype(bf16))
+                rows_in += [jnp.concatenate([tok[t], cot[t]], axis=1), jnp.zeros((BIN - slot_rows, 2 * width), bf16)]
                 start = jnp.where(q_iota >= o + n, o + n, start)
+            x = dot(jnp.concatenate(picks, 1), jnp.concatenate(rows_in, 0))
             toks.append(x[:, :width])
             cots.append(x[:, width:])
             biases.append(jnp.where((k_iota <= q_iota) & (k_iota >= start), 0.0, dead_score))
@@ -194,36 +195,35 @@
             q = ((joint[:, :width] + qvb[l, 0:1, :]) * (LOG2E * HEAD ** -0.5)).astype(bf16)
             k = joint[:, width:2 * width].astype(bf16)
             v = (joint[:, 2 * width:] + qvb[l, 1:2, :]).astype(bf16)
-            bins = range(UNIT_BINS)
-            rows_of = [slice(b * BIN, (b + 1) * BIN) for b in bins]
-            acc = [None] * UNIT_BINS
-
-            def scores(j):
-                return [dot_nt(q[rows_of[b]], pair_rows(k[rows_of[b]], j)) for b in bins]
-
-            ahead = scores(0)
-            for j in range(pairs):
-                s = ahead
-                if j + 1 < pairs:
-                    ahead = scores(j + 1)
-                es = []
+            rows_of = [slice(b * BIN, (b + 1) * BIN) for b in range(UNIT_BINS)]
+            mixed_bins, rl_bins = [], []
+            for first in range(0, UNIT_BINS, FWD_GROUP):
+                bins = range(first, first + FWD_GROUP)
+                acc = {b: None for b in bins}
+
+                def scores(j):
+                    return {b: dot_nt(q[rows_of[b]], pair_rows(k[rows_of[b]], j)) for b in bins}
+
+                ahead = scores(0)
+                for j in range(pairs):
+                    s = ahead
+                    if j + 1 < pairs:
+                        ahead = scores(j + 1)
+                    es = {}
+                    for b in bins:
+                        halves = []
+                        for half in range(2):
+                            sh = s[b][:, half * BIN:(half + 1) * BIN] + biases[b]
+                            halves.append(jnp.exp2(sh - jnp.max(sh, -1, keepdims=True)).astype(bf16))
+                        es[b] = jnp.concatenate(halves, 1)
+                        e_scr[l, rows_of[b], 2 * j * BIN:(2 * j + 2) * BIN] = es[b]
+                    for b in bins:
+                        part = dot(es[b], jnp.concatenate([pair_rows(v[rows_of[b]], j), mask_pairs[j]], 1))
+                        acc[b] = part if acc[b] is None else acc[b] + part
                 for b in bins:
-                    halves = []
-                    for half in range(2):
-                        sh = s[b][:, half * BIN:(half + 1) * BIN] + biases[b]
-                        halves.append(jnp.exp2(sh - jnp.max(sh, -1, keepdims=True)).astype(bf16))
-                    e = jnp.concatenate(halves, 1)
-                    e_scr[l, rows_of[b], 2 * j * BIN:(2 * j + 2) * BIN] = e
-                    es.append(e)
-                for b in bins:
-                    r = jnp.concatenate([pair_rows(v[rows_of[b]], j), mask_pairs[j]], 1)
-                    part = dot(es[b], r)
-                    acc[b] = part if acc[b] is None else acc[b] + part
-            mixed_bins, rl_bins = [], []
-            for b in bins:
-                rl = 1.0 / acc[b][:, width:]
-                mixed_bins.append((acc[b][:, :width] * rl).astype(bf16))
-                rl_bins.append(rl)
+                    rl = 1.0 / acc[b][:, width:]
+                    mixed_bins.append((acc[b][:, :width] * rl).astype(bf16))
+                    rl_bins.append(rl)
             mixed = jnp.concatenate(mixed_bins, 0)
             rl = jnp.concatenate(rl_bins, 0)
             x1 = x + dot(mixed, wout[l]) + outb[l, 0:1, :]
@@ -244,70 +244,67 @@
         for l in reversed(range(LAYERS)):
             n1, rstd1, h1, q, k, v, mixed, rl, n2, rstd2, h2 = saved[l]
             e2 = g.astype(bf16)
+            a_small[l, 7:8, :] += row_sum(e2.astype(f32))
+            du = (dot_nt(e2, wdown[l]) * gp_scr[l].astype(f32)).astype(bf16)
+            dh2 = dot_nt(du, wup[l])
             a_down[l] += dot(e2.T, act_scr[l])
-            a_small[l, 7:8, :] += row_sum(e2.astype(f32))
-            da = dot_nt(e2, wdown[l])
-            du = (da * gp_scr[l].astype(f32)).astype(bf16)
             a_up[l] += dot(h2.T, du)
             dus = row_sum(du.astype(f32))
             for c in range(hidden // width):
                 a_small[l, 8 + c:9 + c, :] += dus[:, c * width:(c + 1) * width]
-            dh2 = dot_nt(du, wup[l])
             a_small[l, 1:2, :] += row_sum(dh2 * n2)
             a_small[l, 3:4, :] += row_sum(dh2)
             g1 = g + norm_back(dh2, n2, rstd2, gains[l, 1:2, :])
             e1 = g1.astype(bf16)
+            dm = dot_nt(e1, wout[l])
             a_out[l] += dot(mixed.T, e1)
             a_small[l, 6:7, :] += row_sum(e1.astype(f32))
-            dm = dot_nt(e1, wout[l])
             dm1 = dm * rl
             dmo = -(dm1 * mixed.astype(f32))
             dm1 = dm1.astype(bf16)
             dmo = dmo.astype(bf16)
-            lhs, dm_t, q_t, v_t, dq, dv_t, dk_t = [], [], [], [], [], [], []
-            for b in range(UNIT_BINS):
-                rows = slice(b * BIN, (b + 1) * BIN)
-                lhs.append(jnp.concatenate([dm1[rows], dmo[rows]], 1))
-                dm_t.append(dm1[rows].T)
-                q_t.append(q[rows].T)
-                v_t.append(v[rows].T)
-                dq.append(None)
-                dv_t.append([])
-                dk_t.append([])
-            bins = range(UNIT_BINS)
-            rows_of = [slice(b * BIN, (b + 1) * BIN) for b in bins]
-
-            def d_scores(j):
-                return [dot(lhs[b], jnp.concatenate([pair_columns(v_t[b], j), mask_columns[j]], 0)) for b in bins]
-
-            ahead = d_scores(0)
-            for j in range(pairs):
-                top, low = 2 * j * HEAD, (2 * j + 2) * HEAD
-                z = ahead
-                if j + 1 < pairs:
-                    ahead = d_scores(j + 1)
-                es = [e_scr[l, rows_of[b], 2 * j * BIN:(2 * j + 2) * BIN] for b in bins]
+            rows_of = [slice(b * BIN, (b + 1) * BIN) for b in range(UNIT_BINS)]
+            dqkv_bins = []
+            for first in range(0, UNIT_BINS, BWD_GROUP):
+                bins = range(first, first + BWD_GROUP)
+                lhs = {b: jnp.concatenate([dm1[rows_of[b]], dmo[rows_of[b]]], 1) for b in bins}
+                dm_t = {b: dm1[rows_of[b]].T for b in bins}
+                q_t = {b: q[rows_of[b]].T for b in bins}
+                v_t = {b: v[rows_of[b]].T for b in bins}
+                dq = {b: None for b in bins}
+                dv_t = {b: [] for b in bins}
+                dk_t = {b: [] for b in bins}
+
+                def d_scores(j):
+                    return {b: dot(lhs[b], jnp.concatenate([pair_columns(v_t[b], j), mask_columns[j]], 0)) for b in bins}
+
+                ahead = d_scores(0)
+                for j in range(pairs):
+                    top, low = 2 * j * HEAD, (2 * j + 2) * HEAD
+                    z = ahead
+                    if j + 1 < pairs:
+                        ahead = d_scores(j + 1)
+                    es = {b: e_scr[l, rows_of[b], 2 * j * BIN:(2 * j + 2) * BIN] for b in bins}
+                    for b in bins:
+                        pv = dot(dm_t[b][top:low], es[b])
+                        dv_t[b] += [pv[:HEAD, :BIN], pv[HEAD:, BIN:]]
+                    ds = {b: es[b] * z[b].astype(bf16) for b in bins}
+                    for b in bins:
+                        part = dot(ds[b], pair_rows(k[rows_of[b]], j))
+                        dq[b] = part if dq[b] is None else dq[b] + part
+                    for b in bins:
+                        pk = dot(q_t[b][top:low], ds[b])
+                        dk_t[b] += [pk[:HEAD, :BIN], pk[HEAD:, BIN:]]
                 for b in bins:
-                    pv = dot(dm_t[b][top:low], es[b])
-                    dv_t[b] += [pv[:HEAD, :BIN], pv[HEAD:, BIN:]]
-                ds = [es[b] * z[b].astype(bf16) for b in bins]
-                for b in bins:
-                    part = dot(ds[b], pair_rows(k[rows_of[b]], j))
-                    dq[b] = part if dq[b] is None else dq[b] + part
-                for b in bins:
-                    pk = dot(q_t[b][top:low], ds[b])
-                    dk_t[b] += [pk[:HEAD, :BIN], pk[HEAD:, BIN:]]
-            dqkv_bins = []
-            for b in range(UNIT_BINS):
-                dv = jnp.concatenate(dv_t[b], 0).T
-                dk = jnp.concatenate(dk_t[b], 0).T * LN2
-                dqkv_bins.append(jnp.concatenate([(dq[b] * HEAD ** -0.5).astype(bf16), dk.astype(bf16), dv.astype(bf16)], 1))
+                    dv = jnp.concatenate(dv_t[b], 0).T
+                    dk = jnp.concatenate(dk_t[b], 0).T * LN2
+                    dqkv_bins.append(jnp.concatenate([(dq[b] * HEAD ** -0.5).astype(bf16), dk.astype(bf16), dv.astype(bf16)], 1))
             dqkv = jnp.concatenate(dqkv_bins, 0)
+            dh = dot_nt(dqkv, wqkv[l])
             a_qkv[l] += dot(h1.T, dqkv)
             sums = row_sum(dqkv.astype(f32))
             a_small[l, 4:5, :] += sums[:, :width]
             a_small[l, 5:6, :] += sums[:, 2 * width:]
-            dh = dot_nt(dqkv, wqkv[l])
             a_small[l, 0:1, :] += row_sum(dh * n1)
             a_small[l, 2:3, :] += row_sum(dh)
             g = g1 + norm_back(dh, n1, rstd1, gains[l, 0:1, :])
@@ -317,15 +314,16 @@
         p_iota = lax.broadcasted_iota(jnp.int32, (slot_rows, BIN), 1)
         both = jnp.concatenate([out_b, grad_b], 1)
         for b in range(UNIT_BINS):
+            homes, picks = [], []
             for m in range(MEMBERS):
                 slot = (u * UNIT_BINS + b) * MEMBERS + m
                 t, o, n = mem_traj[slot], mem_off[slot], mem_len[slot]
-                pick = jnp.where((p_iota - o == s_iota) & (s_iota < n), 1.0, 0.0).astype(bf16)
-                rows = dot(pick, both[b * BIN:(b + 1) * BIN]).astype(bf16)
-
-                home = jnp.where(n > 0, t, trajs)
-                out[home] = rows[:, :width]
-                gtok[home] = rows[:, width:]
+                picks.append(jnp.where((p_iota - o == s_iota) & (s_iota < n), 1.0, 0.0).astype(bf16))
+                homes.append(jnp.where(n > 0, t, trajs))
+            rows = dot(jnp.concatenate(picks, 0), both[b * BIN:(b + 1) * BIN]).astype(bf16)
+            for m, home in enumerate(homes):
+                out[home] = rows[m * slot_rows:(m + 1) * slot_rows, :width]
+                gtok[home] = rows[m * slot_rows:(m + 1) * slot_rows, width:]
         return carry
 
     lax.fori_loop(0, units, body, 0)
@@ -351,9 +349,11 @@
             at += width
         gsum[l, at:at + SMALL, :] = a_small[l].astype(bf16)
     mine = parity[0]
+    half = gsum.shape[1] // 2
     stores += [
-        pltpu.make_async_copy(gsum.at[mine], mine_hbm, sems.at[2]),
-        pltpu.make_async_copy(gsum.at[1 - mine], other_hbm, sems.at[3]),
+        pltpu.make_async_copy(gsum.at[l, pl.ds(i * half, half)], to, sems.at[2 + 2 * k + i])
+        for k, (l, pair) in enumerate(((1 - mine, (other_a, other_b)), (mine, (mine_a, mine_b))))
+        for i, to in enumerate(pair)
     ]
     for copy in stores[2:]:
         copy.start()
@@ -368,10 +368,9 @@
     unit = BIN * UNIT_BINS
     slots = 2 * (trajs + UNIT_BINS)
     per_layer = 4 * width + 2 * hidden + SMALL
-    vm = pl.BlockSpec(memory_space=pltpu.VMEM)
     sm = pl.BlockSpec(memory_space=pltpu.SMEM)
     hbm = pl.BlockSpec(memory_space=pl.ANY)
-    sums = jax.ShapeDtypeStruct((per_layer, width), bf16)
+    sums = jax.ShapeDtypeStruct((per_layer // 2, width), bf16)
     return pl.pallas_call(
         functools.partial(main_kernel, steps_top=steps_top),
         out_shape=(
@@ -379,12 +378,17 @@
             jax.ShapeDtypeStruct(tokens.shape, bf16),
             sums,
             sums,
+            sums,
+            sums,
         ),
-        in_specs=[sm, sm, hbm, hbm] + [vm] * 9,
-        out_specs=(hbm, hbm, hbm, hbm),
+        in_specs=[sm, sm] + [hbm] * 11,
+        out_specs=(hbm,) * 6,
         scratch_shapes=[
             pltpu.VMEM(tokens.shape, bf16),
             pltpu.VMEM(tokens.shape, bf16),
+        ]
+        + [pltpu.VMEM(a.shape, a.dtype) for a in (gains, shifts, wqkv, qvb, wout, outb, wup, upb, wdown)]
+        + [
             pltpu.VMEM((trajs + 1, slot_rows, width), bf16),
             pltpu.VMEM((trajs + 1, slot_rows, width), bf16),
             pltpu.VMEM((LAYERS, per_layer, width), bf16),
@@ -401,7 +405,7 @@
             pltpu.SMEM((slots,), jnp.int32),
             pltpu.SMEM((slots,), jnp.int32),
             pltpu.SMEM((slots,), jnp.int32),
-            pltpu.SemaphoreType.DMA((4,)),
+            pltpu.SemaphoreType.DMA((11,)),
         ],
         compiler_params=pltpu.CompilerParams(vmem_limit_bytes=56 * 1024 * 1024),
         name="layers",
@@ -411,27 +415,37 @@
 AXES = ("dp", "group")
 
 
-def finish_kernel(parity, mine, other, gains, shifts, qkv, qvb, out, outb, up, upb, down):
-    width = mine.shape[1]
+def finish_kernel(parity, mine_a, mine_b, other_a, other_b, gains, shifts, qkv, qvb, out, outb, up, upb, down):
+    rows, width = mine_a.shape
     hidden = up.shape[2]
     for p in range(LAYERS):
 
         @pl.when(parity[0] == p)
         def _():
             for l in range(LAYERS):
-                src = mine if l == p else other
+                pieces = (mine_a, mine_b) if l == p else (other_a, other_b)
+
+                def take(at, count):
+                    found = []
+                    while count > 0:
+                        piece, first = divmod(at, rows)
+                        now = min(count, rows - first)
+                        found.append(pieces[piece][first:first + now, :].astype(f32))
+                        at, count = at + now, count - now
+                    return found[0] if len(found) == 1 else jnp.concatenate(found, 0)
+
                 at = 0
                 for c in range(3):
-                    qkv[l, :, c * width:(c + 1) * width] = src[at:at + width, :].astype(f32)
+                    qkv[l, :, c * width:(c + 1) * width] = take(at, width)
                     at += width
-                out[l] = src[at:at + width, :].astype(f32)
+                out[l] = take(at, width)
                 at += width
                 for c in range(hidden // width):
-                    up[l, :, c * width:(c + 1) * width] = src[at:at + width, :].astype(f32)
+                    up[l, :, c * width:(c + 1) * width] = take(at, width)
                     at += width
-                down[l] = src[at:at + hidden, :].astype(f32)
+                down[l] = take(at, hidden)
                 at += hidden
-                small = src[at:at + SMALL, :].astype(f32)
+                small = take(at, SMALL)
                 gains[l] = small[0:2]
                 shifts[l] = small[2:4]
                 qvb[l] = small[4:6]
@@ -446,11 +460,11 @@
     return pl.pallas_call(
         finish_kernel,
         out_shape=tuple(jax.ShapeDtypeStruct(a.shape, f32) for a in args[2:11]),
-        in_specs=[sm, vm, vm],
+        in_specs=[sm] + [vm] * 4,
         out_specs=(vm,) * 9,
         compiler_params=pltpu.CompilerParams(vmem_limit_bytes=16 * 1024 * 1024),
         name="finish",
-    )(parity, mine, other)
+    )(parity, *mine, *other)
 
 
 def exchange(x, bits, devices):
@@ -462,18 +476,22 @@
 
 
 def all_sum(mine, other, index, devices):
-    x = added(mine, exchange(other, (1, 1), devices))
     bits = [1 << i for i in range(1, devices.bit_length() - 1)]
     crossed = list(bits)
     for i in range(0, len(bits) - 1, 2):
         crossed[i], crossed[i + 1] = bits[i + 1], bits[i]
     steps = list(zip(bits, crossed))
-    turn = len(steps) // 2
-    orders = [steps, steps[turn:] + steps[:turn]]
-    size = x.shape[0] // len(orders)
-    parts = [x[i * size:(i + 1) * size] for i in range(len(orders))]
+    order = []
+    for i in range(0, len(steps), 4):
+        some = steps[i:i + 4]
+        order += some[0::2] + some[1::2]
+    turned = list(order)
+    for i in range(0, len(order) - 1, 2):
+        turned[i], turned[i + 1] = order[i + 1], order[i]
+    orders = [order, turned]
+    parts = [added(m, exchange(o, (1, 1), devices)) for m, o in zip(mine, other)]
     lows = [(index // jnp.where(index % 2 == 0, order[0][0], order[0][1])) % 2 == 0 for order in orders]
-    half = size // 2
+    half = parts[0].shape[0] // 2
     kept = [jnp.where(low, p[:half], p[half:]) for p, low in zip(parts, lows)]
     sent = [jnp.where(low, p[half:], p[:half]) for p, low in zip(parts, lows)]
     for step in range(len(steps)):
@@ -485,8 +503,7 @@
         jnp.where(low, jnp.concatenate([p, q]), jnp.concatenate([q, p]))
         for p, q, low in zip(kept, got, lows)
     ]
-    x = jnp.concatenate(parts)
-    return x, exchange(x, (1, 1), devices)
+    return parts, [exchange(p, (1, 1), devices) for p in parts]
 
 
 def solution(mesh):
@@ -496,8 +513,8 @@
     def per_device(*args):
         index = lax.axis_index("dp") * mesh_shape["group"] + lax.axis_index("group")
         parity = (index % 2).astype(jnp.int32).reshape(1)
-        output, grad_tokens, mine, other = main_call(args, STEPS, parity)
-        mine, other = all_sum(mine, other, index, devices)
+        output, grad_tokens, mine_a, mine_b, other_a, other_b = main_call(args, STEPS, parity)
+        mine, other = all_sum((mine_a, mine_b), (other_a, other_b), index, devices)
         return (output, grad_tokens) + tuple(finish_call(parity, mine, other, args))
 
     rows = P(AXES, None, None)

time: 75.5 us -> 67.5 us (0.89)
  Pallas kernels: 37.5 us -> 32.8 us
  waiting for transfers between devices: 17.6 us -> 12.9 us
  starting transfers between devices: 17.9 us -> 19.4 us
    pallas_call x1, Pallas kernels: 36.2 us -> 31.5 us  [main_call(): pl.pallas_call(functools.partial(main_kernel, steps_top=steps_top), out_s...]
    ppermute x12 -> x14, waiting for transfers between devices: 17.6 us -> 12.9 us  [exchange(): return lax.ppermute(x, AXES, [(i, i ^ bits[i % 2]) for i in range(devices)])]
    ppermute x12 -> x14, starting transfers between devices: 17.9 us -> 19.4 us  [exchange(): return lax.ppermute(x, AXES, [(i, i ^ bits[i % 2]) for i in range(devices)])]
  transfers between devices with their start and end apart: 12 -> 14, of which waited for: 10 -> 12; matrix products, arithmetic and copies ran while one was open for 0% -> 2% of each run, Pallas kernels for 0% -> 0%
where the time goes in v3:
time: 67.5 us; the launch traced here: 67.3 us
  Pallas kernels  32.8 us (49%)
  starting transfers between devices  19.4 us (29%)
  waiting for transfers between devices  12.9 us (19%)
  other arithmetic  1.46 us (2%)
  between operations  0.78 us (1%)
    pallas_call x1, Pallas kernels, main_call(): pl.pallas_call(functools.partial(main_kernel, steps_top=steps_top), out_s...  31.5 us
    ppermute x14, starting transfers between devices, exchange(): return lax.ppermute(x, AXES, [(i, i ^ bits[i % 2]) for i in range(devices)])  19.4 us
    ppermute x14, waiting for transfers between devices, exchange(): return lax.ppermute(x, AXES, [(i, i ^ bits[i % 2]) for i in range(devices)])  12.9 us
  transfers between devices with their start and end apart: 14, of which 12 were waited for; matrix products, arithmetic and copies ran while one was open for 2% of the time, Pallas kernels for 0%

profile of v3, /device:TPU:0, one launch (start us, length us, event | category | flops | bytes accessed | tf_op | source)
XLA Modules:
  0.0 67.3 jit_solution(4080667706037734074)
XLA Ops:
  0.7 31.5 %layers.1 = (bf16[32,96,128]{2,1,0:T(8,128)(2,1)}, bf16[32,96,128]{2,1,0:T(8,128)(2,1)}, bf16[800,128]{1,0:T(8,128)(2,1)}, bf16[800,128]{1,0:T(8,128)(2,1)}, bf1...) custom-call(s32[32]{0:T(128)} %lengths.1, s32[1]{0:T(128)} %bitcast.parity, bf16[32,96,128]{2,1,0:T(8,128)(2,1)} %tok_hbm.1, ...), custom_call_target="tpu_custom_call" | custom-call | tf_op jit(solution)/shard_map/layers/pallas_call | solution.py:374
  32.1 0.5 collective-permute-start
  32.7 0.1 collective-permute-start.6
  32.7 1.2 %collective-permute-done = bf16[800,128]{1,0:T(8,128)(2,1)S(1)} collective-permute-done((bf16[800,128]{1,0:T(8,128)(2,1)}, bf16[800,128]{1,0:T(8,128)(2,1)S(1)}, u32[]{:S(2)}, u32[]{:S(2)}) %collective-permute-start) | collective-permute-done | bytes 204832 | tf_op jit(solution)/shard_map/ppermute | solution.py:471
  33.9 1.0 %add_convert_fusion.1 = bf16[800,128]{1,0:T(8,128)(2,1)S(1)} fusion(bf16[800,128]{1,0:T(8,128)(2,1)S(1)} %collective-permute-done, bf16[800,128]{1,0:T(8,128)(2,1)} %get-tuple-element.28), kind=kLoop, calls=%fused_computation.1 | loop fusion | flops 409600 | bytes 614400 | tf_op jit(solution)/shard_map/convert_element_type | solution.py:475
  34.9 0.0 copy-start
  35.0 2.9 %collective-permute-start.1 = (bf16[400,128]{1,0:T(8,128)(2,1)S(1)}, bf16[400,128]{1,0:T(8,128)(2,1)S(1)}, u32[]{:S(2)}, u32[]{:S(2)}) collective-permute-start(bf16[400,128]{1,0:T(8,128)(2,1)S(1)} %broadcast_select_fusion.1), channel_id=1, source_target_pairs={{0,2},{1,5},{2,0},{3,7},{4,6},{5,1},{6,4},{7,3},{8,10},{9,13},{10,... | collective-permute-start | bytes 307208 | tf_op jit(solution)/shard_map/ppermute | solution.py:471
  37.9 0.0 collective-permute-done.6
  37.9 0.0 copy-done
  37.9 0.1 add_convert_fusion
  38.0 1.6 %collective-permute-start.7 = (bf16[400,128]{1,0:T(8,128)(2,1)S(1)}, bf16[400,128]{1,0:T(8,128)(2,1)S(1)}, u32[]{:S(2)}, u32[]{:S(2)}) collective-permute-start(bf16[400,128]{1,0:T(8,128)(2,1)S(1)} %broadcast_select_fusion), channel_id=1, source_target_pairs={{0,8},{1,17},{2,10},{3,19},{4,12},{5,21},{6,14},{7,23},{8,0},{9,25... | collective-permute-start | bytes 307208 | tf_op jit(solution)/shard_map/ppermute | solution.py:471
  39.6 0.9 %collective-permute-done.1 = bf16[400,128]{1,0:T(8,128)(2,1)S(1)} collective-permute-done((bf16[400,128]{1,0:T(8,128)(2,1)S(1)}, bf16[400,128]{1,0:T(8,128)(2,1)S(1)}, u32[]{:S(2)}, u32[]{:S(2)}) %collective-permute-start.1) | collective-permute-done | bytes 102432 | tf_op jit(solution)/shard_map/ppermute | solution.py:471
  40.6 2.2 %collective-permute-start.2 = (bf16[400,128]{1,0:T(8,128)(2,1)S(1)}, bf16[400,128]{1,0:T(8,128)(2,1)S(1)}, u32[]{:S(2)}, u32[]{:S(2)}) collective-permute-start(bf16[400,128]{1,0:T(8,128)(2,1)S(1)} %add_convert_fusion.9), channel_id=1, source_target_pairs={{0,8},{1,17},{2,10},{3,19},{4,12},{5,21},{6,14},{7,23},{8,0},{9,25... | collective-permute-start | bytes 307208 | tf_op jit(solution)/shard_map/ppermute | solution.py:471
  42.8 0.8 %collective-permute-done.7 = bf16[400,128]{1,0:T(8,128)(2,1)S(1)} collective-permute-done((bf16[400,128]{1,0:T(8,128)(2,1)S(1)}, bf16[400,128]{1,0:T(8,128)(2,1)S(1)}, u32[]{:S(2)}, u32[]{:S(2)}) %collective-permute-start.7) | collective-permute-done | bytes 102432 | tf_op jit(solution)/shard_map/ppermute | solution.py:471
  43.6 1.1 %collective-permute-start.8 = (bf16[400,128]{1,0:T(8,128)(2,1)S(1)}, bf16[400,128]{1,0:T(8,128)(2,1)S(1)}, u32[]{:S(2)}, u32[]{:S(2)}) collective-permute-start(bf16[400,128]{1,0:T(8,128)(2,1)S(1)} %add_convert_fusion.5), channel_id=1, source_target_pairs={{0,2},{1,5},{2,0},{3,7},{4,6},{5,1},{6,4},{7,3},{8,10},{9,13},{10,... | collective-permute-start | bytes 307208 | tf_op jit(solution)/shard_map/ppermute | solution.py:471
  44.7 1.4 %collective-permute-done.2 = bf16[400,128]{1,0:T(8,128)(2,1)S(1)} collective-permute-done((bf16[400,128]{1,0:T(8,128)(2,1)S(1)}, bf16[400,128]{1,0:T(8,128)(2,1)S(1)}, u32[]{:S(2)}, u32[]{:S(2)}) %collective-permute-start.2) | collective-permute-done | bytes 102432 | tf_op jit(solution)/shard_map/ppermute | solution.py:471
  46.1 1.6 %collective-permute-start.3 = (bf16[400,128]{1,0:T(8,128)(2,1)S(1)}, bf16[400,128]{1,0:T(8,128)(2,1)S(1)}, u32[]{:S(2)}, u32[]{:S(2)}) collective-permute-start(bf16[400,128]{1,0:T(8,128)(2,1)S(1)} %add_convert_fusion.8), channel_id=1, source_target_pairs={{0,4},{1,3},{2,6},{3,1},{4,0},{5,7},{6,2},{7,5},{8,12},{9,11},{10,... | collective-permute-start | bytes 307208 | tf_op jit(solution)/shard_map/ppermute | solution.py:471
  47.7 0.6 collective-permute-done.8
  48.4 1.8 %collective-permute-start.9 = (bf16[400,128]{1,0:T(8,128)(2,1)S(1)}, bf16[400,128]{1,0:T(8,128)(2,1)S(1)}, u32[]{:S(2)}, u32[]{:S(2)}) collective-permute-start(bf16[400,128]{1,0:T(8,128)(2,1)S(1)} %add_convert_fusion.4), channel_id=1, source_target_pairs={{0,16},{1,9},{2,18},{3,11},{4,20},{5,13},{6,22},{7,15},{8,24},{9,1... | collective-permute-start | bytes 307208 | tf_op jit(solution)/shard_map/ppermute | solution.py:471
  50.2 0.6 collective-permute-done.3
  50.9 2.5 %collective-permute-start.4 = (bf16[400,128]{1,0:T(8,128)(2,1)S(1)}, bf16[400,128]{1,0:T(8,128)(2,1)S(1)}, u32[]{:S(2)}, u32[]{:S(2)}) collective-permute-start(bf16[400,128]{1,0:T(8,128)(2,1)S(1)} %add_convert_fusion.7), channel_id=1, source_target_pairs={{0,16},{1,9},{2,18},{3,11},{4,20},{5,13},{6,22},{7,15},{8,24},{9,1... | collective-permute-start | bytes 307208 | tf_op jit(solution)/shard_map/ppermute | solution.py:471
  53.3 0.8 %collective-permute-done.9 = bf16[400,128]{1,0:T(8,128)(2,1)S(1)} collective-permute-done((bf16[400,128]{1,0:T(8,128)(2,1)S(1)}, bf16[400,128]{1,0:T(8,128)(2,1)S(1)}, u32[]{:S(2)}, u32[]{:S(2)}) %collective-permute-start.9) | collective-permute-done | bytes 102432 | tf_op jit(solution)/shard_map/ppermute | solution.py:471
  54.2 2.2 %collective-permute-start.10 = (bf16[400,128]{1,0:T(8,128)(2,1)S(1)}, bf16[400,128]{1,0:T(8,128)(2,1)S(1)}, u32[]{:S(2)}, u32[]{:S(2)}) collective-permute-start(bf16[400,128]{1,0:T(8,128)(2,1)S(1)} %add_convert_fusion.3), channel_id=1, source_target_pairs={{0,4},{1,3},{2,6},{3,1},{4,0},{5,7},{6,2},{7,5},{8,12},{9,11},{10,... | collective-permute-start | bytes 307208 | tf_op jit(solution)/shard_map/ppermute | solution.py:471
  56.3 1.9 %collective-permute-done.4 = bf16[400,128]{1,0:T(8,128)(2,1)S(1)} collective-permute-done((bf16[400,128]{1,0:T(8,128)(2,1)S(1)}, bf16[400,128]{1,0:T(8,128)(2,1)S(1)}, u32[]{:S(2)}, u32[]{:S(2)}) %collective-permute-start.4) | collective-permute-done | bytes 102432 | tf_op jit(solution)/shard_map/ppermute | solution.py:471
  58.3 0.1 collective-permute-start.5
  58.3 0.7 %collective-permute-done.10 = bf16[400,128]{1,0:T(8,128)(2,1)S(1)} collective-permute-done((bf16[400,128]{1,0:T(8,128)(2,1)S(1)}, bf16[400,128]{1,0:T(8,128)(2,1)S(1)}, u32[]{:S(2)}, u32[]{:S(2)}) %collective-permute-start.10) | collective-permute-done | bytes 102432 | tf_op jit(solution)/shard_map/ppermute | solution.py:471
  59.1 2.7 %collective-permute-start.11 = (bf16[400,128]{1,0:T(8,128)(2,1)S(1)}, bf16[400,128]{1,0:T(8,128)(2,1)S(1)}, u32[]{:S(2)}, u32[]{:S(2)}) collective-permute-start(bf16[400,128]{1,0:T(8,128)(2,1)S(1)} %add_convert_fusion.2), channel_id=1, source_target_pairs={{0,8},{1,17},{2,10},{3,19},{4,12},{5,21},{6,14},{7,23},{8,0},{9,25... | collective-permute-start | bytes 307208 | tf_op jit(solution)/shard_map/ppermute | solution.py:471
  61.8 1.2 %collective-permute-done.5 = bf16[400,128]{1,0:T(8,128)(2,1)S(1)} collective-permute-done((bf16[400,128]{1,0:T(8,128)(2,1)S(1)}, bf16[400,128]{1,0:T(8,128)(2,1)S(1)}, u32[]{:S(2)}, u32[]{:S(2)}) %collective-permute-start.5) | collective-permute-done | bytes 102432 | tf_op jit(solution)/shard_map/ppermute | solution.py:471
  63.0 0.1 maximum_select_fusion.mine_a
  63.0 0.1 collective-permute-start.12
  63.1 1.3 %collective-permute-done.11 = bf16[400,128]{1,0:T(8,128)(2,1)S(1)} collective-permute-done((bf16[400,128]{1,0:T(8,128)(2,1)S(1)}, bf16[400,128]{1,0:T(8,128)(2,1)S(1)}, u32[]{:S(2)}, u32[]{:S(2)}) %collective-permute-start.11) | collective-permute-done | bytes 102432 | tf_op jit(solution)/shard_map/ppermute | solution.py:471
  64.4 0.1 maximum_select_fusion.1.mine_b
  64.5 0.1 collective-permute-start.13
  64.6 0.0 collective-permute-done.12.other_a
  64.6 1.4 %collective-permute-done.13.other_b = bf16[800,128]{1,0:T(8,128)(2,1)S(1)} collective-permute-done((bf16[800,128]{1,0:T(8,128)(2,1)S(1)}, bf16[800,128]{1,0:T(8,128)(2,1)S(1)}, u32[]{:S(2)}, u32[]{:S(2)}) %collective-permute-start.13) | collective-permute-done | bytes 204832 | tf_op jit(solution)/shard_map/ppermute | solution.py:471
  66.0 1.3 %finish.1 = (f32[2,2,128]{2,1,0:T(2,128)}, f32[2,2,128]{2,1,0:T(2,128)}, f32[2,128,384]{2,1,0:T(8,128)}, f32[2,2,128]{2,1,0:T(2,128)}, f32[2,128,128]{2,1,0:T(8,...) custom-call(s32[1]{0:T(128)} %bitcast.parity, ...), custom_call_target="tpu_custom_call" | custom-call | tf_op jit(solution)/shard_map/finish/pallas_call | solution.py:460
  (10 shorter events, 0.3 us)
Async XLA Ops:
  32.1 1.8 %collective-permute-start = (bf16[800,128]{1,0:T(8,128)(2,1)}, bf16[800,128]{1,0:T(8,128)(2,1)S(1)}, u32[]{:S(2)}, u32[]{:S(2)}) collective-permute-start(bf16[800,128]{1,0:T(8,128)(2,1)} %get-tuple-element.29), channel_id=1, source_target_pairs={{0,1},{1,0},{2,3},{3,2},{4,5},{5,4},{6,7},{7,6},{8,9},{9,8},{10,11... | collective-permute-start | bytes 614408 | tf_op jit(solution)/shard_map/ppermute | solution.py:471
  32.7 5.3 %collective-permute-start.6 = (bf16[800,128]{1,0:T(8,128)(2,1)}, bf16[800,128]{1,0:T(8,128)(2,1)S(1)}, u32[]{:S(2)}, u32[]{:S(2)}) collective-permute-start(bf16[800,128]{1,0:T(8,128)(2,1)} %get-tuple-element.31), channel_id=1, source_target_pairs={{0,1},{1,0},{2,3},{3,2},{4,5},{5,4},{6,7},{7,6},{8,9},{9,8},{10,11... | collective-permute-start | bytes 614408 | tf_op jit(solution)/shard_map/ppermute | solution.py:471
  34.9 3.0 %copy-start = (bf16[800,128]{1,0:T(8,128)(2,1)S(1)}, bf16[800,128]{1,0:T(8,128)(2,1)}, u32[]{:S(2)}) copy-start(bf16[800,128]{1,0:T(8,128)(2,1)} %get-tuple-element.30) | copy-start | bytes 614404
  35.0 5.6 %collective-permute-start.1 = (bf16[400,128]{1,0:T(8,128)(2,1)S(1)}, bf16[400,128]{1,0:T(8,128)(2,1)S(1)}, u32[]{:S(2)}, u32[]{:S(2)}) collective-permute-start(bf16[400,128]{1,0:T(8,128)(2,1)S(1)} %broadcast_select_fusion.1), channel_id=1, source_target_pairs={{0,2},{1,5},{2,0},{3,7},{4,6},{5,1},{6,4},{7,3},{8,10},{9,13},{10,... | collective-permute-start | bytes 307208 | tf_op jit(solution)/shard_map/ppermute | solution.py:471
  38.0 5.6 %collective-permute-start.7 = (bf16[400,128]{1,0:T(8,128)(2,1)S(1)}, bf16[400,128]{1,0:T(8,128)(2,1)S(1)}, u32[]{:S(2)}, u32[]{:S(2)}) collective-permute-start(bf16[400,128]{1,0:T(8,128)(2,1)S(1)} %broadcast_select_fusion), channel_id=1, source_target_pairs={{0,8},{1,17},{2,10},{3,19},{4,12},{5,21},{6,14},{7,23},{8,0},{9,25... | collective-permute-start | bytes 307208 | tf_op jit(solution)/shard_map/ppermute | solution.py:471
  40.6 5.5 %collective-permute-start.2 = (bf16[400,128]{1,0:T(8,128)(2,1)S(1)}, bf16[400,128]{1,0:T(8,128)(2,1)S(1)}, u32[]{:S(2)}, u32[]{:S(2)}) collective-permute-start(bf16[400,128]{1,0:T(8,128)(2,1)S(1)} %add_convert_fusion.9), channel_id=1, source_target_pairs={{0,8},{1,17},{2,10},{3,19},{4,12},{5,21},{6,14},{7,23},{8,0},{9,25... | collective-permute-start | bytes 307208 | tf_op jit(solution)/shard_map/ppermute | solution.py:471
  43.6 4.7 %collective-permute-start.8 = (bf16[400,128]{1,0:T(8,128)(2,1)S(1)}, bf16[400,128]{1,0:T(8,128)(2,1)S(1)}, u32[]{:S(2)}, u32[]{:S(2)}) collective-permute-start(bf16[400,128]{1,0:T(8,128)(2,1)S(1)} %add_convert_fusion.5), channel_id=1, source_target_pairs={{0,2},{1,5},{2,0},{3,7},{4,6},{5,1},{6,4},{7,3},{8,10},{9,13},{10,... | collective-permute-start | bytes 307208 | tf_op jit(solution)/shard_map/ppermute | solution.py:471
  46.1 4.7 %collective-permute-start.3 = (bf16[400,128]{1,0:T(8,128)(2,1)S(1)}, bf16[400,128]{1,0:T(8,128)(2,1)S(1)}, u32[]{:S(2)}, u32[]{:S(2)}) collective-permute-start(bf16[400,128]{1,0:T(8,128)(2,1)S(1)} %add_convert_fusion.8), channel_id=1, source_target_pairs={{0,4},{1,3},{2,6},{3,1},{4,0},{5,7},{6,2},{7,5},{8,12},{9,11},{10,... | collective-permute-start | bytes 307208 | tf_op jit(solution)/shard_map/ppermute | solution.py:471
  48.4 5.7 %collective-permute-start.9 = (bf16[400,128]{1,0:T(8,128)(2,1)S(1)}, bf16[400,128]{1,0:T(8,128)(2,1)S(1)}, u32[]{:S(2)}, u32[]{:S(2)}) collective-permute-start(bf16[400,128]{1,0:T(8,128)(2,1)S(1)} %add_convert_fusion.4), channel_id=1, source_target_pairs={{0,16},{1,9},{2,18},{3,11},{4,20},{5,13},{6,22},{7,15},{8,24},{9,1... | collective-permute-start | bytes 307208 | tf_op jit(solution)/shard_map/ppermute | solution.py:471
  50.9 7.3 %collective-permute-start.4 = (bf16[400,128]{1,0:T(8,128)(2,1)S(1)}, bf16[400,128]{1,0:T(8,128)(2,1)S(1)}, u32[]{:S(2)}, u32[]{:S(2)}) collective-permute-start(bf16[400,128]{1,0:T(8,128)(2,1)S(1)} %add_convert_fusion.7), channel_id=1, source_target_pairs={{0,16},{1,9},{2,18},{3,11},{4,20},{5,13},{6,22},{7,15},{8,24},{9,1... | collective-permute-start | bytes 307208 | tf_op jit(solution)/shard_map/ppermute | solution.py:471
  54.2 4.9 %collective-permute-start.10 = (bf16[400,128]{1,0:T(8,128)(2,1)S(1)}, bf16[400,128]{1,0:T(8,128)(2,1)S(1)}, u32[]{:S(2)}, u32[]{:S(2)}) collective-permute-start(bf16[400,128]{1,0:T(8,128)(2,1)S(1)} %add_convert_fusion.3), channel_id=1, source_target_pairs={{0,4},{1,3},{2,6},{3,1},{4,0},{5,7},{6,2},{7,5},{8,12},{9,11},{10,... | collective-permute-start | bytes 307208 | tf_op jit(solution)/shard_map/ppermute | solution.py:471
  58.3 4.7 %collective-permute-start.5 = (bf16[400,128]{1,0:T(8,128)(2,1)S(1)}, bf16[400,128]{1,0:T(8,128)(2,1)S(1)}, u32[]{:S(2)}, u32[]{:S(2)}) collective-permute-start(bf16[400,128]{1,0:T(8,128)(2,1)S(1)} %add_convert_fusion.6), channel_id=1, source_target_pairs={{0,2},{1,5},{2,0},{3,7},{4,6},{5,1},{6,4},{7,3},{8,10},{9,13},{10,... | collective-permute-start | bytes 307208 | tf_op jit(solution)/shard_map/ppermute | solution.py:471
  59.1 5.3 %collective-permute-start.11 = (bf16[400,128]{1,0:T(8,128)(2,1)S(1)}, bf16[400,128]{1,0:T(8,128)(2,1)S(1)}, u32[]{:S(2)}, u32[]{:S(2)}) collective-permute-start(bf16[400,128]{1,0:T(8,128)(2,1)S(1)} %add_convert_fusion.2), channel_id=1, source_target_pairs={{0,8},{1,17},{2,10},{3,19},{4,12},{5,21},{6,14},{7,23},{8,0},{9,25... | collective-permute-start | bytes 307208 | tf_op jit(solution)/shard_map/ppermute | solution.py:471
  63.0 1.5 %collective-permute-start.12 = (bf16[800,128]{1,0:T(8,128)(2,1)S(1)}, bf16[800,128]{1,0:T(8,128)(2,1)S(1)}, u32[]{:S(2)}, u32[]{:S(2)}) collective-permute-start(bf16[800,128]{1,0:T(8,128)(2,1)S(1)} %maximum_select_fusion.mine_a), channel_id=1, source_target_pairs={{0,1},{1,0},{2,3},{3,2},{4,5},{5,4},{6,7},{7,6},{8,9},{9,8},{10,11... | collective-permute-start | bytes 614408 | tf_op jit(solution)/shard_map/ppermute | solution.py:471
  64.5 1.5 %collective-permute-start.13 = (bf16[800,128]{1,0:T(8,128)(2,1)S(1)}, bf16[800,128]{1,0:T(8,128)(2,1)S(1)}, u32[]{:S(2)}, u32[]{:S(2)}) collective-permute-start(bf16[800,128]{1,0:T(8,128)(2,1)S(1)} %maximum_select_fusion.1.mine_b), channel_id=1, source_target_pairs={{0,1},{1,0},{2,3},{3,2},{4,5},{5,4},{6,7},{7,6},{8,9},{9,8},{10,11... | collective-permute-start | bytes 614408 | tf_op jit(solution)/shard_map/ppermute | solution.py:471

commit v4 on v3

--- a/solution.py
+++ b/solution.py
@@ -117,7 +117,7 @@
     lengths, parity, tok_hbm, cot_hbm, gains_hbm, shifts_hbm, wqkv_hbm, qvb_hbm, wout_hbm, outb_hbm, wup_hbm, upb_hbm, wdown_hbm,
     out_hbm, gtok_hbm, mine_a, mine_b, other_a, other_b,
     tok, cot, gains, shifts, wqkv, qvb, wout, outb, wup, upb, wdown, out, gtok, gsum,
-    a_qkv, a_out, a_up, a_down, a_small, e_scr, act_scr, gp_scr,
+    a_qkv, a_out, a_up, a_down, a_small, e_scr, act_scr, gp_scr, half_up, half_down,
     order, count, mem_traj, mem_off, mem_len, sems,
     *, steps_top,
 ):
@@ -137,6 +137,14 @@
     for copy in loads:
         copy.wait()
 
+    at = lax.broadcasted_iota(jnp.int32, (width, hidden), 0)
+    for l in range(LAYERS):
+        bias = 0.5 * upb[l:l + 1, :]
+        high = bias.astype(bf16).astype(f32)
+        half_up[l, :width, :] = wup[l] * jnp.asarray(0.5, bf16)
+        half_up[l, width:, :] = jnp.where(at == 0, high, jnp.where(at == 1, bias - high, 0.0)).astype(bf16)
+        half_down[l] = wdown[l] * jnp.asarray(0.5, bf16)
+
     masks = head_masks(width)
     mask_pairs = [
         jnp.concatenate([jnp.broadcast_to(masks[2 * j], (BIN, width)), jnp.broadcast_to(masks[2 * j + 1], (BIN, width))], 0)
@@ -163,6 +171,10 @@
 
     ones_t = jnp.ones((width, BIN), bf16)
     mask_columns = [pair_columns(ones_t, j) for j in range(pairs)]
+
+    lane = lax.broadcasted_iota(jnp.int32, (unit, width), 1)
+    ones_rows = jnp.ones((16, unit), bf16)
+    ones_lanes = jnp.where(lane < 2, 1.0, 0.0).astype(bf16)
 
     def body(u, carry):
         q_iota = lax.broadcasted_iota(jnp.int32, (BIN, BIN), 0)
@@ -229,14 +241,15 @@
             x1 = x + dot(mixed, wout[l]) + outb[l, 0:1, :]
             n2, rstd2 = norm_parts(x1)
             h2 = (n2 * gains[l, 1:2, :] + shifts[l, 1:2, :]).astype(bf16)
-            hid = dot(h2, wup[l]) + upb[l:l + 1, :]
+            hid = dot(jnp.concatenate([h2, ones_lanes], 1), half_up[l])
             sq = hid * hid
-            w = 0.5 * jnp.tanh(hid * (GELU_C + (GELU_C * GELU_K) * sq)) + 0.5
-            act = hid * w
-            gp = w + (act * (1.0 - w)) * (2 * GELU_C + (6 * GELU_C * GELU_K) * sq)
+            t = 1.0 + jnp.tanh(hid * (2 * GELU_C + (8 * GELU_C * GELU_K) * sq))
+            act = hid * t
             act_b = act.astype(bf16)
             act_scr[l] = act_b
-            gp_scr[l] = gp.astype(bf16)
+            rest = (2.0 - t).astype(bf16)
+            slope = jnp.asarray(2 * GELU_C, bf16) + jnp.asarray(24 * GELU_C * GELU_K, bf16) * sq.astype(bf16)
+            gp_scr[l] = t.astype(bf16) + act_b * rest * slope
             saved.append((n1, rstd1, h1, q, k, v, mixed, rl, n2, rstd2, h2))
             x = x1 + dot(act_b, wdown[l]) + outb[l, 1:2, :]
 
@@ -245,11 +258,12 @@
             n1, rstd1, h1, q, k, v, mixed, rl, n2, rstd2, h2 = saved[l]
             e2 = g.astype(bf16)
             a_small[l, 7:8, :] += row_sum(e2.astype(f32))
-            du = (dot_nt(e2, wdown[l]) * gp_scr[l].astype(f32)).astype(bf16)
+            du = dot_nt(e2, half_down[l]).astype(bf16) * gp_scr[l]
             dh2 = dot_nt(du, wup[l])
             a_down[l] += dot(e2.T, act_scr[l])
-            a_up[l] += dot(h2.T, du)
-            dus = row_sum(du.astype(f32))
+            both_up = dot(jnp.concatenate([h2.T, ones_rows], 0), du)
+            a_up[l] += both_up[:width]
+            dus = both_up[width:width + 1]
             for c in range(hidden // width):
                 a_small[l, 8 + c:9 + c, :] += dus[:, c * width:(c + 1) * width]
             a_small[l, 1:2, :] += row_sum(dh2 * n2)
@@ -301,8 +315,9 @@
                     dqkv_bins.append(jnp.concatenate([(dq[b] * HEAD ** -0.5).astype(bf16), dk.astype(bf16), dv.astype(bf16)], 1))
             dqkv = jnp.concatenate(dqkv_bins, 0)
             dh = dot_nt(dqkv, wqkv[l])
-            a_qkv[l] += dot(h1.T, dqkv)
-            sums = row_sum(dqkv.astype(f32))
+            both_qkv = dot(jnp.concatenate([h1.T, ones_rows], 0), dqkv)
+            a_qkv[l] += both_qkv[:width]
+            sums = both_qkv[width:width + 1]
             a_small[l, 4:5, :] += sums[:, :width]
             a_small[l, 5:6, :] += sums[:, 2 * width:]
             a_small[l, 0:1, :] += row_sum(dh * n1)
@@ -400,6 +415,8 @@
             pltpu.VMEM((LAYERS, unit, width // HEAD * BIN), bf16),
             pltpu.VMEM((LAYERS, unit, hidden), bf16),
             pltpu.VMEM((LAYERS, unit, hidden), bf16),
+            pltpu.VMEM((LAYERS, 2 * width, hidden), bf16),
+            pltpu.VMEM((LAYERS, hidden, width), bf16),
             pltpu.SMEM((trajs,), jnp.int32),
             pltpu.SMEM((steps_top + 1,), jnp.int32),
             pltpu.SMEM((slots,), jnp.int32),

time: 67.5 us -> 66.8 us (0.990)
  Pallas kernels: 32.8 us -> 32 us
    pallas_call x1, Pallas kernels: 31.5 us -> 30.7 us  [main_call(): pl.pallas_call(functools.partial(main_kernel, steps_top=steps_top), out_s...]
where the time goes in v4:
time: 66.8 us; the launch traced here: 66.6 us
  Pallas kernels  32 us (48%)
  starting transfers between devices  19.4 us (29%)
  waiting for transfers between devices  12.9 us (19%)
  other arithmetic  1.46 us (2%)
  between operations  0.78 us (1%)
    pallas_call x1, Pallas kernels, main_call(): pl.pallas_call(functools.partial(main_kernel, steps_top=steps_top), out_s...  30.7 us
    ppermute x14, starting transfers between devices, exchange(): return lax.ppermute(x, AXES, [(i, i ^ bits[i % 2]) for i in range(devices)])  19.4 us
    ppermute x14, waiting for transfers between devices, exchange(): return lax.ppermute(x, AXES, [(i, i ^ bits[i % 2]) for i in range(devices)])  12.9 us
  transfers between devices with their start and end apart: 14, of which 12 were waited for; matrix products, arithmetic and copies ran while one was open for 2% of the time, Pallas kernels for 0%

profile of v4, /device:TPU:0, one launch (start us, length us, event | category | flops | bytes accessed | tf_op | source)
XLA Modules:
  0.0 66.6 jit_solution(7964134546150222931)
XLA Ops:
  0.7 30.7 %layers.1 = (bf16[32,96,128]{2,1,0:T(8,128)(2,1)}, bf16[32,96,128]{2,1,0:T(8,128)(2,1)}, bf16[800,128]{1,0:T(8,128)(2,1)}, bf16[800,128]{1,0:T(8,128)(2,1)}, bf1...) custom-call(s32[32]{0:T(128)} %lengths.1, s32[1]{0:T(128)} %bitcast.parity, bf16[32,96,128]{2,1,0:T(8,128)(2,1)} %tok_hbm.1, ...), custom_call_target="tpu_custom_call" | custom-call | tf_op jit(solution)/shard_map/layers/pallas_call | solution.py:389
  31.4 0.5 collective-permute-start
  31.9 0.1 collective-permute-start.6
  32.0 1.2 %collective-permute-done = bf16[800,128]{1,0:T(8,128)(2,1)S(1)} collective-permute-done((bf16[800,128]{1,0:T(8,128)(2,1)}, bf16[800,128]{1,0:T(8,128)(2,1)S(1)}, u32[]{:S(2)}, u32[]{:S(2)}) %collective-permute-start) | collective-permute-done | bytes 204832 | tf_op jit(solution)/shard_map/ppermute | solution.py:488
  33.2 1.0 %add_convert_fusion.1 = bf16[800,128]{1,0:T(8,128)(2,1)S(1)} fusion(bf16[800,128]{1,0:T(8,128)(2,1)S(1)} %collective-permute-done, bf16[800,128]{1,0:T(8,128)(2,1)} %get-tuple-element.28), kind=kLoop, calls=%fused_computation.1 | loop fusion | flops 409600 | bytes 614400 | tf_op jit(solution)/shard_map/convert_element_type | solution.py:492
  34.2 0.0 copy-start
  34.2 3.0 %collective-permute-start.1 = (bf16[400,128]{1,0:T(8,128)(2,1)S(1)}, bf16[400,128]{1,0:T(8,128)(2,1)S(1)}, u32[]{:S(2)}, u32[]{:S(2)}) collective-permute-start(bf16[400,128]{1,0:T(8,128)(2,1)S(1)} %broadcast_select_fusion.1), channel_id=1, source_target_pairs={{0,2},{1,5},{2,0},{3,7},{4,6},{5,1},{6,4},{7,3},{8,10},{9,13},{10,... | collective-permute-start | bytes 307208 | tf_op jit(solution)/shard_map/ppermute | solution.py:488
  37.2 0.0 collective-permute-done.6
  37.2 0.0 copy-done
  37.2 0.1 add_convert_fusion
  37.3 1.6 %collective-permute-start.7 = (bf16[400,128]{1,0:T(8,128)(2,1)S(1)}, bf16[400,128]{1,0:T(8,128)(2,1)S(1)}, u32[]{:S(2)}, u32[]{:S(2)}) collective-permute-start(bf16[400,128]{1,0:T(8,128)(2,1)S(1)} %broadcast_select_fusion), channel_id=1, source_target_pairs={{0,8},{1,17},{2,10},{3,19},{4,12},{5,21},{6,14},{7,23},{8,0},{9,25... | collective-permute-start | bytes 307208 | tf_op jit(solution)/shard_map/ppermute | solution.py:488
  38.9 0.9 %collective-permute-done.1 = bf16[400,128]{1,0:T(8,128)(2,1)S(1)} collective-permute-done((bf16[400,128]{1,0:T(8,128)(2,1)S(1)}, bf16[400,128]{1,0:T(8,128)(2,1)S(1)}, u32[]{:S(2)}, u32[]{:S(2)}) %collective-permute-start.1) | collective-permute-done | bytes 102432 | tf_op jit(solution)/shard_map/ppermute | solution.py:488
  39.9 2.1 %collective-permute-start.2 = (bf16[400,128]{1,0:T(8,128)(2,1)S(1)}, bf16[400,128]{1,0:T(8,128)(2,1)S(1)}, u32[]{:S(2)}, u32[]{:S(2)}) collective-permute-start(bf16[400,128]{1,0:T(8,128)(2,1)S(1)} %add_convert_fusion.9), channel_id=1, source_target_pairs={{0,8},{1,17},{2,10},{3,19},{4,12},{5,21},{6,14},{7,23},{8,0},{9,25... | collective-permute-start | bytes 307208 | tf_op jit(solution)/shard_map/ppermute | solution.py:488
  42.0 0.8 %collective-permute-done.7 = bf16[400,128]{1,0:T(8,128)(2,1)S(1)} collective-permute-done((bf16[400,128]{1,0:T(8,128)(2,1)S(1)}, bf16[400,128]{1,0:T(8,128)(2,1)S(1)}, u32[]{:S(2)}, u32[]{:S(2)}) %collective-permute-start.7) | collective-permute-done | bytes 102432 | tf_op jit(solution)/shard_map/ppermute | solution.py:488
  42.9 1.1 %collective-permute-start.8 = (bf16[400,128]{1,0:T(8,128)(2,1)S(1)}, bf16[400,128]{1,0:T(8,128)(2,1)S(1)}, u32[]{:S(2)}, u32[]{:S(2)}) collective-permute-start(bf16[400,128]{1,0:T(8,128)(2,1)S(1)} %add_convert_fusion.5), channel_id=1, source_target_pairs={{0,2},{1,5},{2,0},{3,7},{4,6},{5,1},{6,4},{7,3},{8,10},{9,13},{10,... | collective-permute-start | bytes 307208 | tf_op jit(solution)/shard_map/ppermute | solution.py:488
  44.0 1.4 %collective-permute-done.2 = bf16[400,128]{1,0:T(8,128)(2,1)S(1)} collective-permute-done((bf16[400,128]{1,0:T(8,128)(2,1)S(1)}, bf16[400,128]{1,0:T(8,128)(2,1)S(1)}, u32[]{:S(2)}, u32[]{:S(2)}) %collective-permute-start.2) | collective-permute-done | bytes 102432 | tf_op jit(solution)/shard_map/ppermute | solution.py:488
  45.4 1.6 %collective-permute-start.3 = (bf16[400,128]{1,0:T(8,128)(2,1)S(1)}, bf16[400,128]{1,0:T(8,128)(2,1)S(1)}, u32[]{:S(2)}, u32[]{:S(2)}) collective-permute-start(bf16[400,128]{1,0:T(8,128)(2,1)S(1)} %add_convert_fusion.8), channel_id=1, source_target_pairs={{0,4},{1,3},{2,6},{3,1},{4,0},{5,7},{6,2},{7,5},{8,12},{9,11},{10,... | collective-permute-start | bytes 307208 | tf_op jit(solution)/shard_map/ppermute | solution.py:488
  47.0 0.6 collective-permute-done.8
  47.7 1.8 %collective-permute-start.9 = (bf16[400,128]{1,0:T(8,128)(2,1)S(1)}, bf16[400,128]{1,0:T(8,128)(2,1)S(1)}, u32[]{:S(2)}, u32[]{:S(2)}) collective-permute-start(bf16[400,128]{1,0:T(8,128)(2,1)S(1)} %add_convert_fusion.4), channel_id=1, source_target_pairs={{0,16},{1,9},{2,18},{3,11},{4,20},{5,13},{6,22},{7,15},{8,24},{9,1... | collective-permute-start | bytes 307208 | tf_op jit(solution)/shard_map/ppermute | solution.py:488
  49.5 0.6 collective-permute-done.3
  50.2 2.4 %collective-permute-start.4 = (bf16[400,128]{1,0:T(8,128)(2,1)S(1)}, bf16[400,128]{1,0:T(8,128)(2,1)S(1)}, u32[]{:S(2)}, u32[]{:S(2)}) collective-permute-start(bf16[400,128]{1,0:T(8,128)(2,1)S(1)} %add_convert_fusion.7), channel_id=1, source_target_pairs={{0,16},{1,9},{2,18},{3,11},{4,20},{5,13},{6,22},{7,15},{8,24},{9,1... | collective-permute-start | bytes 307208 | tf_op jit(solution)/shard_map/ppermute | solution.py:488
  52.6 0.8 %collective-permute-done.9 = bf16[400,128]{1,0:T(8,128)(2,1)S(1)} collective-permute-done((bf16[400,128]{1,0:T(8,128)(2,1)S(1)}, bf16[400,128]{1,0:T(8,128)(2,1)S(1)}, u32[]{:S(2)}, u32[]{:S(2)}) %collective-permute-start.9) | collective-permute-done | bytes 102432 | tf_op jit(solution)/shard_map/ppermute | solution.py:488
  53.4 2.2 %collective-permute-start.10 = (bf16[400,128]{1,0:T(8,128)(2,1)S(1)}, bf16[400,128]{1,0:T(8,128)(2,1)S(1)}, u32[]{:S(2)}, u32[]{:S(2)}) collective-permute-start(bf16[400,128]{1,0:T(8,128)(2,1)S(1)} %add_convert_fusion.3), channel_id=1, source_target_pairs={{0,4},{1,3},{2,6},{3,1},{4,0},{5,7},{6,2},{7,5},{8,12},{9,11},{10,... | collective-permute-start | bytes 307208 | tf_op jit(solution)/shard_map/ppermute | solution.py:488
  55.6 1.9 %collective-permute-done.4 = bf16[400,128]{1,0:T(8,128)(2,1)S(1)} collective-permute-done((bf16[400,128]{1,0:T(8,128)(2,1)S(1)}, bf16[400,128]{1,0:T(8,128)(2,1)S(1)}, u32[]{:S(2)}, u32[]{:S(2)}) %collective-permute-start.4) | collective-permute-done | bytes 102432 | tf_op jit(solution)/shard_map/ppermute | solution.py:488
  57.5 0.1 collective-permute-start.5
  57.6 0.7 %collective-permute-done.10 = bf16[400,128]{1,0:T(8,128)(2,1)S(1)} collective-permute-done((bf16[400,128]{1,0:T(8,128)(2,1)S(1)}, bf16[400,128]{1,0:T(8,128)(2,1)S(1)}, u32[]{:S(2)}, u32[]{:S(2)}) %collective-permute-start.10) | collective-permute-done | bytes 102432 | tf_op jit(solution)/shard_map/ppermute | solution.py:488
  58.4 2.7 %collective-permute-start.11 = (bf16[400,128]{1,0:T(8,128)(2,1)S(1)}, bf16[400,128]{1,0:T(8,128)(2,1)S(1)}, u32[]{:S(2)}, u32[]{:S(2)}) collective-permute-start(bf16[400,128]{1,0:T(8,128)(2,1)S(1)} %add_convert_fusion.2), channel_id=1, source_target_pairs={{0,8},{1,17},{2,10},{3,19},{4,12},{5,21},{6,14},{7,23},{8,0},{9,25... | collective-permute-start | bytes 307208 | tf_op jit(solution)/shard_map/ppermute | solution.py:488
  61.1 1.2 %collective-permute-done.5 = bf16[400,128]{1,0:T(8,128)(2,1)S(1)} collective-permute-done((bf16[400,128]{1,0:T(8,128)(2,1)S(1)}, bf16[400,128]{1,0:T(8,128)(2,1)S(1)}, u32[]{:S(2)}, u32[]{:S(2)}) %collective-permute-start.5) | collective-permute-done | bytes 102432 | tf_op jit(solution)/shard_map/ppermute | solution.py:488
  62.3 0.1 maximum_select_fusion.mine_a
  62.3 0.1 collective-permute-start.12
  62.4 1.3 %collective-permute-done.11 = bf16[400,128]{1,0:T(8,128)(2,1)S(1)} collective-permute-done((bf16[400,128]{1,0:T(8,128)(2,1)S(1)}, bf16[400,128]{1,0:T(8,128)(2,1)S(1)}, u32[]{:S(2)}, u32[]{:S(2)}) %collective-permute-start.11) | collective-permute-done | bytes 102432 | tf_op jit(solution)/shard_map/ppermute | solution.py:488
  63.7 0.1 maximum_select_fusion.1.mine_b
  63.8 0.1 collective-permute-start.13
  63.9 0.0 collective-permute-done.12.other_a
  63.9 1.4 %collective-permute-done.13.other_b = bf16[800,128]{1,0:T(8,128)(2,1)S(1)} collective-permute-done((bf16[800,128]{1,0:T(8,128)(2,1)S(1)}, bf16[800,128]{1,0:T(8,128)(2,1)S(1)}, u32[]{:S(2)}, u32[]{:S(2)}) %collective-permute-start.13) | collective-permute-done | bytes 204832 | tf_op jit(solution)/shard_map/ppermute | solution.py:488
  65.3 1.3 %finish.1 = (f32[2,2,128]{2,1,0:T(2,128)}, f32[2,2,128]{2,1,0:T(2,128)}, f32[2,128,384]{2,1,0:T(8,128)}, f32[2,2,128]{2,1,0:T(2,128)}, f32[2,128,128]{2,1,0:T(8,...) custom-call(s32[1]{0:T(128)} %bitcast.parity, ...), custom_call_target="tpu_custom_call" | custom-call | tf_op jit(solution)/shard_map/finish/pallas_call | solution.py:477
  (10 shorter events, 0.3 us)
Async XLA Ops:
  31.4 1.8 %collective-permute-start = (bf16[800,128]{1,0:T(8,128)(2,1)}, bf16[800,128]{1,0:T(8,128)(2,1)S(1)}, u32[]{:S(2)}, u32[]{:S(2)}) collective-permute-start(bf16[800,128]{1,0:T(8,128)(2,1)} %get-tuple-element.29), channel_id=1, source_target_pairs={{0,1},{1,0},{2,3},{3,2},{4,5},{5,4},{6,7},{7,6},{8,9},{9,8},{10,11... | collective-permute-start | bytes 614408 | tf_op jit(solution)/shard_map/ppermute | solution.py:488
  31.9 5.3 %collective-permute-start.6 = (bf16[800,128]{1,0:T(8,128)(2,1)}, bf16[800,128]{1,0:T(8,128)(2,1)S(1)}, u32[]{:S(2)}, u32[]{:S(2)}) collective-permute-start(bf16[800,128]{1,0:T(8,128)(2,1)} %get-tuple-element.31), channel_id=1, source_target_pairs={{0,1},{1,0},{2,3},{3,2},{4,5},{5,4},{6,7},{7,6},{8,9},{9,8},{10,11... | collective-permute-start | bytes 614408 | tf_op jit(solution)/shard_map/ppermute | solution.py:488
  34.2 3.0 %copy-start = (bf16[800,128]{1,0:T(8,128)(2,1)S(1)}, bf16[800,128]{1,0:T(8,128)(2,1)}, u32[]{:S(2)}) copy-start(bf16[800,128]{1,0:T(8,128)(2,1)} %get-tuple-element.30) | copy-start | bytes 614404
  34.2 5.6 %collective-permute-start.1 = (bf16[400,128]{1,0:T(8,128)(2,1)S(1)}, bf16[400,128]{1,0:T(8,128)(2,1)S(1)}, u32[]{:S(2)}, u32[]{:S(2)}) collective-permute-start(bf16[400,128]{1,0:T(8,128)(2,1)S(1)} %broadcast_select_fusion.1), channel_id=1, source_target_pairs={{0,2},{1,5},{2,0},{3,7},{4,6},{5,1},{6,4},{7,3},{8,10},{9,13},{10,... | collective-permute-start | bytes 307208 | tf_op jit(solution)/shard_map/ppermute | solution.py:488
  37.3 5.6 %collective-permute-start.7 = (bf16[400,128]{1,0:T(8,128)(2,1)S(1)}, bf16[400,128]{1,0:T(8,128)(2,1)S(1)}, u32[]{:S(2)}, u32[]{:S(2)}) collective-permute-start(bf16[400,128]{1,0:T(8,128)(2,1)S(1)} %broadcast_select_fusion), channel_id=1, source_target_pairs={{0,8},{1,17},{2,10},{3,19},{4,12},{5,21},{6,14},{7,23},{8,0},{9,25... | collective-permute-start | bytes 307208 | tf_op jit(solution)/shard_map/ppermute | solution.py:488
  39.9 5.5 %collective-permute-start.2 = (bf16[400,128]{1,0:T(8,128)(2,1)S(1)}, bf16[400,128]{1,0:T(8,128)(2,1)S(1)}, u32[]{:S(2)}, u32[]{:S(2)}) collective-permute-start(bf16[400,128]{1,0:T(8,128)(2,1)S(1)} %add_convert_fusion.9), channel_id=1, source_target_pairs={{0,8},{1,17},{2,10},{3,19},{4,12},{5,21},{6,14},{7,23},{8,0},{9,25... | collective-permute-start | bytes 307208 | tf_op jit(solution)/shard_map/ppermute | solution.py:488
  42.9 4.7 %collective-permute-start.8 = (bf16[400,128]{1,0:T(8,128)(2,1)S(1)}, bf16[400,128]{1,0:T(8,128)(2,1)S(1)}, u32[]{:S(2)}, u32[]{:S(2)}) collective-permute-start(bf16[400,128]{1,0:T(8,128)(2,1)S(1)} %add_convert_fusion.5), channel_id=1, source_target_pairs={{0,2},{1,5},{2,0},{3,7},{4,6},{5,1},{6,4},{7,3},{8,10},{9,13},{10,... | collective-permute-start | bytes 307208 | tf_op jit(solution)/shard_map/ppermute | solution.py:488
  45.4 4.7 %collective-permute-start.3 = (bf16[400,128]{1,0:T(8,128)(2,1)S(1)}, bf16[400,128]{1,0:T(8,128)(2,1)S(1)}, u32[]{:S(2)}, u32[]{:S(2)}) collective-permute-start(bf16[400,128]{1,0:T(8,128)(2,1)S(1)} %add_convert_fusion.8), channel_id=1, source_target_pairs={{0,4},{1,3},{2,6},{3,1},{4,0},{5,7},{6,2},{7,5},{8,12},{9,11},{10,... | collective-permute-start | bytes 307208 | tf_op jit(solution)/shard_map/ppermute | solution.py:488
  47.7 5.7 %collective-permute-start.9 = (bf16[400,128]{1,0:T(8,128)(2,1)S(1)}, bf16[400,128]{1,0:T(8,128)(2,1)S(1)}, u32[]{:S(2)}, u32[]{:S(2)}) collective-permute-start(bf16[400,128]{1,0:T(8,128)(2,1)S(1)} %add_convert_fusion.4), channel_id=1, source_target_pairs={{0,16},{1,9},{2,18},{3,11},{4,20},{5,13},{6,22},{7,15},{8,24},{9,1... | collective-permute-start | bytes 307208 | tf_op jit(solution)/shard_map/ppermute | solution.py:488
  50.2 7.3 %collective-permute-start.4 = (bf16[400,128]{1,0:T(8,128)(2,1)S(1)}, bf16[400,128]{1,0:T(8,128)(2,1)S(1)}, u32[]{:S(2)}, u32[]{:S(2)}) collective-permute-start(bf16[400,128]{1,0:T(8,128)(2,1)S(1)} %add_convert_fusion.7), channel_id=1, source_target_pairs={{0,16},{1,9},{2,18},{3,11},{4,20},{5,13},{6,22},{7,15},{8,24},{9,1... | collective-permute-start | bytes 307208 | tf_op jit(solution)/shard_map/ppermute | solution.py:488
  53.4 4.9 %collective-permute-start.10 = (bf16[400,128]{1,0:T(8,128)(2,1)S(1)}, bf16[400,128]{1,0:T(8,128)(2,1)S(1)}, u32[]{:S(2)}, u32[]{:S(2)}) collective-permute-start(bf16[400,128]{1,0:T(8,128)(2,1)S(1)} %add_convert_fusion.3), channel_id=1, source_target_pairs={{0,4},{1,3},{2,6},{3,1},{4,0},{5,7},{6,2},{7,5},{8,12},{9,11},{10,... | collective-permute-start | bytes 307208 | tf_op jit(solution)/shard_map/ppermute | solution.py:488
  57.5 4.7 %collective-permute-start.5 = (bf16[400,128]{1,0:T(8,128)(2,1)S(1)}, bf16[400,128]{1,0:T(8,128)(2,1)S(1)}, u32[]{:S(2)}, u32[]{:S(2)}) collective-permute-start(bf16[400,128]{1,0:T(8,128)(2,1)S(1)} %add_convert_fusion.6), channel_id=1, source_target_pairs={{0,2},{1,5},{2,0},{3,7},{4,6},{5,1},{6,4},{7,3},{8,10},{9,13},{10,... | collective-permute-start | bytes 307208 | tf_op jit(solution)/shard_map/ppermute | solution.py:488
  58.4 5.3 %collective-permute-start.11 = (bf16[400,128]{1,0:T(8,128)(2,1)S(1)}, bf16[400,128]{1,0:T(8,128)(2,1)S(1)}, u32[]{:S(2)}, u32[]{:S(2)}) collective-permute-start(bf16[400,128]{1,0:T(8,128)(2,1)S(1)} %add_convert_fusion.2), channel_id=1, source_target_pairs={{0,8},{1,17},{2,10},{3,19},{4,12},{5,21},{6,14},{7,23},{8,0},{9,25... | collective-permute-start | bytes 307208 | tf_op jit(solution)/shard_map/ppermute | solution.py:488
  62.3 1.5 %collective-permute-start.12 = (bf16[800,128]{1,0:T(8,128)(2,1)S(1)}, bf16[800,128]{1,0:T(8,128)(2,1)S(1)}, u32[]{:S(2)}, u32[]{:S(2)}) collective-permute-start(bf16[800,128]{1,0:T(8,128)(2,1)S(1)} %maximum_select_fusion.mine_a), channel_id=1, source_target_pairs={{0,1},{1,0},{2,3},{3,2},{4,5},{5,4},{6,7},{7,6},{8,9},{9,8},{10,11... | collective-permute-start | bytes 614408 | tf_op jit(solution)/shard_map/ppermute | solution.py:488
  63.8 1.5 %collective-permute-start.13 = (bf16[800,128]{1,0:T(8,128)(2,1)S(1)}, bf16[800,128]{1,0:T(8,128)(2,1)S(1)}, u32[]{:S(2)}, u32[]{:S(2)}) collective-permute-start(bf16[800,128]{1,0:T(8,128)(2,1)S(1)} %maximum_select_fusion.1.mine_b), channel_id=1, source_target_pairs={{0,1},{1,0},{2,3},{3,2},{4,5},{5,4},{6,7},{7,6},{8,9},{9,8},{10,11... | collective-permute-start | bytes 614408 | tf_op jit(solution)/shard_map/ppermute | solution.py:488

commit v5 on v4

--- a/solution.py
+++ b/solution.py
@@ -492,34 +492,34 @@
     return (a.astype(f32) + b.astype(f32)).astype(bf16)
 
 
+def picked(pieces, at):
+    first, low = (at // 2) % 2 == 0, at % 2 == 0
+    return jnp.where(first, jnp.where(low, pieces[0], pieces[1]), jnp.where(low, pieces[2], pieces[3]))
+
+
 def all_sum(mine, other, index, devices):
+    parts = [added(m, exchange(o, (1, 1), devices)) for m, o in zip(mine, other)]
+    half = parts[0].shape[0] // 2
+    quarters = [parts[0][:half], parts[0][half:], parts[1][:half], parts[1][half:]]
     bits = [1 << i for i in range(1, devices.bit_length() - 1)]
-    crossed = list(bits)
-    for i in range(0, len(bits) - 1, 2):
-        crossed[i], crossed[i + 1] = bits[i + 1], bits[i]
-    steps = list(zip(bits, crossed))
-    order = []
-    for i in range(0, len(steps), 4):
-        some = steps[i:i + 4]
-        order += some[0::2] + some[1::2]
-    turned = list(order)
-    for i in range(0, len(order) - 1, 2):
-        turned[i], turned[i + 1] = order[i + 1], order[i]
-    orders = [order, turned]
-    parts = [added(m, exchange(o, (1, 1), devices)) for m, o in zip(mine, other)]
-    lows = [(index // jnp.where(index % 2 == 0, order[0][0], order[0][1])) % 2 == 0 for order in orders]
-    half = parts[0].shape[0] // 2
-    kept = [jnp.where(low, p[:half], p[half:]) for p, low in zip(parts, lows)]
-    sent = [jnp.where(low, p[half:], p[:half]) for p, low in zip(parts, lows)]
-    for step in range(len(steps)):
-        got = [exchange(p, order[step], devices) for p, order in zip(sent, orders)]
-        kept = [added(p, q) for p, q in zip(kept, got)]
-        sent = kept
-    got = [exchange(p, order[0], devices) for p, order in zip(kept, orders)]
-    parts = [
-        jnp.where(low, jnp.concatenate([p, q]), jnp.concatenate([q, p]))
-        for p, q, low in zip(kept, got, lows)
-    ]
+    rest = bits[2:]
+    crossed = list(rest)
+    for i in range(0, len(rest) - 1, 2):
+        crossed[i], crossed[i + 1] = rest[i + 1], rest[i]
+    turns = {m: m * bits[0] for m in (1, 2, 3)}
+    place = (index // bits[0]) % 4
+    got = [exchange(picked(quarters, place ^ m), (bit, bit), devices) for m, bit in turns.items()]
+    total = picked(quarters, place).astype(f32)
+    for piece in got:
+        total = total + piece.astype(f32)
+    total = total.astype(bf16)
+    for step in zip(rest, crossed):
+        total = added(total, exchange(total, step, devices))
+    have = {0: total}
+    for m, bit in turns.items():
+        have[m] = exchange(total, (bit, bit), devices)
+    pieces = [have[m] for m in range(4)]
+    parts = [jnp.concatenate([picked(pieces, place ^ j), picked(pieces, place ^ (j + 1))]) for j in (0, 2)]
     return parts, [exchange(p, (1, 1), devices) for p in parts]
 
 

time: 66.8 us -> 65.7 us (0.984)
  starting transfers between devices: 19.4 us -> 13.6 us
  waiting for transfers between devices: 12.9 us -> 18.2 us
  other arithmetic: 1.46 us -> 0.41 us
    ppermute x14 -> x12, starting transfers between devices: 19.4 us -> 13.6 us  [exchange(): return lax.ppermute(x, AXES, [(i, i ^ bits[i % 2]) for i in range(devices)])]
    ppermute x14 -> x12, waiting for transfers between devices: 12.9 us -> 18.2 us  [exchange(): return lax.ppermute(x, AXES, [(i, i ^ bits[i % 2]) for i in range(devices)])]
    convert_element_type x10 -> x4, other arithmetic: 1.32 us -> 0.17 us  [added(): return (a.astype(f32) + b.astype(f32)).astype(bf16)]
  transfers between devices with their start and end apart: 14 -> 12, of which waited for: 12 -> 12; matrix products, arithmetic and copies ran while one was open for 2% -> 0% of each run, Pallas kernels for 0% -> 0%
where the time goes in v5:
time: 65.7 us; the launch traced here: 65.5 us
  Pallas kernels  32 us (49%)
  waiting for transfers between devices  18.2 us (28%)
  starting transfers between devices  13.6 us (21%)
  between operations  0.75 us (1%)
    pallas_call x1, Pallas kernels, main_call(): pl.pallas_call(functools.partial(main_kernel, steps_top=steps_top), out_s...  30.7 us
    ppermute x12, waiting for transfers between devices, exchange(): return lax.ppermute(x, AXES, [(i, i ^ bits[i % 2]) for i in range(devices)])  18.2 us
    ppermute x12, starting transfers between devices, exchange(): return lax.ppermute(x, AXES, [(i, i ^ bits[i % 2]) for i in range(devices)])  13.6 us
  transfers between devices with their start and end apart: 12, of which 12 were waited for; matrix products, arithmetic and copies ran while one was open for 0% of the time, Pallas kernels for 0%

profile of v5, /device:TPU:0, one launch (start us, length us, event | category | flops | bytes accessed | tf_op | source)
XLA Modules:
  0.0 65.5 jit_solution(16539429499579964952)
XLA Ops:
  0.7 30.7 %layers.1 = (bf16[32,96,128]{2,1,0:T(8,128)(2,1)}, bf16[32,96,128]{2,1,0:T(8,128)(2,1)}, bf16[800,128]{1,0:T(8,128)(2,1)}, bf16[800,128]{1,0:T(8,128)(2,1)}, bf1...) custom-call(s32[32]{0:T(128)} %lengths.1, s32[1]{0:T(128)} %bitcast.parity, bf16[32,96,128]{2,1,0:T(8,128)(2,1)} %tok_hbm.1, ...), custom_call_target="tpu_custom_call" | custom-call | tf_op jit(solution)/shard_map/layers/pallas_call | solution.py:389
  31.4 0.0 copy-start.1
  31.4 0.5 collective-permute-start
  31.9 0.1 collective-permute-start.1
  32.0 1.2 %collective-permute-done = bf16[800,128]{1,0:T(8,128)(2,1)S(1)} collective-permute-done((bf16[800,128]{1,0:T(8,128)(2,1)}, bf16[800,128]{1,0:T(8,128)(2,1)S(1)}, u32[]{:S(2)}, u32[]{:S(2)}) %collective-permute-start) | collective-permute-done | bytes 204832 | tf_op jit(solution)/shard_map/ppermute | solution.py:488
  33.2 0.0 copy-done.1
  33.2 0.0 copy-start
  33.2 0.1 add_convert_fusion.1
  33.3 0.3 collective-permute-done.1
  33.6 0.6 copy-done
  34.2 0.1 add_convert_fusion
  34.3 3.0 %collective-permute-start.2 = (bf16[400,128]{1,0:T(8,128)(2,1)S(1)}, bf16[400,128]{1,0:T(8,128)(2,1)S(1)}, u32[]{:S(2)}, u32[]{:S(2)}) collective-permute-start(bf16[400,128]{1,0:T(8,128)(2,1)S(1)} %get-tuple-element.45), channel_id=1, source_target_pairs={{0,2},{1,3},{2,0},{3,1},{4,6},{5,7},{6,4},{7,5},{8,10},{9,11},{10,... | collective-permute-start | bytes 307208 | tf_op jit(solution)/shard_map/ppermute | solution.py:488
  37.2 1.5 %collective-permute-start.3 = (bf16[400,128]{1,0:T(8,128)(2,1)S(1)}, bf16[400,128]{1,0:T(8,128)(2,1)S(1)}, u32[]{:S(2)}, u32[]{:S(2)}) collective-permute-start(bf16[400,128]{1,0:T(8,128)(2,1)S(1)} %get-tuple-element.46), channel_id=1, source_target_pairs={{0,4},{1,5},{2,6},{3,7},{4,0},{5,1},{6,2},{7,3},{8,12},{9,13},{10,... | collective-permute-start | bytes 307208 | tf_op jit(solution)/shard_map/ppermute | solution.py:488
  38.7 0.1 collective-permute-start.4
  38.8 1.6 %collective-permute-done.2 = bf16[400,128]{1,0:T(8,128)(2,1)S(1)} collective-permute-done((bf16[400,128]{1,0:T(8,128)(2,1)S(1)}, bf16[400,128]{1,0:T(8,128)(2,1)S(1)}, u32[]{:S(2)}, u32[]{:S(2)}) %collective-permute-start.2) | collective-permute-done | bytes 102432 | tf_op jit(solution)/shard_map/ppermute | solution.py:488
  40.4 2.5 %collective-permute-done.3 = bf16[400,128]{1,0:T(8,128)(2,1)S(1)} collective-permute-done((bf16[400,128]{1,0:T(8,128)(2,1)S(1)}, bf16[400,128]{1,0:T(8,128)(2,1)S(1)}, u32[]{:S(2)}, u32[]{:S(2)}) %collective-permute-start.3) | collective-permute-done | bytes 102432 | tf_op jit(solution)/shard_map/ppermute | solution.py:488
  43.0 1.3 %collective-permute-done.4 = bf16[400,128]{1,0:T(8,128)(2,1)S(1)} collective-permute-done((bf16[400,128]{1,0:T(8,128)(2,1)S(1)}, bf16[400,128]{1,0:T(8,128)(2,1)S(1)}, u32[]{:S(2)}, u32[]{:S(2)}) %collective-permute-start.4) | collective-permute-done | bytes 102432 | tf_op jit(solution)/shard_map/ppermute | solution.py:488
  44.3 0.1 add_convert_fusion.4
  44.4 1.6 %collective-permute-start.5 = (bf16[400,128]{1,0:T(8,128)(2,1)S(1)}, bf16[400,128]{1,0:T(8,128)(2,1)S(1)}, u32[]{:S(2)}, u32[]{:S(2)}) collective-permute-start(bf16[400,128]{1,0:T(8,128)(2,1)S(1)} %add_convert_fusion.4), channel_id=1, source_target_pairs={{0,8},{1,17},{2,10},{3,19},{4,12},{5,21},{6,14},{7,23},{8,0},{9,25... | collective-permute-start | bytes 307208 | tf_op jit(solution)/shard_map/ppermute | solution.py:488
  46.0 3.1 %collective-permute-done.5 = bf16[400,128]{1,0:T(8,128)(2,1)S(1)} collective-permute-done((bf16[400,128]{1,0:T(8,128)(2,1)S(1)}, bf16[400,128]{1,0:T(8,128)(2,1)S(1)}, u32[]{:S(2)}, u32[]{:S(2)}) %collective-permute-start.5) | collective-permute-done | bytes 102432 | tf_op jit(solution)/shard_map/ppermute | solution.py:488
  49.1 2.7 %collective-permute-start.6 = (bf16[400,128]{1,0:T(8,128)(2,1)S(1)}, bf16[400,128]{1,0:T(8,128)(2,1)S(1)}, u32[]{:S(2)}, u32[]{:S(2)}) collective-permute-start(bf16[400,128]{1,0:T(8,128)(2,1)S(1)} %add_convert_fusion.3), channel_id=1, source_target_pairs={{0,16},{1,9},{2,18},{3,11},{4,20},{5,13},{6,22},{7,15},{8,24},{9,1... | collective-permute-start | bytes 307208 | tf_op jit(solution)/shard_map/ppermute | solution.py:488
  51.8 3.0 %collective-permute-done.6 = bf16[400,128]{1,0:T(8,128)(2,1)S(1)} collective-permute-done((bf16[400,128]{1,0:T(8,128)(2,1)S(1)}, bf16[400,128]{1,0:T(8,128)(2,1)S(1)}, u32[]{:S(2)}, u32[]{:S(2)}) %collective-permute-start.6) | collective-permute-done | bytes 102432 | tf_op jit(solution)/shard_map/ppermute | solution.py:488
  54.8 2.2 %collective-permute-start.9 = (bf16[400,128]{1,0:T(8,128)(2,1)S(1)}, bf16[400,128]{1,0:T(8,128)(2,1)S(1)}, u32[]{:S(2)}, u32[]{:S(2)}) collective-permute-start(bf16[400,128]{1,0:T(8,128)(2,1)S(1)} %add_convert_fusion.2), channel_id=1, source_target_pairs={{0,6},{1,7},{2,4},{3,5},{4,2},{5,3},{6,0},{7,1},{8,14},{9,15},{10,... | collective-permute-start | bytes 307208 | tf_op jit(solution)/shard_map/ppermute | solution.py:488
  57.0 0.6 collective-permute-start.8
  57.7 0.7 %collective-permute-start.7 = (bf16[400,128]{1,0:T(8,128)(2,1)S(1)}, bf16[400,128]{1,0:T(8,128)(2,1)S(1)}, u32[]{:S(2)}, u32[]{:S(2)}) collective-permute-start(bf16[400,128]{1,0:T(8,128)(2,1)S(1)} %add_convert_fusion.2), channel_id=1, source_target_pairs={{0,2},{1,3},{2,0},{3,1},{4,6},{5,7},{6,4},{7,5},{8,10},{9,11},{10,... | collective-permute-start | bytes 307208 | tf_op jit(solution)/shard_map/ppermute | solution.py:488
  58.4 2.1 %collective-permute-done.9 = bf16[400,128]{1,0:T(8,128)(2,1)S(1)} collective-permute-done((bf16[400,128]{1,0:T(8,128)(2,1)S(1)}, bf16[400,128]{1,0:T(8,128)(2,1)S(1)}, u32[]{:S(2)}, u32[]{:S(2)}) %collective-permute-start.9) | collective-permute-done | bytes 102432 | tf_op jit(solution)/shard_map/ppermute | solution.py:488
  60.4 1.3 %collective-permute-done.8 = bf16[400,128]{1,0:T(8,128)(2,1)S(1)} collective-permute-done((bf16[400,128]{1,0:T(8,128)(2,1)S(1)}, bf16[400,128]{1,0:T(8,128)(2,1)S(1)}, u32[]{:S(2)}, u32[]{:S(2)}) %collective-permute-start.8) | collective-permute-done | bytes 102432 | tf_op jit(solution)/shard_map/ppermute | solution.py:488
  61.7 0.6 collective-permute-done.7
  62.3 0.1 select_select_fusion.1
  62.4 0.1 collective-permute-start.10
  62.5 0.6 collective-permute-start.11
  63.1 0.9 %collective-permute-done.10.other_a = bf16[800,128]{1,0:T(8,128)(2,1)S(1)} collective-permute-done((bf16[800,128]{1,0:T(8,128)(2,1)S(1)}, bf16[800,128]{1,0:T(8,128)(2,1)S(1)}, u32[]{:S(2)}, u32[]{:S(2)}) %collective-permute-start.10) | collective-permute-done | bytes 204832 | tf_op jit(solution)/shard_map/ppermute | solution.py:488
  63.9 0.3 collective-permute-done.11.other_b
  64.2 1.3 %finish.1 = (f32[2,2,128]{2,1,0:T(2,128)}, f32[2,2,128]{2,1,0:T(2,128)}, f32[2,128,384]{2,1,0:T(8,128)}, f32[2,2,128]{2,1,0:T(2,128)}, f32[2,128,128]{2,1,0:T(8,...) custom-call(s32[1]{0:T(128)} %bitcast.parity, ...), custom_call_target="tpu_custom_call" | custom-call | tf_op jit(solution)/shard_map/finish/pallas_call | solution.py:477
  (5 shorter events, 0.1 us)
Async XLA Ops:
  31.4 1.8 %copy-start.1 = (bf16[800,128]{1,0:T(8,128)(2,1)S(1)}, bf16[800,128]{1,0:T(8,128)(2,1)}, u32[]{:S(2)}) copy-start(bf16[800,128]{1,0:T(8,128)(2,1)} %get-tuple-element.28) | copy-start | bytes 614404
  31.4 1.8 %collective-permute-start = (bf16[800,128]{1,0:T(8,128)(2,1)}, bf16[800,128]{1,0:T(8,128)(2,1)S(1)}, u32[]{:S(2)}, u32[]{:S(2)}) collective-permute-start(bf16[800,128]{1,0:T(8,128)(2,1)} %get-tuple-element.29), channel_id=1, source_target_pairs={{0,1},{1,0},{2,3},{3,2},{4,5},{5,4},{6,7},{7,6},{8,9},{9,8},{10,11... | collective-permute-start | bytes 614408 | tf_op jit(solution)/shard_map/ppermute | solution.py:488
  31.9 1.7 %collective-permute-start.1 = (bf16[800,128]{1,0:T(8,128)(2,1)}, bf16[800,128]{1,0:T(8,128)(2,1)S(1)}, u32[]{:S(2)}, u32[]{:S(2)}) collective-permute-start(bf16[800,128]{1,0:T(8,128)(2,1)} %get-tuple-element.31), channel_id=1, source_target_pairs={{0,1},{1,0},{2,3},{3,2},{4,5},{5,4},{6,7},{7,6},{8,9},{9,8},{10,11... | collective-permute-start | bytes 614408 | tf_op jit(solution)/shard_map/ppermute | solution.py:488
  33.2 0.9 %copy-start = (bf16[800,128]{1,0:T(8,128)(2,1)S(1)}, bf16[800,128]{1,0:T(8,128)(2,1)}, u32[]{:S(2)}) copy-start(bf16[800,128]{1,0:T(8,128)(2,1)} %get-tuple-element.30) | copy-start | bytes 614404
  34.3 6.1 %collective-permute-start.2 = (bf16[400,128]{1,0:T(8,128)(2,1)S(1)}, bf16[400,128]{1,0:T(8,128)(2,1)S(1)}, u32[]{:S(2)}, u32[]{:S(2)}) collective-permute-start(bf16[400,128]{1,0:T(8,128)(2,1)S(1)} %get-tuple-element.45), channel_id=1, source_target_pairs={{0,2},{1,3},{2,0},{3,1},{4,6},{5,7},{6,4},{7,5},{8,10},{9,11},{10,... | collective-permute-start | bytes 307208 | tf_op jit(solution)/shard_map/ppermute | solution.py:488
  37.2 5.7 %collective-permute-start.3 = (bf16[400,128]{1,0:T(8,128)(2,1)S(1)}, bf16[400,128]{1,0:T(8,128)(2,1)S(1)}, u32[]{:S(2)}, u32[]{:S(2)}) collective-permute-start(bf16[400,128]{1,0:T(8,128)(2,1)S(1)} %get-tuple-element.46), channel_id=1, source_target_pairs={{0,4},{1,5},{2,6},{3,7},{4,0},{5,1},{6,2},{7,3},{8,12},{9,13},{10,... | collective-permute-start | bytes 307208 | tf_op jit(solution)/shard_map/ppermute | solution.py:488
  38.7 5.6 %collective-permute-start.4 = (bf16[400,128]{1,0:T(8,128)(2,1)S(1)}, bf16[400,128]{1,0:T(8,128)(2,1)S(1)}, u32[]{:S(2)}, u32[]{:S(2)}) collective-permute-start(bf16[400,128]{1,0:T(8,128)(2,1)S(1)} %get-tuple-element.47), channel_id=1, source_target_pairs={{0,6},{1,7},{2,4},{3,5},{4,2},{5,3},{6,0},{7,1},{8,14},{9,15},{10,... | collective-permute-start | bytes 307208 | tf_op jit(solution)/shard_map/ppermute | solution.py:488
  44.4 4.7 %collective-permute-start.5 = (bf16[400,128]{1,0:T(8,128)(2,1)S(1)}, bf16[400,128]{1,0:T(8,128)(2,1)S(1)}, u32[]{:S(2)}, u32[]{:S(2)}) collective-permute-start(bf16[400,128]{1,0:T(8,128)(2,1)S(1)} %add_convert_fusion.4), channel_id=1, source_target_pairs={{0,8},{1,17},{2,10},{3,19},{4,12},{5,21},{6,14},{7,23},{8,0},{9,25... | collective-permute-start | bytes 307208 | tf_op jit(solution)/shard_map/ppermute | solution.py:488
  49.1 5.6 %collective-permute-start.6 = (bf16[400,128]{1,0:T(8,128)(2,1)S(1)}, bf16[400,128]{1,0:T(8,128)(2,1)S(1)}, u32[]{:S(2)}, u32[]{:S(2)}) collective-permute-start(bf16[400,128]{1,0:T(8,128)(2,1)S(1)} %add_convert_fusion.3), channel_id=1, source_target_pairs={{0,16},{1,9},{2,18},{3,11},{4,20},{5,13},{6,22},{7,15},{8,24},{9,1... | collective-permute-start | bytes 307208 | tf_op jit(solution)/shard_map/ppermute | solution.py:488
  54.8 5.6 %collective-permute-start.9 = (bf16[400,128]{1,0:T(8,128)(2,1)S(1)}, bf16[400,128]{1,0:T(8,128)(2,1)S(1)}, u32[]{:S(2)}, u32[]{:S(2)}) collective-permute-start(bf16[400,128]{1,0:T(8,128)(2,1)S(1)} %add_convert_fusion.2), channel_id=1, source_target_pairs={{0,6},{1,7},{2,4},{3,5},{4,2},{5,3},{6,0},{7,1},{8,14},{9,15},{10,... | collective-permute-start | bytes 307208 | tf_op jit(solution)/shard_map/ppermute | solution.py:488
  57.0 4.7 %collective-permute-start.8 = (bf16[400,128]{1,0:T(8,128)(2,1)S(1)}, bf16[400,128]{1,0:T(8,128)(2,1)S(1)}, u32[]{:S(2)}, u32[]{:S(2)}) collective-permute-start(bf16[400,128]{1,0:T(8,128)(2,1)S(1)} %add_convert_fusion.2), channel_id=1, source_target_pairs={{0,4},{1,5},{2,6},{3,7},{4,0},{5,1},{6,2},{7,3},{8,12},{9,13},{10,... | collective-permute-start | bytes 307208 | tf_op jit(solution)/shard_map/ppermute | solution.py:488
  57.7 4.7 %collective-permute-start.7 = (bf16[400,128]{1,0:T(8,128)(2,1)S(1)}, bf16[400,128]{1,0:T(8,128)(2,1)S(1)}, u32[]{:S(2)}, u32[]{:S(2)}) collective-permute-start(bf16[400,128]{1,0:T(8,128)(2,1)S(1)} %add_convert_fusion.2), channel_id=1, source_target_pairs={{0,2},{1,3},{2,0},{3,1},{4,6},{5,7},{6,4},{7,5},{8,10},{9,11},{10,... | collective-permute-start | bytes 307208 | tf_op jit(solution)/shard_map/ppermute | solution.py:488
  62.4 1.5 %collective-permute-start.10 = (bf16[800,128]{1,0:T(8,128)(2,1)S(1)}, bf16[800,128]{1,0:T(8,128)(2,1)S(1)}, u32[]{:S(2)}, u32[]{:S(2)}) collective-permute-start(bf16[800,128]{1,0:T(8,128)(2,1)S(1)} %pad_maximum_fusion.mine_a), channel_id=1, source_target_pairs={{0,1},{1,0},{2,3},{3,2},{4,5},{5,4},{6,7},{7,6},{8,9},{9,8},{10,11... | collective-permute-start | bytes 614408 | tf_op jit(solution)/shard_map/ppermute | solution.py:488
  62.5 1.7 %collective-permute-start.11 = (bf16[800,128]{1,0:T(8,128)(2,1)S(1)}, bf16[800,128]{1,0:T(8,128)(2,1)S(1)}, u32[]{:S(2)}, u32[]{:S(2)}) collective-permute-start(bf16[800,128]{1,0:T(8,128)(2,1)S(1)} %pad_maximum_fusion.1.mine_b), channel_id=1, source_target_pairs={{0,1},{1,0},{2,3},{3,2},{4,5},{5,4},{6,7},{7,6},{8,9},{9,8},{10,11... | collective-permute-start | bytes 614408 | tf_op jit(solution)/shard_map/ppermute | solution.py:488

commit v6 on v5

--- a/solution.py
+++ b/solution.py
@@ -10,7 +10,7 @@
 HEAD = 16
 LAYERS = 2
 BIN = 128
-SMALL = 64
+SMALL = 32
 FWD_GROUP = 1
 BWD_GROUP = 4
 MEMBERS = 2

time: 65.7 us -> 65.7 us (level)
  no operation moved by 1% of the time
where the time goes in v6:
time: 65.7 us; the launch traced here: 65.5 us
  Pallas kernels  32 us (49%)
  waiting for transfers between devices  18.1 us (28%)
  starting transfers between devices  13.6 us (21%)
  between operations  0.74 us (1%)
    pallas_call x1, Pallas kernels, main_call(): pl.pallas_call(functools.partial(main_kernel, steps_top=steps_top), out_s...  30.7 us
    ppermute x12, waiting for transfers between devices, exchange(): return lax.ppermute(x, AXES, [(i, i ^ bits[i % 2]) for i in range(devices)])  18.1 us
    ppermute x12, starting transfers between devices, exchange(): return lax.ppermute(x, AXES, [(i, i ^ bits[i % 2]) for i in range(devices)])  13.6 us
  transfers between devices with their start and end apart: 12, of which 12 were waited for; matrix products, arithmetic and copies ran while one was open for 0% of the time, Pallas kernels for 0%

profile of v6, /device:TPU:0, one launch (start us, length us, event | category | flops | bytes accessed | tf_op | source)
XLA Modules:
  0.0 65.5 jit_solution(4518329879551804800)
XLA Ops:
  0.7 30.7 %layers.1 = (bf16[32,96,128]{2,1,0:T(8,128)(2,1)}, bf16[32,96,128]{2,1,0:T(8,128)(2,1)}, bf16[784,128]{1,0:T(8,128)(2,1)}, bf16[784,128]{1,0:T(8,128)(2,1)}, bf1...) custom-call(s32[32]{0:T(128)} %lengths.1, s32[1]{0:T(128)} %bitcast.parity, bf16[32,96,128]{2,1,0:T(8,128)(2,1)} %tok_hbm.1, ...), custom_call_target="tpu_custom_call" | custom-call | tf_op jit(solution)/shard_map/layers/pallas_call | solution.py:389
  31.4 0.0 copy-start.1
  31.4 0.5 collective-permute-start
  31.9 0.1 collective-permute-start.1
  32.0 1.2 %collective-permute-done = bf16[784,128]{1,0:T(8,128)(2,1)S(1)} collective-permute-done((bf16[784,128]{1,0:T(8,128)(2,1)}, bf16[784,128]{1,0:T(8,128)(2,1)S(1)}, u32[]{:S(2)}, u32[]{:S(2)}) %collective-permute-start) | collective-permute-done | bytes 200736 | tf_op jit(solution)/shard_map/ppermute | solution.py:488
  33.2 0.0 copy-done.1
  33.2 0.0 copy-start
  33.2 0.1 add_convert_fusion.1
  33.3 0.3 collective-permute-done.1
  33.6 0.6 copy-done
  34.2 0.1 add_convert_fusion
  34.2 0.1 select_select_fusion.6
  34.3 2.9 %collective-permute-start.2 = (bf16[392,128]{1,0:T(8,128)(2,1)S(1)}, bf16[392,128]{1,0:T(8,128)(2,1)S(1)}, u32[]{:S(2)}, u32[]{:S(2)}) collective-permute-start(bf16[392,128]{1,0:T(8,128)(2,1)S(1)} %get-tuple-element.45), channel_id=1, source_target_pairs={{0,2},{1,3},{2,0},{3,1},{4,6},{5,7},{6,4},{7,5},{8,10},{9,11},{10,... | collective-permute-start | bytes 301064 | tf_op jit(solution)/shard_map/ppermute | solution.py:488
  37.3 1.5 %collective-permute-start.3 = (bf16[392,128]{1,0:T(8,128)(2,1)S(1)}, bf16[392,128]{1,0:T(8,128)(2,1)S(1)}, u32[]{:S(2)}, u32[]{:S(2)}) collective-permute-start(bf16[392,128]{1,0:T(8,128)(2,1)S(1)} %get-tuple-element.46), channel_id=1, source_target_pairs={{0,4},{1,5},{2,6},{3,7},{4,0},{5,1},{6,2},{7,3},{8,12},{9,13},{10,... | collective-permute-start | bytes 301064 | tf_op jit(solution)/shard_map/ppermute | solution.py:488
  38.8 0.1 collective-permute-start.4
  38.8 1.6 %collective-permute-done.2 = bf16[392,128]{1,0:T(8,128)(2,1)S(1)} collective-permute-done((bf16[392,128]{1,0:T(8,128)(2,1)S(1)}, bf16[392,128]{1,0:T(8,128)(2,1)S(1)}, u32[]{:S(2)}, u32[]{:S(2)}) %collective-permute-start.2) | collective-permute-done | bytes 100384 | tf_op jit(solution)/shard_map/ppermute | solution.py:488
  40.4 2.5 %collective-permute-done.3 = bf16[392,128]{1,0:T(8,128)(2,1)S(1)} collective-permute-done((bf16[392,128]{1,0:T(8,128)(2,1)S(1)}, bf16[392,128]{1,0:T(8,128)(2,1)S(1)}, u32[]{:S(2)}, u32[]{:S(2)}) %collective-permute-start.3) | collective-permute-done | bytes 100384 | tf_op jit(solution)/shard_map/ppermute | solution.py:488
  43.0 1.4 %collective-permute-done.4 = bf16[392,128]{1,0:T(8,128)(2,1)S(1)} collective-permute-done((bf16[392,128]{1,0:T(8,128)(2,1)S(1)}, bf16[392,128]{1,0:T(8,128)(2,1)S(1)}, u32[]{:S(2)}, u32[]{:S(2)}) %collective-permute-start.4) | collective-permute-done | bytes 100384 | tf_op jit(solution)/shard_map/ppermute | solution.py:488
  44.3 0.1 add_convert_fusion.4
  44.4 1.6 %collective-permute-start.5 = (bf16[392,128]{1,0:T(8,128)(2,1)S(1)}, bf16[392,128]{1,0:T(8,128)(2,1)S(1)}, u32[]{:S(2)}, u32[]{:S(2)}) collective-permute-start(bf16[392,128]{1,0:T(8,128)(2,1)S(1)} %add_convert_fusion.4), channel_id=1, source_target_pairs={{0,8},{1,17},{2,10},{3,19},{4,12},{5,21},{6,14},{7,23},{8,0},{9,25... | collective-permute-start | bytes 301064 | tf_op jit(solution)/shard_map/ppermute | solution.py:488
  46.1 3.1 %collective-permute-done.5 = bf16[392,128]{1,0:T(8,128)(2,1)S(1)} collective-permute-done((bf16[392,128]{1,0:T(8,128)(2,1)S(1)}, bf16[392,128]{1,0:T(8,128)(2,1)S(1)}, u32[]{:S(2)}, u32[]{:S(2)}) %collective-permute-start.5) | collective-permute-done | bytes 100384 | tf_op jit(solution)/shard_map/ppermute | solution.py:488
  49.1 2.6 %collective-permute-start.6 = (bf16[392,128]{1,0:T(8,128)(2,1)S(1)}, bf16[392,128]{1,0:T(8,128)(2,1)S(1)}, u32[]{:S(2)}, u32[]{:S(2)}) collective-permute-start(bf16[392,128]{1,0:T(8,128)(2,1)S(1)} %add_convert_fusion.3), channel_id=1, source_target_pairs={{0,16},{1,9},{2,18},{3,11},{4,20},{5,13},{6,22},{7,15},{8,24},{9,1... | collective-permute-start | bytes 301064 | tf_op jit(solution)/shard_map/ppermute | solution.py:488
  51.8 3.0 %collective-permute-done.6 = bf16[392,128]{1,0:T(8,128)(2,1)S(1)} collective-permute-done((bf16[392,128]{1,0:T(8,128)(2,1)S(1)}, bf16[392,128]{1,0:T(8,128)(2,1)S(1)}, u32[]{:S(2)}, u32[]{:S(2)}) %collective-permute-start.6) | collective-permute-done | bytes 100384 | tf_op jit(solution)/shard_map/ppermute | solution.py:488
  54.8 2.2 %collective-permute-start.9 = (bf16[392,128]{1,0:T(8,128)(2,1)S(1)}, bf16[392,128]{1,0:T(8,128)(2,1)S(1)}, u32[]{:S(2)}, u32[]{:S(2)}) collective-permute-start(bf16[392,128]{1,0:T(8,128)(2,1)S(1)} %add_convert_fusion.2), channel_id=1, source_target_pairs={{0,6},{1,7},{2,4},{3,5},{4,2},{5,3},{6,0},{7,1},{8,14},{9,15},{10,... | collective-permute-start | bytes 301064 | tf_op jit(solution)/shard_map/ppermute | solution.py:488
  57.0 0.7 %collective-permute-start.8 = (bf16[392,128]{1,0:T(8,128)(2,1)S(1)}, bf16[392,128]{1,0:T(8,128)(2,1)S(1)}, u32[]{:S(2)}, u32[]{:S(2)}) collective-permute-start(bf16[392,128]{1,0:T(8,128)(2,1)S(1)} %add_convert_fusion.2), channel_id=1, source_target_pairs={{0,4},{1,5},{2,6},{3,7},{4,0},{5,1},{6,2},{7,3},{8,12},{9,13},{10,... | collective-permute-start | bytes 301064 | tf_op jit(solution)/shard_map/ppermute | solution.py:488
  57.6 0.7 %collective-permute-start.7 = (bf16[392,128]{1,0:T(8,128)(2,1)S(1)}, bf16[392,128]{1,0:T(8,128)(2,1)S(1)}, u32[]{:S(2)}, u32[]{:S(2)}) collective-permute-start(bf16[392,128]{1,0:T(8,128)(2,1)S(1)} %add_convert_fusion.2), channel_id=1, source_target_pairs={{0,2},{1,3},{2,0},{3,1},{4,6},{5,7},{6,4},{7,5},{8,10},{9,11},{10,... | collective-permute-start | bytes 301064 | tf_op jit(solution)/shard_map/ppermute | solution.py:488
  58.3 2.0 %collective-permute-done.9 = bf16[392,128]{1,0:T(8,128)(2,1)S(1)} collective-permute-done((bf16[392,128]{1,0:T(8,128)(2,1)S(1)}, bf16[392,128]{1,0:T(8,128)(2,1)S(1)}, u32[]{:S(2)}, u32[]{:S(2)}) %collective-permute-start.9) | collective-permute-done | bytes 100384 | tf_op jit(solution)/shard_map/ppermute | solution.py:488
  60.4 1.2 %collective-permute-done.8 = bf16[392,128]{1,0:T(8,128)(2,1)S(1)} collective-permute-done((bf16[392,128]{1,0:T(8,128)(2,1)S(1)}, bf16[392,128]{1,0:T(8,128)(2,1)S(1)}, u32[]{:S(2)}, u32[]{:S(2)}) %collective-permute-start.8) | collective-permute-done | bytes 100384 | tf_op jit(solution)/shard_map/ppermute | solution.py:488
  61.6 0.7 %collective-permute-done.7 = bf16[392,128]{1,0:T(8,128)(2,1)S(1)} collective-permute-done((bf16[392,128]{1,0:T(8,128)(2,1)S(1)}, bf16[392,128]{1,0:T(8,128)(2,1)S(1)}, u32[]{:S(2)}, u32[]{:S(2)}) %collective-permute-start.7) | collective-permute-done | bytes 100384 | tf_op jit(solution)/shard_map/ppermute | solution.py:488
  62.3 0.1 select_select_fusion.1
  62.4 0.1 collective-permute-start.10
  62.5 0.6 collective-permute-start.11
  63.1 0.9 %collective-permute-done.10.other_a = bf16[784,128]{1,0:T(8,128)(2,1)S(1)} collective-permute-done((bf16[784,128]{1,0:T(8,128)(2,1)S(1)}, bf16[784,128]{1,0:T(8,128)(2,1)S(1)}, u32[]{:S(2)}, u32[]{:S(2)}) %collective-permute-start.10) | collective-permute-done | bytes 200736 | tf_op jit(solution)/shard_map/ppermute | solution.py:488
  63.9 0.3 collective-permute-done.11.other_b
  64.2 1.3 %finish.1 = (f32[2,2,128]{2,1,0:T(2,128)}, f32[2,2,128]{2,1,0:T(2,128)}, f32[2,128,384]{2,1,0:T(8,128)}, f32[2,2,128]{2,1,0:T(2,128)}, f32[2,128,128]{2,1,0:T(8,...) custom-call(s32[1]{0:T(128)} %bitcast.parity, ...), custom_call_target="tpu_custom_call" | custom-call | tf_op jit(solution)/shard_map/finish/pallas_call | solution.py:477
  (4 shorter events, 0.1 us)
Async XLA Ops:
  31.4 1.8 %copy-start.1 = (bf16[784,128]{1,0:T(8,128)(2,1)S(1)}, bf16[784,128]{1,0:T(8,128)(2,1)}, u32[]{:S(2)}) copy-start(bf16[784,128]{1,0:T(8,128)(2,1)} %get-tuple-element.28) | copy-start | bytes 602116
  31.4 1.8 %collective-permute-start = (bf16[784,128]{1,0:T(8,128)(2,1)}, bf16[784,128]{1,0:T(8,128)(2,1)S(1)}, u32[]{:S(2)}, u32[]{:S(2)}) collective-permute-start(bf16[784,128]{1,0:T(8,128)(2,1)} %get-tuple-element.29), channel_id=1, source_target_pairs={{0,1},{1,0},{2,3},{3,2},{4,5},{5,4},{6,7},{7,6},{8,9},{9,8},{10,11... | collective-permute-start | bytes 602120 | tf_op jit(solution)/shard_map/ppermute | solution.py:488
  31.9 1.7 %collective-permute-start.1 = (bf16[784,128]{1,0:T(8,128)(2,1)}, bf16[784,128]{1,0:T(8,128)(2,1)S(1)}, u32[]{:S(2)}, u32[]{:S(2)}) collective-permute-start(bf16[784,128]{1,0:T(8,128)(2,1)} %get-tuple-element.31), channel_id=1, source_target_pairs={{0,1},{1,0},{2,3},{3,2},{4,5},{5,4},{6,7},{7,6},{8,9},{9,8},{10,11... | collective-permute-start | bytes 602120 | tf_op jit(solution)/shard_map/ppermute | solution.py:488
  33.2 0.9 %copy-start = (bf16[784,128]{1,0:T(8,128)(2,1)S(1)}, bf16[784,128]{1,0:T(8,128)(2,1)}, u32[]{:S(2)}) copy-start(bf16[784,128]{1,0:T(8,128)(2,1)} %get-tuple-element.30) | copy-start | bytes 602116
  34.3 6.1 %collective-permute-start.2 = (bf16[392,128]{1,0:T(8,128)(2,1)S(1)}, bf16[392,128]{1,0:T(8,128)(2,1)S(1)}, u32[]{:S(2)}, u32[]{:S(2)}) collective-permute-start(bf16[392,128]{1,0:T(8,128)(2,1)S(1)} %get-tuple-element.45), channel_id=1, source_target_pairs={{0,2},{1,3},{2,0},{3,1},{4,6},{5,7},{6,4},{7,5},{8,10},{9,11},{10,... | collective-permute-start | bytes 301064 | tf_op jit(solution)/shard_map/ppermute | solution.py:488
  37.3 5.7 %collective-permute-start.3 = (bf16[392,128]{1,0:T(8,128)(2,1)S(1)}, bf16[392,128]{1,0:T(8,128)(2,1)S(1)}, u32[]{:S(2)}, u32[]{:S(2)}) collective-permute-start(bf16[392,128]{1,0:T(8,128)(2,1)S(1)} %get-tuple-element.46), channel_id=1, source_target_pairs={{0,4},{1,5},{2,6},{3,7},{4,0},{5,1},{6,2},{7,3},{8,12},{9,13},{10,... | collective-permute-start | bytes 301064 | tf_op jit(solution)/shard_map/ppermute | solution.py:488
  38.8 5.5 %collective-permute-start.4 = (bf16[392,128]{1,0:T(8,128)(2,1)S(1)}, bf16[392,128]{1,0:T(8,128)(2,1)S(1)}, u32[]{:S(2)}, u32[]{:S(2)}) collective-permute-start(bf16[392,128]{1,0:T(8,128)(2,1)S(1)} %get-tuple-element.47), channel_id=1, source_target_pairs={{0,6},{1,7},{2,4},{3,5},{4,2},{5,3},{6,0},{7,1},{8,14},{9,15},{10,... | collective-permute-start | bytes 301064 | tf_op jit(solution)/shard_map/ppermute | solution.py:488
  44.4 4.7 %collective-permute-start.5 = (bf16[392,128]{1,0:T(8,128)(2,1)S(1)}, bf16[392,128]{1,0:T(8,128)(2,1)S(1)}, u32[]{:S(2)}, u32[]{:S(2)}) collective-permute-start(bf16[392,128]{1,0:T(8,128)(2,1)S(1)} %add_convert_fusion.4), channel_id=1, source_target_pairs={{0,8},{1,17},{2,10},{3,19},{4,12},{5,21},{6,14},{7,23},{8,0},{9,25... | collective-permute-start | bytes 301064 | tf_op jit(solution)/shard_map/ppermute | solution.py:488
  49.1 5.6 %collective-permute-start.6 = (bf16[392,128]{1,0:T(8,128)(2,1)S(1)}, bf16[392,128]{1,0:T(8,128)(2,1)S(1)}, u32[]{:S(2)}, u32[]{:S(2)}) collective-permute-start(bf16[392,128]{1,0:T(8,128)(2,1)S(1)} %add_convert_fusion.3), channel_id=1, source_target_pairs={{0,16},{1,9},{2,18},{3,11},{4,20},{5,13},{6,22},{7,15},{8,24},{9,1... | collective-permute-start | bytes 301064 | tf_op jit(solution)/shard_map/ppermute | solution.py:488
  54.8 5.6 %collective-permute-start.9 = (bf16[392,128]{1,0:T(8,128)(2,1)S(1)}, bf16[392,128]{1,0:T(8,128)(2,1)S(1)}, u32[]{:S(2)}, u32[]{:S(2)}) collective-permute-start(bf16[392,128]{1,0:T(8,128)(2,1)S(1)} %add_convert_fusion.2), channel_id=1, source_target_pairs={{0,6},{1,7},{2,4},{3,5},{4,2},{5,3},{6,0},{7,1},{8,14},{9,15},{10,... | collective-permute-start | bytes 301064 | tf_op jit(solution)/shard_map/ppermute | solution.py:488
  57.0 4.6 %collective-permute-start.8 = (bf16[392,128]{1,0:T(8,128)(2,1)S(1)}, bf16[392,128]{1,0:T(8,128)(2,1)S(1)}, u32[]{:S(2)}, u32[]{:S(2)}) collective-permute-start(bf16[392,128]{1,0:T(8,128)(2,1)S(1)} %add_convert_fusion.2), channel_id=1, source_target_pairs={{0,4},{1,5},{2,6},{3,7},{4,0},{5,1},{6,2},{7,3},{8,12},{9,13},{10,... | collective-permute-start | bytes 301064 | tf_op jit(solution)/shard_map/ppermute | solution.py:488
  57.6 4.6 %collective-permute-start.7 = (bf16[392,128]{1,0:T(8,128)(2,1)S(1)}, bf16[392,128]{1,0:T(8,128)(2,1)S(1)}, u32[]{:S(2)}, u32[]{:S(2)}) collective-permute-start(bf16[392,128]{1,0:T(8,128)(2,1)S(1)} %add_convert_fusion.2), channel_id=1, source_target_pairs={{0,2},{1,3},{2,0},{3,1},{4,6},{5,7},{6,4},{7,5},{8,10},{9,11},{10,... | collective-permute-start | bytes 301064 | tf_op jit(solution)/shard_map/ppermute | solution.py:488
  62.4 1.5 %collective-permute-start.10 = (bf16[784,128]{1,0:T(8,128)(2,1)S(1)}, bf16[784,128]{1,0:T(8,128)(2,1)S(1)}, u32[]{:S(2)}, u32[]{:S(2)}) collective-permute-start(bf16[784,128]{1,0:T(8,128)(2,1)S(1)} %pad_maximum_fusion.mine_a), channel_id=1, source_target_pairs={{0,1},{1,0},{2,3},{3,2},{4,5},{5,4},{6,7},{7,6},{8,9},{9,8},{10,11... | collective-permute-start | bytes 602120 | tf_op jit(solution)/shard_map/ppermute | solution.py:488
  62.5 1.7 %collective-permute-start.11 = (bf16[784,128]{1,0:T(8,128)(2,1)S(1)}, bf16[784,128]{1,0:T(8,128)(2,1)S(1)}, u32[]{:S(2)}, u32[]{:S(2)}) collective-permute-start(bf16[784,128]{1,0:T(8,128)(2,1)S(1)} %pad_maximum_fusion.1.mine_b), channel_id=1, source_target_pairs={{0,1},{1,0},{2,3},{3,2},{4,5},{5,4},{6,7},{7,6},{8,9},{9,8},{10,11... | collective-permute-start | bytes 602120 | tf_op jit(solution)/shard_map/ppermute | solution.py:488
